TPU v7x, 32 devices: a whole 2x2x4 slice. The times are simulated.
32 devices in a mesh: win: 16 (over z, y, x), tp: 2 (over core).
Axes of the slice: x: 2, y: 2, z: 4, core: 2. Of those that a mesh axis runs over, the one named last changes fastest.
Arguments:
- pixels: bfloat16 [128, 20, 20, 512], P(('win', 'tp')), may hold values from -6 to 6
- merge_gain: float32 [2048], P('tp'), may hold values from 0.1 to 1.9
- merge_shift: float32 [2048], P('tp'), may hold values from -3 to 3
- merge_weight: bfloat16 [2048, 1024], P('tp'), may hold values from -0.125 to 0.125
- norm1_gain: float32 [1024], P('tp'), may hold values from 0.1 to 1.9
- norm1_shift: float32 [1024], P('tp'), may hold values from -3 to 3
- qkv_weight: bfloat16 [1024, 3, 1024], P(None, None, 'tp'), may hold values from -0.1875 to 0.1875
- qkv_bias: float32 [2, 1024], P(None, 'tp'), may hold values from -3 to 3
- rel_table: float32 [361, 32], P(None, 'tp'), may hold values from -6 to 6
- proj_weight: bfloat16 [1024, 1024], P('tp'), may hold values from -0.5 to 0.5
- proj_bias: float32 [1024], P('tp'), may hold values from -3 to 3
- norm2_gain: float32 [1024], P('tp'), may hold values from 0.1 to 1.9
- norm2_shift: float32 [1024], P('tp'), may hold values from -3 to 3
- fc1_weight: bfloat16 [1024, 4096], P(None, 'tp'), may hold values from -0.1875 to 0.1875
- fc1_bias: float32 [4096], P('tp'), may hold values from -3 to 3
- fc2_weight: bfloat16 [4096, 1024], P('tp'), may hold values from -0.125 to 0.125
- fc2_bias: float32 [1024], P('tp'), may hold values from -3 to 3
- rel_index: int32 [100, 100], replicated, may hold values from 0 to 360
- keep: int32 [12800], P('win'), may hold values 0 or 1
- cotangent: bfloat16 [12800, 1024], P('win', 'tp'), may hold values from -6 to 6
Outputs:
- out: bfloat16 [12800, 1024], P('win', 'tp')
- pixels_grad: float32 [128, 20, 20, 512], P(('win', 'tp'))
- merge_gain_grad: float32 [2048], P('tp')
- merge_shift_grad: float32 [2048], P('tp')
- merge_weight_grad: float32 [2048, 1024], P('tp', 'win')
- norm1_gain_grad: float32 [1024], P('tp')
- norm1_shift_grad: float32 [1024], P('tp')
- qkv_weight_grad: float32 [1024, 3, 1024], P('win', None, 'tp')
- qkv_bias_grad: float32 [2, 1024], P(None, 'tp')
- rel_table_grad: float32 [361, 32], P(None, 'tp')
- proj_weight_grad: float32 [1024, 1024], P('tp', 'win')
- proj_bias_grad: float32 [1024], P('tp')
- norm2_gain_grad: float32 [1024], P('tp')
- norm2_shift_grad: float32 [1024], P('tp')
- fc1_weight_grad: float32 [1024, 4096], P('win', 'tp')
- fc1_bias_grad: float32 [4096], P('tp')
- fc2_weight_grad: float32 [4096, 1024], P('tp', 'win')
- fc2_bias_grad: float32 [1024], P('tp')
All inputs are finite; a program needn't handle non-finite values. No bound on the sum of `keep` on one device may be relied on, other than what follows from the above.
Results may differ from a plain program's by a relative error of at most 0.015.
Values may be sent and summed in bfloat16 or wider, within the bound.
A program may use at most 192 MiB of HBM per device.

v0:
```python
from functools import partial

import jax
import jax.numpy as jnp
from jax import lax
from jax.sharding import PartitionSpec as P

EPS = 1e-05
HIGH = lax.Precision.HIGHEST


def finish_norm(values, totals, width, gain, shift):
    mean = totals[0] / width
    second = totals[1] / width
    scale = lax.rsqrt(second - mean * mean + EPS)
    centred = (values - mean[:, None]) * scale[:, None]
    return (centred, scale, centred * gain + shift)


def norm_grads(grad, centred, gain):
    scaled = grad * gain
    local = (jnp.sum(scaled, 1), jnp.sum(scaled * centred, 1))
    return (scaled, local, jnp.sum(grad * centred, 0), jnp.sum(grad, 0))


def spread_back(scaled, centred, scale, totals, width):
    first_mean = totals[0][:, None] / width
    cross_mean = totals[1][:, None] / width
    return scale[:, None] * (scaled - first_mean - centred * cross_mean)


def block_norm(values, gain, shift, width):
    totals = lax.psum((jnp.sum(values, 1), jnp.sum(values * values, 1)), "tp")
    return finish_norm(values, totals, width, gain, shift)


def block_norm_back(grad, centred, scale, gain, width):
    scaled, local, gain_grad, shift_grad = norm_grads(grad, centred, gain)
    totals = lax.psum((local[0], local[1]), "tp")
    return (spread_back(scaled, centred, scale, totals, width), gain_grad, shift_grad)


def spread_sum(partial_rows):
    return lax.psum_scatter(partial_rows, "tp", scatter_dimension=1, tiled=True)


def return_sum(partial_rows):
    return lax.psum_scatter(
        partial_rows.astype(jnp.bfloat16), "tp", scatter_dimension=1, tiled=True
    ).astype(jnp.float32)


def gather_grad(grad_low):
    return lax.all_gather(grad_low, "tp", axis=1, tiled=True)


def times_transposed(left, right):
    return lax.dot_general(
        left, right, (((1,), (1,)), ((), ())), preferred_element_type=jnp.float32
    )


def project_in(normed_low, weight_rows):
    whole = lax.all_gather(normed_low, "tp", axis=1, tiled=True)
    return (whole, jnp.dot(whole, weight_rows, preferred_element_type=jnp.float32))


def weight_grad_in(kept, grad_low):
    return jnp.einsum("tc,tf->cf", kept, grad_low, preferred_element_type=jnp.float32)


def window_scores(query, key_rows, bias, scale):
    return (
        jnp.einsum("wqhd,wkhd->whqk", query, key_rows, preferred_element_type=jnp.float32) * scale
        + bias[None]
    )


def shards(
    pixels,
    merge_gain,
    merge_shift,
    merge_weight,
    norm1_gain,
    norm1_shift,
    qkv_weight,
    qkv_bias,
    rel_table,
    proj_weight,
    proj_bias,
    norm2_gain,
    norm2_shift,
    fc1_weight,
    fc1_bias,
    fc2_weight,
    fc2_bias,
    rel_index,
    keep,
    cotangent,
):
    wins, height, _, channels = pixels.shape
    side = height // 2
    width = 4 * channels
    area = side * side
    model = merge_weight.shape[1]
    local_width = qkv_weight.shape[2]
    heads_here = rel_table.shape[1]
    head_dim = local_width // heads_here
    table_rows = rel_table.shape[0]
    scale = head_dim ** (-0.5)
    grid = (
        pixels.reshape(wins, side, 2, side, 2, channels)
        .transpose(0, 1, 3, 4, 2, 5)
        .reshape(wins * area, width)
    )
    merged = lax.all_to_all(grid, "tp", split_axis=1, concat_axis=0, tiled=True).astype(jnp.float32)
    tokens = merged.shape[0]
    windows = tokens // area
    merge_totals = lax.psum((jnp.sum(merged, 1), jnp.sum(merged * merged, 1)), "tp")
    merge_centred, merge_scale, merge_out = finish_norm(
        merged, merge_totals, width, merge_gain, merge_shift
    )
    merge_low = merge_out.astype(jnp.bfloat16)
    stream0 = spread_sum(jnp.dot(merge_low, merge_weight, preferred_element_type=jnp.float32))
    first_centred, first_scale, first_out = block_norm(stream0, norm1_gain, norm1_shift, model)
    first_low = first_out.astype(jnp.bfloat16)
    qkv_rows = qkv_weight.reshape(model, 3 * local_width)
    first_kept, qkv_raw = project_in(first_low, qkv_rows)
    zero_bias = jnp.zeros_like(qkv_bias[0])
    qkv_full = (
        qkv_raw.reshape(tokens, 3, local_width)
        + jnp.stack([qkv_bias[0], zero_bias, qkv_bias[1]])[None]
    )
    shaped = qkv_full.astype(jnp.bfloat16).reshape(windows, area, 3, heads_here, head_dim)
    query = shaped[:, :, 0]
    key_rows = shaped[:, :, 1]
    value_rows = shaped[:, :, 2]
    onehot = (
        rel_index.reshape(area * area, 1) == jnp.arange(table_rows, dtype=jnp.int32)[None]
    ).astype(jnp.float32)
    bias = (
        jnp.dot(onehot, rel_table, precision=HIGH)
        .reshape(area, area, heads_here)
        .transpose(2, 0, 1)
    )
    scores = window_scores(query, key_rows, bias, scale)
    top = jnp.max(scores, -1, keepdims=True)
    raised = jnp.exp(scores - top)
    total = jnp.sum(raised, -1, keepdims=True)
    probs = raised / total
    log_total = top + jnp.log(total)
    attended = jnp.einsum(
        "whqk,wkhd->wqhd",
        probs.astype(jnp.bfloat16),
        value_rows,
        preferred_element_type=jnp.float32,
    )
    attended_low = attended.reshape(tokens, local_width).astype(jnp.bfloat16)
    attention = (
        spread_sum(jnp.dot(attended_low, proj_weight, preferred_element_type=jnp.float32))
        + proj_bias
    )
    stream1 = stream0 + attention
    second_centred, second_scale, second_out = block_norm(stream1, norm2_gain, norm2_shift, model)
    second_low = second_out.astype(jnp.bfloat16)
    second_kept, hidden_raw = project_in(second_low, fc1_weight)
    hidden = hidden_raw + fc1_bias
    activated_low = jax.nn.gelu(hidden, approximate=False).astype(jnp.bfloat16)
    feed = (
        spread_sum(jnp.dot(activated_low, fc2_weight, preferred_element_type=jnp.float32))
        + fc2_bias
    )
    keep_rows = keep.astype(jnp.float32)[:, None]
    out = (keep_rows * (stream1 + feed)).astype(jnp.bfloat16)
    d_out = keep_rows * cotangent.astype(jnp.float32)
    g_feed = d_out.astype(jnp.bfloat16)
    fc2_bias_grad = jnp.sum(g_feed.astype(jnp.float32), 0)
    g_feed_all = gather_grad(g_feed)
    fc2_weight_grad = jnp.einsum(
        "tc,tf->cf", activated_low, g_feed_all, preferred_element_type=jnp.float32
    )
    d_activated = times_transposed(g_feed_all, fc2_weight)
    gelu_pull = jax.vjp(partial(jax.nn.gelu, approximate=False), hidden)[1]
    g_hidden = gelu_pull(d_activated)[0].astype(jnp.bfloat16)
    fc1_bias_grad = jnp.sum(g_hidden.astype(jnp.float32), 0)
    fc1_weight_grad = weight_grad_in(second_kept, g_hidden)
    g_second = return_sum(times_transposed(g_hidden, fc1_weight))
    d_second, norm2_gain_grad, norm2_shift_grad = block_norm_back(
        g_second, second_centred, second_scale, norm2_gain, model
    )
    d_stream1 = d_out + d_second
    g_attention = d_stream1.astype(jnp.bfloat16)
    proj_bias_grad = jnp.sum(g_attention.astype(jnp.float32), 0)
    g_attention_all = gather_grad(g_attention)
    proj_weight_grad = jnp.einsum(
        "tc,tf->cf", attended_low, g_attention_all, preferred_element_type=jnp.float32
    )
    g_attended = (
        times_transposed(g_attention_all, proj_weight)
        .astype(jnp.bfloat16)
        .reshape(windows, area, heads_here, head_dim)
    )
    again_scores = window_scores(query, key_rows, bias, scale)
    again_probs = jnp.exp(again_scores - log_total)
    probs_low = again_probs.astype(jnp.bfloat16)
    d_probs = jnp.einsum(
        "wqhd,wkhd->whqk", g_attended, value_rows, preferred_element_type=jnp.float32
    )
    g_scores = (again_probs * (d_probs - jnp.sum(d_probs * again_probs, -1, keepdims=True))).astype(
        jnp.bfloat16
    )
    d_query = (
        jnp.einsum("whqk,wkhd->wqhd", g_scores, key_rows, preferred_element_type=jnp.float32)
        * scale
    )
    d_key = (
        jnp.einsum("whqk,wqhd->wkhd", g_scores, query, preferred_element_type=jnp.float32) * scale
    )
    d_value = jnp.einsum(
        "whqk,wqhd->wkhd", probs_low, g_attended, preferred_element_type=jnp.float32
    )
    g_qkv = (
        jnp.stack([d_query, d_key, d_value], 2)
        .reshape(tokens, 3 * local_width)
        .astype(jnp.bfloat16)
    )
    qkv_sums = jnp.sum(g_qkv.astype(jnp.float32).reshape(tokens, 3, local_width), 0)
    qkv_bias_grad = jnp.stack([qkv_sums[0], qkv_sums[2]])
    score_sums = (
        jnp.sum(g_scores.astype(jnp.float32), 0).transpose(1, 2, 0).reshape(area * area, heads_here)
    )
    rel_table_grad = lax.dot_general(onehot, score_sums, (((0,), (0,)), ((), ())), precision=HIGH)
    qkv_weight_grad = weight_grad_in(first_kept, g_qkv).reshape(model, 3, local_width)
    g_first = return_sum(times_transposed(g_qkv, qkv_rows))
    d_first, norm1_gain_grad, norm1_shift_grad = block_norm_back(
        g_first, first_centred, first_scale, norm1_gain, model
    )
    d_stream0 = d_stream1 + d_first
    g_stream0 = d_stream0.astype(jnp.bfloat16)
    g_stream_all = gather_grad(g_stream0)
    merge_weight_grad = jnp.einsum(
        "tc,tf->cf", merge_low, g_stream_all, preferred_element_type=jnp.float32
    )
    g_merge = times_transposed(g_stream_all, merge_weight)
    scaled, local, merge_gain_grad, merge_shift_grad = norm_grads(
        g_merge, merge_centred, merge_gain
    )
    back_totals = lax.psum((local[0], local[1]), "tp")
    d_merged = spread_back(scaled, merge_centred, merge_scale, back_totals, width)
    d_grid = lax.all_to_all(
        d_merged.astype(jnp.bfloat16), "tp", split_axis=0, concat_axis=1, tiled=True
    ).astype(d_merged.dtype)
    pixels_grad = (
        d_grid.reshape(wins, side, side, 2, 2, channels)
        .transpose(0, 1, 4, 2, 3, 5)
        .reshape(pixels.shape)
    )
    matrices = (
        lax.psum_scatter(merge_weight_grad, "win", scatter_dimension=1, tiled=True),
        lax.psum_scatter(qkv_weight_grad, "win", scatter_dimension=0, tiled=True),
        lax.psum_scatter(proj_weight_grad, "win", scatter_dimension=1, tiled=True),
        lax.psum_scatter(fc1_weight_grad, "win", scatter_dimension=0, tiled=True),
        lax.psum_scatter(fc2_weight_grad, "win", scatter_dimension=1, tiled=True),
    )
    vectors = lax.psum(
        (
            merge_gain_grad,
            merge_shift_grad,
            norm1_gain_grad,
            norm1_shift_grad,
            qkv_bias_grad,
            rel_table_grad,
            proj_bias_grad,
            norm2_gain_grad,
            norm2_shift_grad,
            fc1_bias_grad,
            fc2_bias_grad,
        ),
        "win",
    )
    return (
        out,
        pixels_grad,
        vectors[0],
        vectors[1],
        matrices[0],
        vectors[2],
        vectors[3],
        matrices[1],
        vectors[4],
        vectors[5],
        matrices[2],
        vectors[6],
        vectors[7],
        vectors[8],
        matrices[3],
        vectors[9],
        matrices[4],
        vectors[10],
    )


def solution(mesh):
    in_specs = (
        P(("win", "tp"), None, None, None),
        P("tp"),
        P("tp"),
        P("tp", None),
        P("tp"),
        P("tp"),
        P(None, None, "tp"),
        P(None, "tp"),
        P(None, "tp"),
        P("tp", None),
        P("tp"),
        P("tp"),
        P("tp"),
        P(None, "tp"),
        P("tp"),
        P("tp", None),
        P("tp"),
        P(),
        P("win"),
        P("win", "tp"),
    )
    out_specs = (
        P("win", "tp"),
        P(("win", "tp"), None, None, None),
        P("tp"),
        P("tp"),
        P("tp", "win"),
        P("tp"),
        P("tp"),
        P("win", None, "tp"),
        P(None, "tp"),
        P(None, "tp"),
        P("tp", "win"),
        P("tp"),
        P("tp"),
        P("tp"),
        P("win", "tp"),
        P("tp"),
        P("tp", "win"),
        P("tp"),
    )
    return jax.shard_map(shards, mesh=mesh, in_specs=in_specs, out_specs=out_specs, check_vma=False)
```

profile of v0, /device:TPU:0, one launch (start us, length us, event | category | flops | bytes accessed | tf_op | source)
XLA Modules:
  0.0 995.3 jit_solution(7413651280125380529)
XLA Ops:
  7.2 4.4 copy.68
  11.7 5.0 all_to_all.20
  16.7 6.2 all_to_all.26
  31.5 3.6 fusion.52
  35.1 13.8 %reduce-scatter.11.cloned.1.call-done = f32[800,512]{1,0:T(8,128)} async-done(((f32[800,1024]{1,0:T(8,128)}), f32[800,512]{1,0:T(8,128)}) %reduce-scatter.11.cloned.1.call-update) | async-done | bytes 1638416 | tf_op jit(solution)/shard_map/reduce_scatter | solution.py:44
  57.8 7.7 fusion.1
  68.5 4.8 copy.69
  73.5 6.6 add_convert_fusion.1
  80.0 4.5 copy.70
  84.5 6.9 reshape.141
  104.3 4.3 fusion.63
  109.1 11.8 %reduce-scatter.13.cloned.1.call-done = f32[800,512]{1,0:T(8,128)} async-done(((f32[800,1024]{1,0:T(8,128)}), f32[800,512]{1,0:T(8,128)}) %reduce-scatter.13.cloned.1.call-update) | async-done | bytes 1638416 | tf_op jit(solution)/shard_map/reduce_scatter | solution.py:44
  120.9 3.3 fusion.54
  132.4 8.2 all-gather.8.cloned.1.call-done
  140.6 8.9 fusion.64
  149.4 4.2 all-gather.10.cloned.1.call-done
  153.6 22.3 %convert_reduce_fusion.1 = (f32[2048]{0:T(1024)S(1)}, bf16[800,2048]{1,0:T(8,128)(2,1)S(1)}, f32[800,2048]{1,0:T(8,128)}) fusion(f32[800,2048]{1,0:T(8,128)} %fusion.64, f32[2048]{0:T(1024)S(1)} %copy-done.27, bf16[800,1024]{1,0:T(8,128)(2,1)} %all-gather.10.cloned.1.call-done, bf16[2048,1024]{1,0:T(8,128)(2,1)} %param.35), kind=kOutput, calls=%fused_computation.14 | convolution fusion | flops 3478321152 | bytes 22233088 | tf_op jit(solution)/shard_map/dot_general | solution.py:58
  177.7 4.7 convolution_convert_fusion.1
  182.5 6.6 multiply_convert_fusion.1
  190.8 5.3 fusion.65
  201.3 7.2 reduce-scatter.15.cloned.1.call-done
  208.5 4.1 convert_reduce_fusion.6
  212.9 11.0 %all-gather.12.cloned.1.call-done = bf16[800,1024]{1,0:T(8,128)(2,1)} async-done(((bf16[800,512]{1,0:T(8,128)(2,1)}), bf16[800,1024]{1,0:T(8,128)(2,1)}) %all-gather.12.cloned.1.call-update) | async-done | bytes 1638416 | tf_op jit(solution)/shard_map/all_gather | solution.py:54
  223.8 3.7 convolution_convert_fusion.2
  229.7 3.2 reshape.143
  232.9 5.3 fusion.43
  238.2 5.3 multiply_reduce_fusion
  243.5 3.6 convert_reduce_fusion
  251.5 5.3 copy.83
  256.8 6.1 convert_element_type.152
  262.9 6.7 convolution_convert_fusion
  269.6 10.4 %reduce-scatter.19.cloned.1.call-done = bf16[800,512]{1,0:T(8,128)(2,1)} async-done(((bf16[800,1024]{1,0:T(8,128)(2,1)}), bf16[800,512]{1,0:T(8,128)(2,1)}) %reduce-scatter.19.cloned.1.call-update) | async-done | bytes 819216 | tf_op jit(solution)/shard_map/reduce_scatter | solution.py:48
  285.2 3.6 fusion.31
  289.0 4.0 fusion.66
  293.5 10.3 %fusion.68 = f32[2048,1024]{0,1:T(8,128)} fusion(bf16[800,2048]{1,0:T(8,128)(2,1)} %copy-done.11, bf16[800,1024]{1,0:T(8,128)(2,1)} %all-gather.10.cloned.1.call-done), kind=kOutput, calls=%fused_computation.132 | convolution fusion | flops 3355443200 | bytes 13303808 | tf_op jit(solution)/shard_map/tc,tf->cf/dot_general | solution.py:179
  303.9 10.3 %fusion.67 = f32[1024,2048]{1,0:T(8,128)} fusion(bf16[800,1024]{1,0:T(8,128)(2,1)} %all-gather.8.cloned.1.call-done, bf16[800,2048]{1,0:T(8,128)(2,1)} %copy-done.43), kind=kOutput, calls=%fused_computation.131 | convolution fusion | flops 3355443200 | bytes 13303808 | tf_op jit(solution)/shard_map/tc,tf->cf/dot_general | solution.py:69
  314.2 8.4 fusion.39
  323.4 6.8 fusion.51
  333.0 6.4 fusion
  339.5 6.0 fusion.53
  350.9 5.2 all_to_all.27
  358.2 5.7 reshape.152
  364.0 5.8 copy.84
  369.7 79.4 %all-reduce = (f32[1024]{0:T(1024)}, f32[1024]{0:T(1024)}, f32[512]{0:T(512)}, f32[512]{0:T(512)}, f32[2,512]{1,0:T(2,128)}, /*index=5*/f32[361,16]{0,1:T(8,128)...) all-reduce(f32[1024]{0:T(1024)S(1)} %get-tuple-element.21, ...), channel_id=1, replica_groups=mesh['win'=16,'tp'=2] {'win'}, use_global_device_ids=true, to_apply=%region_33.0 | all-reduce | flops 13968 | bytes 111744 | tf_op jit(solution)/shard_map/psum | solution.py:265
  449.1 115.5 %reduce-scatter.29.cloned.1.call-done = f32[2048,64]{0,1:T(8,128)} async-done(((f32[2048,1024]{0,1:T(8,128)}), f32[2048,64]{0,1:T(8,128)}) %reduce-scatter.29.cloned.1.call-update) | async-done | bytes 524304 | tf_op jit(solution)/shard_map/reduce_scatter | solution.py:263
  564.6 183.2 %reduce-scatter.27.cloned.1.call-done = f32[64,2048]{1,0:T(8,128)} async-done(((f32[1024,2048]{1,0:T(8,128)}), f32[64,2048]{1,0:T(8,128)}) %reduce-scatter.27.cloned.1.call-update) | async-done | bytes 524304 | tf_op jit(solution)/shard_map/reduce_scatter | solution.py:262
  747.8 141.5 %reduce-scatter.23.cloned.1.call-done = f32[64,3,512]{2,0,1:T(8,128)} async-done(((f32[1024,3,512]{2,0,1:T(8,128)}), f32[64,3,512]{2,0,1:T(8,128)}) %reduce-scatter.23.cloned.1.call-update) | async-done | bytes 393232 | tf_op jit(solution)/shard_map/reduce_scatter | solution.py:260
  889.3 99.3 %reduce-scatter.21.cloned.1.call-done = f32[1024,64]{0,1:T(8,128)} async-done(((f32[1024,1024]{0,1:T(8,128)}), f32[1024,64]{0,1:T(8,128)}) %reduce-scatter.21.cloned.1.call-update) | async-done | bytes 262160 | tf_op jit(solution)/shard_map/reduce_scatter | solution.py:259
  (177 shorter events, 74.4 us)
Async XLA Ops:
  7.2 24.3 %copy-start = (bf16[1024,1024]{1,0:T(8,128)(2,1)S(1)}, bf16[1024,1024]{1,0:T(8,128)(2,1)}, u32[]{:S(2)}) copy-start(bf16[1024,1024]{1,0:T(8,128)(2,1)} %param.23) | copy-start | bytes 6291460
  7.2 41.8 %reduce-scatter.11.cloned.1.call-start = ((), (), s32[]{:S(2)}) async-start(), calls=%async_computation.12 | async-start | bytes 4915200 | tf_op jit(solution)/shard_map/reduce_scatter | solution.py:44
  24.1 7.3 copy-start.31
  24.1 7.3 copy-start.41
  35.0 18.8 %copy-start.24 = (f32[512]{0:T(512)S(1)}, f32[512]{0:T(512)}, u32[]{:S(2)}) copy-start(f32[512]{0:T(512)} %param.24) | copy-start | bytes 6148
  35.0 18.8 %copy-start.33 = (f32[512]{0:T(512)S(1)}, f32[512]{0:T(512)}, u32[]{:S(2)}) copy-start(f32[512]{0:T(512)} %param.25) | copy-start | bytes 6148
  35.1 22.0 %copy-start.17 = (s32[100,100]{1,0:T(8,128)S(1)}, s32[100,100]{1,0:T(8,128)}, u32[]{:S(2)}) copy-start(s32[100,100]{1,0:T(8,128)} %param.37) | copy-start | bytes 120004
  35.1 22.7 %copy-start.40 = (f32[361,16]{0,1:T(8,128)S(1)}, f32[361,16]{0,1:T(8,128)}, u32[]{:S(2)}) copy-start(f32[361,16]{0,1:T(8,128)} %param.28) | copy-start | bytes 69316
  35.1 38.4 %all-gather.6.cloned.1.call-start = ((), (), s32[]{:S(2)}) async-start(), calls=%async_computation.13 | async-start | bytes 2457600 | tf_op jit(solution)/shard_map/all_gather | solution.py:64
  56.5 64.4 %reduce-scatter.13.cloned.1.call-start = ((), (), s32[]{:S(2)}) async-start(), calls=%async_computation.14 | async-start | bytes 4915200 | tf_op jit(solution)/shard_map/reduce_scatter | solution.py:44
  68.5 4.9 copy-start.29
  93.6 4.0 copy-start.8
  95.6 2.9 copy-start.1
  104.3 16.6 %copy-start.34 = (f32[512]{0:T(512)S(1)}, f32[512]{0:T(512)}, u32[]{:S(2)}) copy-start(f32[512]{0:T(512)} %param.30) | copy-start | bytes 6148
  108.6 18.1 %copy-start.26 = (f32[512]{0:T(512)S(1)}, f32[512]{0:T(512)}, u32[]{:S(2)}) copy-start(f32[512]{0:T(512)} %param.31) | copy-start | bytes 6148
  108.6 18.1 %copy-start.35 = (f32[512]{0:T(512)S(1)}, f32[512]{0:T(512)}, u32[]{:S(2)}) copy-start(f32[512]{0:T(512)} %param.32) | copy-start | bytes 6148
  108.6 20.8 %copy-start.30 = (s32[800]{0:T(1024)S(1)}, s32[800]{0:T(1024)}, u32[]{:S(2)}) copy-start(s32[800]{0:T(1024)} %param.38) | copy-start | bytes 9604
  108.6 31.9 %all-gather.8.cloned.1.call-start = ((), (), s32[]{:S(2)}) async-start(), calls=%async_computation.15 | async-start | bytes 2457600 | tf_op jit(solution)/shard_map/all_gather | solution.py:64
  129.3 24.3 %all-gather.10.cloned.1.call-start = ((), (), s32[]{:S(2)}) async-start(), calls=%async_computation.17 | async-start | bytes 2457600 | tf_op jit(solution)/shard_map/all_gather | solution.py:54
  132.3 21.3 %copy-start.27 = (f32[2048]{0:T(1024)S(1)}, f32[2048]{0:T(1024)}, u32[]{:S(2)}) copy-start(f32[2048]{0:T(1024)} %param.34) | copy-start | bytes 24580
  132.3 63.9 %reduce-scatter.17.cloned.1.call-start = ((), (), s32[]{:S(2)}) async-start(), calls=%async_computation.18 | async-start | bytes 2457600 | tf_op jit(solution)/shard_map/reduce_scatter | solution.py:48
  153.6 24.0 %copy-start.37 = (bf16[1024,2048]{1,0:T(8,128)(2,1)S(1)}, bf16[1024,2048]{1,0:T(8,128)(2,1)}, u32[]{:S(2)}) copy-start(bf16[1024,2048]{1,0:T(8,128)(2,1)} %param.33) | copy-start | bytes 12582916
  182.4 26.1 %reduce-scatter.15.cloned.1.call-start = ((), (), s32[]{:S(2)}) async-start(), calls=%async_computation.16 | async-start | bytes 4915200 | tf_op jit(solution)/shard_map/reduce_scatter | solution.py:44
  182.4 8.3 copy-start.38
  196.1 12.4 %copy-start.36 = (f32[512]{0:T(512)S(1)}, f32[512]{0:T(512)}, u32[]{:S(2)}) copy-start(f32[512]{0:T(512)} %param.36) | copy-start | bytes 6148
  196.1 27.7 %all-gather.12.cloned.1.call-start = ((), (), s32[]{:S(2)}) async-start(), calls=%async_computation.19 | async-start | bytes 2457600 | tf_op jit(solution)/shard_map/all_gather | solution.py:54
  212.6 67.4 %reduce-scatter.19.cloned.1.call-start = ((), (), s32[]{:S(2)}) async-start(), calls=%async_computation.20 | async-start | bytes 2457600 | tf_op jit(solution)/shard_map/reduce_scatter | solution.py:48
  232.9 5.3 copy-start.6
  232.9 5.3 copy-start.9
  232.9 10.6 %slice-start = ((s8[6815744]{0:T(1024)(128)(4,1)}), s8[4194304]{0:T(1024)(128)(4,1)S(1)}, s32[]{:S(2)}) async-start(s8[6815744]{0:T(1024)(128)(4,1)} %bitcast.124), calls=%async_computation.27 | async-start | bytes 8388608
  238.2 5.3 slice-start.1
  243.5 3.6 copy-start.5
  262.9 17.1 %copy-start.14 = (f32[800]{0:T(1024)S(1)}, f32[800]{0:T(1024)}, u32[]{:S(2)}) copy-start(f32[800]{0:T(1024)} %copy-done.13) | copy-start | bytes 9604
  262.9 17.1 %copy-start.16 = (f32[800]{0:T(1024)S(1)}, f32[800]{0:T(1024)}, u32[]{:S(2)}) copy-start(f32[800]{0:T(1024)} %copy-done.15) | copy-start | bytes 9604
  262.9 17.1 %copy-start.25 = (f32[512]{0:T(512)S(1)}, f32[512]{0:T(512)}, u32[]{:S(2)}) copy-start(f32[512]{0:T(512)} %param.24) | copy-start | bytes 6148
  269.6 53.3 %all-gather.14.cloned.1.call-start = ((), (), s32[]{:S(2)}) async-start(), calls=%async_computation.21 | async-start | bytes 2457600 | tf_op jit(solution)/shard_map/all_gather | solution.py:54
  282.6 6.4 copy-start.7
  288.9 160.2 %reduce-scatter.25.cloned.1.call-start = ((), (), s32[]{:S(2)}) async-start(), calls=%async_computation.24 | async-start | bytes 2228224 | tf_op jit(solution)/shard_map/reduce_scatter | solution.py:261
  293.0 271.6 %reduce-scatter.29.cloned.1.call-start = ((), (), s32[]{:S(2)}) async-start(), calls=%async_computation.26 | async-start | bytes 8912896 | tf_op jit(solution)/shard_map/reduce_scatter | solution.py:263
  303.8 444.0 %reduce-scatter.27.cloned.1.call-start = ((), (), s32[]{:S(2)}) async-start(), calls=%async_computation.25 | async-start | bytes 8912896 | tf_op jit(solution)/shard_map/reduce_scatter | solution.py:262
  314.2 575.1 %reduce-scatter.23.cloned.1.call-start = ((), (), s32[]{:S(2)}) async-start(), calls=%async_computation.23 | async-start | bytes 6684672 | tf_op jit(solution)/shard_map/reduce_scatter | solution.py:260
  322.7 665.9 %reduce-scatter.21.cloned.1.call-start = ((), (), s32[]{:S(2)}) async-start(), calls=%async_computation.22 | async-start | bytes 4456448 | tf_op jit(solution)/shard_map/reduce_scatter | solution.py:259
  330.2 2.8 copy-start.19
  331.7 7.7 copy-start.21
  331.7 7.7 copy-start.23
  333.0 6.4 copy-start.3
  333.0 6.4 copy-start.39
  364.0 5.8 copy-start.28
  (13 other events, 16.7 us)
Sparse Core Ops, SparseCore 0:
  35.2 13.7 reduce-scatter.10
  56.6 11.0 all-gather.5
  108.7 12.1 reduce-scatter.12
  129.5 11.0 all-gather.7
  142.5 11.0 all-gather.9
  182.5 10.2 reduce-scatter.16
  196.2 12.2 reduce-scatter.14
  212.7 11.0 all-gather.11
  269.7 10.2 reduce-scatter.18
  289.0 11.1 all-gather.13
  303.1 81.7 reduce-scatter.24
  387.8 176.8 reduce-scatter.28
  567.6 180.1 reduce-scatter.26
  750.7 138.5 reduce-scatter.22
  892.1 96.4 reduce-scatter.20
where the time goes:
time: 1000 us; the launch traced here: 995 us
  waiting for transfers between devices  606 us (61%)
  matrix products  143 us (14%)
  blocking collectives  106 us (11%)
  local copies, waits for them, and re-layouts  76.1 us (8%)
  other arithmetic  47.2 us (5%)
  between operations  14.7 us (1%)
    reduce_scatter x1, waiting for transfers between devices, shards(): lax.psum_scatter(fc1_weight_grad, 'win', scatter_dimension=0, tiled=True)  183 us
    reduce_scatter x1, waiting for transfers between devices, shards(): lax.psum_scatter(qkv_weight_grad, 'win', scatter_dimension=0, tiled=True)  141 us
    reduce_scatter x1, waiting for transfers between devices, shards(): lax.psum_scatter(fc2_weight_grad, 'win', scatter_dimension=1, tiled=True)  115 us
    reduce_scatter x1, waiting for transfers between devices, shards(): lax.psum_scatter(merge_weight_grad, 'win', scatter_dimension=1, tiled=True)  99.3 us
    psum x1, blocking collectives, shards(): lax.psum((merge_gain_grad, merge_shift_grad, norm1_gain_grad, norm1_shift...  79.4 us
    dot_general x5, matrix products, times_transposed(): lax.dot_general(left, right, (((1,), (1,)), ((), ())), preferred_element_...  43.4 us
    reduce_scatter x3, waiting for transfers between devices, spread_sum(): return lax.psum_scatter(partial_rows, 'tp', scatter_dimension=1, tiled=True)  32.9 us
  transfers between devices with their start and end apart: 15, of which 11 were waited for; matrix products, arithmetic and copies ran while one was open for 11% of the time, Pallas kernels for 0%

commit v1 on v0

v1 whole, which is shorter than its diff:
```python
import jax
import jax.numpy as jnp
from jax import lax
from jax.experimental import pallas as pl
from jax.experimental.pallas import tpu as pltpu
from jax.sharding import PartitionSpec as P

EPS = 1e-05
F32 = jnp.float32
BF16 = jnp.bfloat16
VMEM = pl.BlockSpec(memory_space=pltpu.VMEM)
SMEM = pl.BlockSpec(memory_space=pltpu.SMEM)
PAD = 112
LIMIT = 56 * 1024 * 1024


def call(body, out, ins, scratch=(), flops=0, nbytes=0, **more):
    return pl.pallas_call(
        body,
        out_shape=out,
        scratch_shapes=list(scratch),
        compiler_params=pltpu.CompilerParams(vmem_limit_bytes=LIMIT),
        cost_estimate=pl.CostEstimate(
            flops=int(flops), bytes_accessed=int(nbytes), transcendentals=0
        ),
        **more,
    )(*ins)


def whole(body, out, ins, scratch=(), flops=0, nbytes=0, smem_first=False):
    specs = [VMEM] * len(ins)
    if smem_first:
        specs[0] = SMEM
    outs = jax.tree.map(lambda _: VMEM, out)
    return call(body, out, ins, scratch, flops, nbytes, in_specs=specs, out_specs=outs)


def shape(dims, dtype=F32):
    return jax.ShapeDtypeStruct(tuple(dims), dtype)


def dot(a, b):
    return jnp.dot(a, b, preferred_element_type=F32)


def dot_nt(a, b):
    return lax.dot_general(a, b, (((1,), (1,)), ((), ())), preferred_element_type=F32)


def stats(x, width):
    mean = jnp.sum(x, 1, keepdims=True) * (1.0 / width)
    second = jnp.sum(x * x, 1, keepdims=True) * (1.0 / width)
    return mean, lax.rsqrt(second - mean * mean + EPS)


def tiles(total, size):
    return total // size


def row_loop(rows, size, fn):
    @pl.loop(0, rows // size)
    def _(step):
        fn(pl.ds(pl.multiple_of(step * size, size), size))


def merge_body(
    t_ref, x_ref, w_own, w_oth, mg, ms, g1, s1, stream0, mn_own, mn_oth, first
):
    t = t_ref[0]
    rows, half = mn_own.shape
    width = 2 * half

    def norm(r):
        xa = x_ref[t, r, :].astype(F32)
        xb = x_ref[1 - t, r, :].astype(F32)
        total = jnp.sum(xa, 1, keepdims=True) + jnp.sum(xb, 1, keepdims=True)
        square = jnp.sum(xa * xa, 1, keepdims=True) + jnp.sum(xb * xb, 1, keepdims=True)
        mean = total * (1.0 / width)
        scale = lax.rsqrt(square * (1.0 / width) - mean * mean + EPS)
        mn_own[r, :] = ((xa - mean) * scale * mg[t] + ms[t]).astype(BF16)
        mn_oth[r, :] = ((xb - mean) * scale * mg[1 - t] + ms[1 - t]).astype(BF16)

    row_loop(rows, 32, norm)
    model = stream0.shape[1]

    @pl.loop(0, model // 256)
    def _(c):
        cols = pl.ds(pl.multiple_of(c * 256, 256), 256)
        stream0[:, cols] = dot(mn_own[...], w_own[:, cols]) + dot(mn_oth[...], w_oth[:, cols])

    def norm1(r):
        x = stream0[r, :]
        mean, scale = stats(x, model)
        first[r, :] = ((x - mean) * scale * g1[...] + s1[...]).astype(BF16)

    row_loop(rows, 32, norm1)


def qkv_body(first, w_own, w_oth, bias, out):
    half = w_own.shape[2]
    for s in range(3):
        for side, w in enumerate((w_own, w_oth)):

            @pl.loop(0, half // 256)
            def _(c):
                src = pl.ds(pl.multiple_of(c * 256, 256), 256)
                dst = pl.ds(pl.multiple_of(side * half + c * 256, 256), 256)
                out[s, :, dst] = (dot(first[...], w[s, :, src]) + bias[s, :, dst]).astype(BF16)


def onehot_of(index_row, entries):
    ids = lax.broadcasted_iota(jnp.int32, (entries, index_row.shape[1]), 0)
    return jnp.where(ids == index_row, 1.0, 0.0).astype(BF16)


def bias_body(index, table, out):
    heads = out.shape[0] // PAD
    entries = table.shape[1]
    area = index.shape[0]

    @pl.loop(0, area)
    def _(j):
        hot = onehot_of(index[pl.ds(j, 1), :], entries)
        both = dot(table[...], hot)
        out[pl.ds(pl.multiple_of(j * heads, heads), heads), :] = both[:heads] + both[heads:]

    out[pl.ds(area * heads, (PAD - area) * heads), :] = jnp.full(
        ((PAD - area) * heads, out.shape[1]), -1e30, F32
    )


def rel_body(index, sums, out):
    heads = sums.shape[0] // PAD
    entries = out.shape[1]
    area = index.shape[0]
    out[...] = jnp.zeros_like(out)

    @pl.loop(0, area)
    def _(j):
        hot = onehot_of(index[pl.ds(j, 1), :], entries)
        s = sums[pl.ds(pl.multiple_of(j * heads, heads), heads), :]
        top = s.astype(BF16)
        low = (s - top.astype(F32)).astype(BF16)
        both = dot_nt(jnp.concatenate([top, low], 0), hot)
        out[...] += both[:heads] + both[heads:]


def head_masks(rows, width, dim):
    lane = lax.broadcasted_iota(jnp.int32, (rows, width), 1) // dim
    return [lane == h for h in range(width // dim)]


def stacked(block, masks):
    return jnp.concatenate([jnp.where(m, block, 0.0).astype(BF16) for m in masks], 0)


def attention_body(dim, heads, q, k, v, bias, out, lse):
    g = pl.program_id(0)
    width = q.shape[1]
    per = width // dim
    windows = q.shape[0] // PAD
    scale = dim ** (-0.5)
    masks = head_masks(PAD, width, dim)
    for w in range(windows):
        rows = pl.ds(w * PAD, PAD)
        kst = stacked(k[rows, :], masks)
        s_all = dot_nt(kst, q[rows, :])
        vt = v[rows, :].T
        outs = []
        for h in range(per):
            b = bias[pl.ds(g * per + h, PAD, stride=heads), :][:, :PAD]
            s = s_all[h * PAD : (h + 1) * PAD] * scale + b
            top = jnp.max(s, 0, keepdims=True)
            e = jnp.exp(s - top)
            total = jnp.sum(e, 0, keepdims=True)
            p = (e * (1.0 / total)).astype(BF16)
            lse[0, pl.ds(w * per + h, 1), :] = top + jnp.log(total)
            outs.append(dot(vt[h * dim : (h + 1) * dim], p))
        out[rows, :] = jnp.concatenate(outs, 0).T.astype(BF16)


def attention_back_body(dim, heads, q, k, v, do, bias, lse, dq, dk, dv, sums, vec):
    g = pl.program_id(0)
    width = q.shape[1]
    per = width // dim
    windows = q.shape[0] // PAD
    scale = dim ** (-0.5)
    masks = head_masks(PAD, width, dim)
    q_sum = jnp.zeros((1, width), F32)
    v_sum = jnp.zeros((1, width), F32)
    for w in range(windows):
        rows = pl.ds(w * PAD, PAD)
        kb, vb, qb, gb = k[rows, :], v[rows, :], q[rows, :], do[rows, :]
        s_all = dot_nt(stacked(kb, masks), qb)
        dp_all = dot_nt(stacked(vb, masks), gb)
        kt = kb.T
        p_parts, g_parts, dqs = [], [], []
        for h in range(per):
            at = pl.ds(g * per + h, PAD, stride=heads)
            b = bias[at, :][:, :PAD]
            p = jnp.exp(
                s_all[h * PAD : (h + 1) * PAD] * scale + b - lse[0, pl.ds(w * per + h, 1), :]
            )
            dp = dp_all[h * PAD : (h + 1) * PAD]
            inner = jnp.sum(dp * p, 0, keepdims=True)
            gs = (p * (dp - inner)).astype(BF16)
            gf = gs.astype(F32)
            if w == 0:
                sums[at, pl.ds(0, PAD)] = gf
            else:
                sums[at, pl.ds(0, PAD)] += gf
            p_parts.append(p.astype(BF16))
            g_parts.append(gs)
            dqs.append(dot(kt[h * dim : (h + 1) * dim], gs))
        dv_all = dot(jnp.concatenate(p_parts, 0), gb)
        dk_all = dot(jnp.concatenate(g_parts, 0), qb)
        dv_w = dv_all[:PAD]
        dk_w = dk_all[:PAD]
        for h in range(1, per):
            dv_w = jnp.where(masks[h], dv_all[h * PAD : (h + 1) * PAD], dv_w)
            dk_w = jnp.where(masks[h], dk_all[h * PAD : (h + 1) * PAD], dk_w)
        dq_w = (jnp.concatenate(dqs, 0).T * scale).astype(BF16)
        dv_w = dv_w.astype(BF16)
        dq[rows, :] = dq_w
        dk[rows, :] = (dk_w * scale).astype(BF16)
        dv[rows, :] = dv_w
        q_sum += jnp.sum(dq_w.astype(F32), 0, keepdims=True)
        v_sum += jnp.sum(dv_w.astype(F32), 0, keepdims=True)
    vec[...] = jnp.concatenate([q_sum, v_sum], 0)


def proj_body(att, w_own, w_oth, pb, stream0, g2, s2, stream1, second):
    rows, model = stream0.shape
    half = w_own.shape[0]

    @pl.loop(0, model // 256)
    def _(c):
        cols = pl.ds(pl.multiple_of(c * 256, 256), 256)
        value = dot(att[:, :half], w_own[:, cols]) + dot(att[:, half:], w_oth[:, cols])
        stream1[:, cols] = stream0[:, cols] + (value + pb[:, cols])

    def norm(r):
        x = stream1[r, :]
        mean, scale = stats(x, model)
        second[r, :] = ((x - mean) * scale * g2[...] + s2[...]).astype(BF16)

    row_loop(rows, 32, norm)


def mlp_body(
    t_ref, sec_own, sec_sib, cot_own, cot_oth, keep, s1, w1, b1, w2,
    wg1, wg2, gb1, gb2, feed, g2_sib, g2_own, d_out,
    gf, gft, sect, facc, gacc,
):
    t = t_ref[0]
    c = pl.program_id(0)
    rows, model = sec_own.shape
    half = model // 2

    @pl.when(c == 0)
    def _():
        own_cols = pl.ds(pl.multiple_of(t * half, half), half)
        oth_cols = pl.ds(pl.multiple_of((1 - t) * half, half), half)
        total = jnp.zeros((1, half), F32)
        for side, who in ((0, t), (1, 1 - t)):
            mine = cot_own[who].astype(F32) * keep[who]
            gf[side, :, own_cols] = mine.astype(BF16)
            gf[side, :, oth_cols] = (cot_oth[who].astype(F32) * keep[who]).astype(BF16)
            total += jnp.sum(mine, 0, keepdims=True)
        gb2[...] = total
        d_out[...] = gf[0]
        for side, sec in ((0, sec_own), (1, sec_sib)):

            @pl.loop(0, model // 128)
            def _(b):
                at = pl.ds(pl.multiple_of(b * 128, 128), 128)
                gft[side, at, :] = gf[side, :, at].T
                sect[side, at, :] = sec[:, at].T

        facc[...] = jnp.zeros_like(facc)
        gacc[...] = jnp.zeros_like(gacc)

    size = w1.shape[1]
    acts, ghs = [], []
    bias_sum = jnp.zeros((1, size), F32)
    for side, sec in ((0, sec_own), (1, sec_sib)):
        hidden = dot(sec[...], w1[...]) + b1[...]
        d_act = dot_nt(gf[side], w2[...])
        cdf = 0.5 * (1.0 + lax.erf(hidden * 0.7071067811865476))
        pdf = jnp.exp(hidden * hidden * -0.5) * 0.3989422804014327
        act = (hidden * cdf).astype(BF16)
        gh = (d_act * (cdf + hidden * pdf)).astype(BF16)
        bias_sum += jnp.sum(gh.astype(F32), 0, keepdims=True)
        facc[side] += dot(act, w2[...])
        gacc[side] += dot_nt(gh, w1[...])
        acts.append(act)
        ghs.append(gh)
    gb1[...] = bias_sum
    wg1[...] = (dot(sect[0], ghs[0]) + dot(sect[1], ghs[1])).astype(BF16)
    wg2[...] = (dot(gft[0], acts[0]) + dot(gft[1], acts[1])).astype(BF16)

    @pl.when(c == pl.num_programs(0) - 1)
    def _():
        own_cols = pl.ds(pl.multiple_of(t * half, half), half)
        oth_cols = pl.ds(pl.multiple_of((1 - t) * half, half), half)
        feed[0, t] = facc[0, :, own_cols] + s1[:, own_cols]
        feed[0, 1 - t] = facc[1, :, own_cols]
        feed[1, t] = facc[0, :, oth_cols] + s1[:, oth_cols]
        feed[1, 1 - t] = facc[1, :, oth_cols]
        g2_own[...] = gacc[0]
        g2_sib[...] = gacc[1].astype(BF16)


def norm_back(e, x, gain, width):
    mean, scale = stats(x, width)
    xhat = (x - mean) * scale
    scaled = e * gain
    first = jnp.sum(scaled, 1, keepdims=True) * (1.0 / width)
    cross = jnp.sum(scaled * xhat, 1, keepdims=True) * (1.0 / width)
    return scale * (scaled - first - xhat * cross), e * xhat


def norm2_back_body(
    g_own, g_recv, stream1, d_out, g2, w_own, w_oth, d_s1, g_att, g_attended, vec
):
    rows, model = g_own.shape
    half = w_own.shape[0]
    vec[...] = jnp.zeros_like(vec)

    def norm(r):
        e = g_own[r, :] + g_recv[r, :].astype(F32)
        dv, ex = norm_back(e, stream1[r, :], g2[...], model)
        d = d_out[r, :].astype(F32) + dv
        d_s1[r, :] = d
        low = d.astype(BF16)
        g_att[r, :] = low
        vec[0:1, :] += jnp.sum(ex, 0, keepdims=True)
        vec[1:2, :] += jnp.sum(e, 0, keepdims=True)
        vec[2:3, :] += jnp.sum(low.astype(F32), 0, keepdims=True)

    row_loop(rows, 32, norm)
    for side, w in enumerate((w_own, w_oth)):

        @pl.loop(0, half // 256)
        def _(c):
            src = pl.ds(pl.multiple_of(c * 256, 256), 256)
            dst = pl.ds(pl.multiple_of(side * half + c * 256, 256), 256)
            g_attended[:, dst] = dot_nt(g_att[...], w[src, :]).astype(BF16)


def norm1_back_body(dq, dk, dv, w_own, w_oth, stream0, d_s1, g1, d_s0, g_s0, vec, acc):
    rows, model = stream0.shape
    half = w_own.shape[2]
    vec[...] = jnp.zeros_like(vec)

    @pl.loop(0, model // 256)
    def _(c):
        at = pl.ds(pl.multiple_of(c * 256, 256), 256)
        value = jnp.zeros((rows, 256), F32)
        for s, d in enumerate((dq, dk, dv)):
            value += dot_nt(d[:, :half], w_own[s, at, :])
            value += dot_nt(d[:, half:], w_oth[s, at, :])
        acc[:, at] = value

    def norm(r):
        e = acc[r, :]
        d, ex = norm_back(e, stream0[r, :], g1[...], model)
        d = d_s1[r, :] + d
        d_s0[r, :] = d.astype(BF16)
        g_s0[r, :] = d.astype(BF16)
        vec[0:1, :] += jnp.sum(ex, 0, keepdims=True)
        vec[1:2, :] += jnp.sum(e, 0, keepdims=True)

    row_loop(rows, 32, norm)


def merge_back_body(t_ref, g_s0, w_own, w_oth, x_ref, mg, d_merged, vec, acc):
    t = t_ref[0]
    rows = g_s0.shape[0]
    half = w_own.shape[0]
    width = 2 * half
    vec[...] = jnp.zeros_like(vec)
    for side, w in enumerate((w_own, w_oth)):

        @pl.loop(0, half // 256)
        def _(c):
            at = pl.ds(pl.multiple_of(c * 256, 256), 256)
            acc[side, :, at] = dot_nt(g_s0[...], w[at, :])

    def norm(r):
        xs = [x_ref[t, r, :].astype(F32), x_ref[1 - t, r, :].astype(F32)]
        es = [acc[0, r, :], acc[1, r, :]]
        gains = [mg[t], mg[1 - t]]
        total = sum(jnp.sum(x, 1, keepdims=True) for x in xs)
        square = sum(jnp.sum(x * x, 1, keepdims=True) for x in xs)
        mean = total * (1.0 / width)
        scale = lax.rsqrt(square * (1.0 / width) - mean * mean + EPS)
        hats = [(x - mean) * scale for x in xs]
        scaled = [e * g for e, g in zip(es, gains)]
        first = sum(jnp.sum(s, 1, keepdims=True) for s in scaled) * (1.0 / width)
        cross = sum(jnp.sum(s * h, 1, keepdims=True) for s, h in zip(scaled, hats)) * (1.0 / width)
        for side, who in ((0, t), (1, 1 - t)):
            d_merged[who, r, :] = scale * (scaled[side] - first - hats[side] * cross)
            vec[2 * side : 2 * side + 1, :] += jnp.sum(es[side] * hats[side], 0, keepdims=True)
            vec[2 * side + 1 : 2 * side + 2, :] += jnp.sum(es[side], 0, keepdims=True)

    row_loop(rows, 16, norm)


def weight_grad_body(l_own, l_sib, r_own, r_sib, out, lt):
    for side, l in enumerate((l_own, l_sib)):

        @pl.loop(0, l.shape[1] // 128)
        def _(b):
            at = pl.ds(pl.multiple_of(b * 128, 128), 128)
            lt[side, at, :] = l[:, at].T

    @pl.loop(0, out.shape[1] // 256)
    def _(c):
        at = pl.ds(pl.multiple_of(c * 256, 256), 256)
        out[:, at] = (dot(lt[0], r_own[:, at]) + dot(lt[1], r_sib[:, at])).astype(BF16)


def weight_grad(l_own, l_sib, r_own, r_sib):
    rows, model = l_own.shape
    n = r_own.shape[1]
    return whole(
        weight_grad_body,
        shape((model, n), BF16),
        (l_own, l_sib, r_own, r_sib),
        [pltpu.VMEM((2, model, rows), BF16)],
        flops=4 * rows * model * n,
        nbytes=2 * (2 * rows * (model + n) + model * n),
    )


def swap(value):
    return lax.ppermute(value, "tp", [(0, 1), (1, 0)])


def take(value, index):
    return lax.dynamic_index_in_dim(value, index, 0, keepdims=False)


class Grid:
    def __init__(self, count):
        side = 1
        while 4 * (side + 1) * (side + 1) <= count:
            side += 1
        self.sizes = {"z": count // (side * side), "y": side, "x": side}
        self.strides = {"z": side * side, "y": side, "x": 1}
        self.count = count

    def place(self, axis):
        me = lax.axis_index("win")
        return (me // self.strides[axis]) % self.sizes[axis]

    def shift(self, value, axis, delta, senders):
        stride, size = self.strides[axis], self.sizes[axis]
        pairs = []
        for w in range(self.count):
            c = (w // stride) % size
            if c in senders:
                pairs.append((w, w + delta * stride))
        return lax.ppermute(value, "win", pairs)

    def chain(self, value, axis):
        size = self.sizes[axis]
        c = self.place(axis)
        right = left = None
        for s in range(1, size):
            go_right = take(value, jnp.clip(size - s + c, 0, size - 1))
            go_left = take(value, jnp.clip(c - 1 - (size - 1 - s), 0, size - 1))
            if s > 1:
                go_right = (go_right.astype(F32) + right.astype(F32)).astype(BF16)
                go_left = (go_left.astype(F32) + left.astype(F32)).astype(BF16)
            right = self.shift(go_right, axis, 1, range(0, min(s, size - 1)))
            left = self.shift(go_left, axis, -1, range(max(size - s, 1), size))
        return take(value, c).astype(F32) + right.astype(F32) + left.astype(F32)

    def scatter(self, value, order):
        sizes = self.sizes
        v = value.reshape(sizes["z"], sizes["y"], sizes["x"], -1, value.shape[1])
        left = ["z", "y", "x"]
        for step, axis in enumerate(order):
            v = self.chain(jnp.moveaxis(v, left.index(axis), 0), axis)
            left.remove(axis)
            if step < 2:
                v = v.astype(BF16)
        return v

    def total(self, value):
        for axis in ("x", "y", "z"):
            size, stride = self.sizes[axis], self.strides[axis]
            hop = 1
            while hop < size:
                pairs = []
                for w in range(self.count):
                    c = (w // stride) % size
                    pairs.append((w, w + ((c ^ hop) - c) * stride))
                value = value + lax.ppermute(value, "win", pairs)
                hop *= 2
        return value


def solution(mesh):
    count = mesh.shape["win"]

    def shards(
        pixels, merge_gain, merge_shift, merge_weight, norm1_gain, norm1_shift, qkv_weight,
        qkv_bias, rel_table, proj_weight, proj_bias, norm2_gain, norm2_shift, fc1_weight,
        fc1_bias, fc2_weight, fc2_bias, rel_index, keep, cotangent,
    ):
        grid = Grid(count)
        t = lax.axis_index("tp")
        t_arr = t.reshape(1).astype(jnp.int32)
        wins, height, _, channels = pixels.shape
        side = height // 2
        area = side * side
        rows = wins * PAD
        model = merge_weight.shape[1]
        half = model // 2
        heads_here = rel_table.shape[1]
        heads = 2 * heads_here
        dim = half // heads_here
        entries = rel_table.shape[0]
        slots = -(-entries // 128) * 128
        hidden = fc1_weight.shape[1]

        def pair(own, oth):
            return jnp.where(
                t == 0, jnp.concatenate([own, oth], -1), jnp.concatenate([oth, own], -1)
            )

        flat = [
            merge_gain, merge_shift, norm1_gain, norm1_shift, qkv_bias, rel_table.T,
            proj_bias, norm2_gain, norm2_shift,
        ]
        packed = jnp.concatenate([f.reshape(-1) for f in flat])
        got = swap(packed)
        others, at = [], 0
        for f in flat:
            others.append(got[at : at + f.size].reshape(f.shape))
            at += f.size
        wm_oth = swap(merge_weight)
        wqkv = qkv_weight.transpose(1, 0, 2)
        wqkv_oth = swap(wqkv)
        wp_oth = swap(proj_weight)
        mg = pair(merge_gain, others[0]).reshape(2, 1, model)
        ms = pair(merge_shift, others[1]).reshape(2, 1, model)
        g1 = pair(norm1_gain, others[2]).reshape(1, model)
        s1 = pair(norm1_shift, others[3]).reshape(1, model)
        qb = jnp.concatenate([qkv_bias, others[4]], -1)
        qb = jnp.stack([qb[0], jnp.zeros_like(qb[0]), qb[1]]).reshape(3, 1, model)
        pb = pair(proj_bias, others[6]).reshape(1, model)
        g2 = pair(norm2_gain, others[7]).reshape(1, model)
        s2 = pair(norm2_shift, others[8]).reshape(1, model)
        table = jnp.concatenate([rel_table.T, others[5].reshape(rel_table.T.shape)], 0)
        table = jnp.pad(table, ((0, 0), (0, slots - entries)))
        top = table.astype(BF16)
        table2 = jnp.concatenate([top, (table - top.astype(F32)).astype(BF16)], 0)

        x = (
            pixels.reshape(wins, side, 2, side, 2, channels)
            .transpose(4, 0, 1, 3, 2, 5)
            .reshape(2, wins, area, model)
        )
        x = jnp.pad(x, ((0, 0), (0, 0), (0, PAD - area), (0, 0))).reshape(2, rows, model)
        stream0, mn_own, mn_oth, first = whole(
            merge_body,
            (shape((rows, model)), shape((rows, model), BF16), shape((rows, model), BF16),
             shape((rows, model), BF16)),
            (t_arr, x, merge_weight, wm_oth, mg, ms, g1, s1),
            flops=4 * rows * model * model, nbytes=1e7, smem_first=True,
        )
        first_sib = swap(first)
        mn_sib = swap(mn_oth)
        qkv = whole(
            qkv_body, shape((3, rows, model), BF16), (first, wqkv, wqkv_oth, qb),
            flops=6 * rows * model * model, nbytes=1e7,
        )
        index_t = jnp.pad(rel_index.T, ((0, 0), (0, PAD - area)))
        bias = whole(
            bias_body, shape((PAD * heads, PAD)), (index_t, table2),
            flops=4 * heads * slots * area * 128, nbytes=2e6,
        )
        groups = model // 128
        per = 128 // dim
        lanes = pl.BlockSpec((rows, 128), lambda g: (0, g))

        def slot(s):
            return pl.BlockSpec((None, rows, 128), lambda g: (s, 0, g))

        lse_spec = pl.BlockSpec((1, wins * per, PAD), lambda g: (g, 0, 0))

        def attention(*refs):
            attention_body(dim, heads, *refs)

        attended, lse = call(
            attention,
            (shape((rows, model), BF16), shape((groups, wins * per, PAD))),
            (qkv, qkv, qkv, bias),
            flops=4 * rows * model * 448, nbytes=6e6,
            grid=(groups,),
            in_specs=[slot(0), slot(1), slot(2), VMEM],
            out_specs=(lanes, lse_spec),
        )
        att_sib = swap(attended[:, half:])
        stream1, second = whole(
            proj_body, (shape((rows, model)), shape((rows, model), BF16)),
            (attended, proj_weight, wp_oth, pb, stream0, g2, s2),
            flops=2 * rows * model * model, nbytes=8e6,
        )
        second_sib = swap(second)
        cot = jnp.pad(
            cotangent.reshape(2 * wins, area, half), ((0, 0), (0, PAD - area), (0, 0))
        ).reshape(2, rows, half)
        cot_oth = swap(cot)
        keep_rows = jnp.pad(
            keep.astype(F32).reshape(2 * wins, area), ((0, 0), (0, PAD - area))
        ).reshape(2, rows, 1)
        chunk = 512
        col_spec = pl.BlockSpec((model, chunk), lambda c: (0, c))
        row_spec = pl.BlockSpec((1, chunk), lambda c: (0, c))
        wg1, wg2, gb1, gb2, feed, g2_send, g2_own, d_out = call(
            mlp_body,
            (
                shape((model, hidden), BF16), shape((model, hidden), BF16), shape((1, hidden)),
                shape((1, half)), shape((2, 2, rows, half)), shape((rows, model), BF16),
                shape((rows, model)), shape((rows, model), BF16),
            ),
            (t_arr, second, second_sib, cot, cot_oth, keep_rows, stream1, fc1_weight,
             fc1_bias.reshape(1, hidden), fc2_weight),
            [
                pltpu.VMEM((2, rows, model), BF16), pltpu.VMEM((2, model, rows), BF16),
                pltpu.VMEM((2, model, rows), BF16), pltpu.VMEM((2, rows, model), F32),
                pltpu.VMEM((2, rows, model), F32),
            ],
            flops=24 * rows * model * hidden, nbytes=3e7,
            grid=(hidden // chunk,),
            in_specs=[SMEM, VMEM, VMEM, VMEM, VMEM, VMEM, VMEM, col_spec, row_spec,
                      pl.BlockSpec((chunk, model), lambda c: (c, 0))],
            out_specs=(col_spec, col_spec, row_spec, VMEM, VMEM, VMEM, VMEM, VMEM),
        )
        g2_recv = swap(g2_send)
        feed_recv = swap(feed[1].astype(BF16))
        out = keep_rows * (feed[0] + feed_recv.astype(F32) + fc2_bias)
        out = out.reshape(2 * wins, PAD, half)[:, :area].reshape(2 * wins * area, half).astype(BF16)
        fc1_grad = grid.scatter(wg1, ("x", "y", "z"))
        fc2_grad = grid.scatter(wg2, ("y", "x", "z")).T

        d_s1, g_att, g_attended, vec2 = whole(
            norm2_back_body,
            (shape((rows, model)), shape((rows, model), BF16), shape((rows, model), BF16),
             shape((3, model))),
            (g2_own, g2_recv, stream1, d_out, g2, proj_weight, wp_oth),
            flops=2 * rows * model * model, nbytes=1e7,
        )
        g_att_sib = swap(g_att)

        def attention_back(*refs):
            attention_back_body(dim, heads, *refs)

        dq, dk, dv, sums, qkv_sums = call(
            attention_back,
            (
                shape((rows, model), BF16), shape((rows, model), BF16), shape((rows, model), BF16),
                shape((PAD * heads, PAD)), shape((2, model)),
            ),
            (qkv, qkv, qkv, g_attended, bias, lse),
            flops=10 * rows * model * 448, nbytes=1e7,
            grid=(groups,),
            in_specs=[slot(0), slot(1), slot(2), lanes, VMEM, lse_spec],
            out_specs=(lanes, lanes, lanes, VMEM, pl.BlockSpec((2, 128), lambda g: (0, g))),
        )
        proj_part = weight_grad(g_att, g_att_sib, attended[:, :half], att_sib)
        d_qkv = jnp.concatenate([dq[:, :half], dk[:, :half], dv[:, :half]], 1)
        d_qkv_sib = swap(jnp.concatenate([dq[:, half:], dk[:, half:], dv[:, half:]], 1))
        qkv_part = weight_grad(first, first_sib, d_qkv, d_qkv_sib)
        d_s0, g_s0, vec1 = whole(
            norm1_back_body,
            (shape((rows, model), BF16), shape((rows, model), BF16), shape((2, model))),
            (dq, dk, dv, wqkv, wqkv_oth, stream0, d_s1, g1),
            [pltpu.VMEM((rows, model), F32)],
            flops=6 * rows * model * model, nbytes=1e7,
        )
        g_s0_sib = swap(g_s0)
        rel_sums = whole(
            rel_body, shape((heads, slots)), (index_t, sums),
            flops=4 * heads * slots * area * 128, nbytes=2e6,
        )
        merge_part = weight_grad(g_s0, g_s0_sib, mn_own, mn_sib)
        d_merged, vec0 = whole(
            merge_back_body,
            (shape((2, rows, model)), shape((4, model))),
            (t_arr, g_s0, merge_weight, wm_oth, x, mg),
            [pltpu.VMEM((2, rows, model), F32)],
            flops=4 * rows * model * model, nbytes=1e7, smem_first=True,
        )
        pixels_grad = (
            d_merged.reshape(2, wins, PAD, 2, channels)[:, :, :area]
            .reshape(2, wins, side, side, 2, channels)
            .transpose(1, 2, 4, 3, 0, 5)
            .reshape(pixels.shape)
        )
        a_part = jnp.concatenate([proj_part, qkv_part[:, :half]], 1)
        b_part = qkv_part[:, half:]
        a_sum = grid.scatter(a_part, ("x", "y", "z"))
        b_sum = grid.scatter(b_part, ("y", "x", "z"))
        ma_sum = grid.scatter(merge_part[:, :half], ("x", "y", "z"))
        mb_sum = grid.scatter(merge_part[:, half:], ("y", "x", "z"))
        proj_grad = a_sum[:, :half].T
        qkv_grad = jnp.stack([a_sum[:, half:], b_sum[:, :half], b_sum[:, half:]], 1)
        merge_grad = jnp.concatenate([ma_sum, mb_sum], 1).T

        def sides(v):
            both = jnp.stack([v[..., :half], v[..., half:]])
            return take(both, t), take(both, 1 - t)

        n2, n1 = sides(vec2), sides(vec1)
        rel = rel_sums[:, :entries]
        keepers = [
            vec0[0:2], n1[0], qkv_sums[:, :half], rel[:heads_here], n2[0]
        ]
        leavers = [
            vec0[2:4], n1[1], qkv_sums[:, half:], rel[heads_here:], n2[1]
        ]
        back = swap(jnp.concatenate([v.reshape(-1) for v in leavers]))
        mine = jnp.concatenate([v.reshape(-1) for v in keepers]) + back
        vectors = grid.total(jnp.concatenate([mine, gb1.reshape(-1), gb2.reshape(-1)]))
        parts, at = [], 0
        for v in keepers + [gb1, gb2]:
            parts.append(vectors[at : at + v.size].reshape(v.shape))
            at += v.size
        v0, v1, vq, vr, v2, vb1, vb2 = parts
        return (
            out, pixels_grad, v0[0], v0[1], merge_grad, v1[0], v1[1], qkv_grad, vq, vr.T,
            proj_grad, v2[2], v2[0], v2[1], fc1_grad, vb1[0], fc2_grad, vb2[0],
        )

    in_specs = (
        P(("win", "tp"), None, None, None), P("tp"), P("tp"), P("tp", None), P("tp"), P("tp"),
        P(None, None, "tp"), P(None, "tp"), P(None, "tp"), P("tp", None), P("tp"), P("tp"),
        P("tp"), P(None, "tp"), P("tp"), P("tp", None), P("tp"), P(), P("win"), P("win", "tp"),
    )
    out_specs = (
        P("win", "tp"), P(("win", "tp"), None, None, None), P("tp"), P("tp"), P("tp", "win"),
        P("tp"), P("tp"), P("win", None, "tp"), P(None, "tp"), P(None, "tp"), P("tp", "win"),
        P("tp"), P("tp"), P("tp"), P("win", "tp"), P("tp"), P("tp", "win"), P("tp"),
    )
    return jax.shard_map(shards, mesh=mesh, in_specs=in_specs, out_specs=out_specs, check_vma=False)
```

time: 1000 us -> 564 us (0.56)
  waiting for transfers between devices: 606 us -> 76 us
  Pallas kernels: 0 us -> 200 us
  starting transfers between devices: 2.3 us -> 180 us
  matrix products: 143 us -> 0 us
  blocking collectives: 106 us -> 0 us
  other arithmetic: 47.2 us -> 28.6 us
  between operations: 14.7 us -> 2.54 us
    reduce_scatter x10 -> x0, waiting for transfers between devices: 583 us -> none  [the longest x1 183 us: shards(): lax.psum_scatter(fc1_weight_grad, 'win', scatter_dimension=0, tiled=True)]
    pallas_call x0 -> x14, Pallas kernels: none -> 200 us  [call(): pl.pallas_call(body, out_shape=out, scratch_shapes=list(scratch), compile...]
    ppermute x0 -> x79, starting transfers between devices: none -> 180 us  [the longest x60 167 us: shift(): return lax.ppermute(value, 'win', pairs)]
    dot_general x23 -> x0, matrix products: 143 us -> none  [the longest x5 43.4 us: times_transposed(): lax.dot_general(left, right, (((1,), (1,)), ((), ())), preferred_element_...]
    psum x7 -> x0, blocking collectives: 94.4 us -> none  [the longest x1 79.4 us: shards(): lax.psum((merge_gain_grad, merge_shift_grad, norm1_gain_grad, norm1_shift...]
    ppermute x0 -> x79, waiting for transfers between devices: none -> 76 us  [the longest x60 70.6 us: shift(): return lax.ppermute(value, 'win', pairs)]
    reduce_sum x10 -> x0, other arithmetic: 24.7 us -> none  [the longest x2 5.13 us: norm_grads(): return (scaled, local, jnp.sum(grad * centred, 0), jnp.sum(grad, 0))]
    all_gather x5 -> x0, waiting for transfers between devices: 23.4 us -> none  [the longest x3 15.2 us: gather_grad(): return lax.all_gather(grad_low, 'tp', axis=1, tiled=True)]
  transfers between devices with their start and end apart: 15 -> 79, of which waited for: 11 -> 25; matrix products, arithmetic and copies ran while one was open for 11% -> 16% of each run, Pallas kernels for 0% -> 36%
where the time goes in v1:
time: 564 us; the launch traced here: 556 us
  Pallas kernels  200 us (35%)
  starting transfers between devices  180 us (32%)
  waiting for transfers between devices  76 us (13%)
  local copies, waits for them, and re-layouts  68.5 us (12%)
  other arithmetic  28.6 us (5%)
    pallas_call x14, Pallas kernels, call(): pl.pallas_call(body, out_shape=out, scratch_shapes=list(scratch), compile...  200 us
    ppermute x60, starting transfers between devices, shift(): return lax.ppermute(value, 'win', pairs)  167 us
    ppermute x60, waiting for transfers between devices, shift(): return lax.ppermute(value, 'win', pairs)  70.6 us
    another operation x18, local copies, waits for them, and re-layouts  19.4 us
    convert_element_type x12, other arithmetic, scatter(): v = v.astype(BF16)  14.1 us
  transfers between devices with their start and end apart: 79, of which 25 were waited for; matrix products, arithmetic and copies ran while one was open for 16% of the time, Pallas kernels for 36%

profile of v1, /device:TPU:0, one launch (start us, length us, event | category | flops | bytes accessed | tf_op | source)
XLA Modules:
  0.0 555.9 jit_solution(18045032201734338677)
XLA Ops:
  16.2 17.4 %shard_map.333.refs_3_.refs_4_ = f32[3584,112]{1,0:T(8,128)} custom-call(s32[100,112]{1,0:T(8,128)} %pad.22.index, bf16[64,384]{1,0:T(8,128)(2,1)} %pad_maximum_fusion.4.table), custom_call_target="tpu_custom_call" | custom-call | flops 629145600 | bytes 2000000 | tf_op jit(solution)/shard_map/pallas_call | solution.py:18
  36.0 11.3 %shard_map.331 = (f32[448,1024]{1,0:T(8,128)}, bf16[448,1024]{1,0:T(8,128)(2,1)}, bf16[448,1024]{1,0:T(8,128)(2,1)}, bf16[448,1024]{1,0:T(8,128)(2,1)}) custom-call(s32[1]{0:T(128)} %bitcast.t_ref, bf16[2,448,1024]{2,1,0:T(8,128)(2,1)} %bitcast.321, bf16[1024,1024]{1,0:T(8,128)(2,1)} %w_own.7, bf16[1024,1024]{1,0:T(8,128)(2,1)} %collective-permute-done.w_oth, ...), custom_call_target="tpu_custom_call" | custom-call | flops 1879048192 | bytes 10000000 | tf_op jit(solution)/shard_map/pallas_call | solution.py:18
  47.3 9.6 %shard_map.332.refs_0_.refs_1_.refs_2_ = bf16[3,448,1024]{2,1,0:T(8,128)(2,1)} custom-call(bf16[448,1024]{1,0:T(8,128)(2,1)} %get-tuple-element.47.first.l_own, bf16[3,1024,512]{2,1,0:T(8,128)(2,1)} %bitcast.329, bf16[3,1024,512]{2,1,0:T(8,128)(2,1)} %collective-permute-done.2.w_oth, f32[3,1,1024]{2,1,0:T(1,128)} %reshape.733.bias), custom_call_target="tpu_custom_call" | custom-call | flops 2818572288 | bytes 10000000 | tf_op jit(solution)/shard_map/pallas_call | solution.py:18
  56.9 12.9 %shard_map.334 = (bf16[448,1024]{1,0:T(8,128)(2,1)}, f32[8,16,112]{2,1,0:T(8,128)}) custom-call(bf16[3,448,1024]{2,1,0:T(8,128)(2,1)} %shard_map.332.refs_0_.refs_1_.refs_2_, bf16[3,448,1024]{2,1,0:T(8,128)(2,1)} %shard_map.332.refs_0_.refs_1_.refs_2_, bf16[3,448,1024]{2,1,0:T(8,128)(2,1)} %shard_map.332.refs_0_.refs_1_.refs_2_, ...), custom_call_target="tpu_custom_call" | custom-call | flops 822083584 | bytes 6000000 | tf_op jit(solution)/shard_map/pallas_call | solution.py:18
  69.8 7.1 %shard_map.335 = (f32[448,1024]{1,0:T(8,128)}, bf16[448,1024]{1,0:T(8,128)(2,1)}) custom-call(bf16[448,1024]{1,0:T(8,128)(2,1)} %get-tuple-element.48.att, bf16[512,1024]{1,0:T(8,128)(2,1)} %w_own.6, bf16[512,1024]{1,0:T(8,128)(2,1)} %collective-permute-done.3.w_oth, f32[1,1024]{1,0:T(1,128)} %get-tuple-element.178.pb, ...), custom_call_target="tpu_custom_call" | custom-call | flops 939524096 | bytes 8000000 | tf_op jit(solution)/shard_map/pallas_call | solution.py:18
  80.6 36.2 %shard_map.336 = (bf16[1024,2048]{1,0:T(8,128)(2,1)}, bf16[1024,2048]{1,0:T(8,128)(2,1)}, f32[1,2048]{1,0:T(1,128)}, f32[1,512]{1,0:T(1,128)}, f32[2,2,448,512]{...) custom-call(s32[1]{0:T(128)} %bitcast.t_ref, ...), custom_call_target="tpu_custom_call" | custom-call | flops 22548578304 | bytes 30000000 | tf_op jit(solution)/shard_map/pallas_call | solution.py:18
  121.0 3.8 constant_dynamic-slice_fusion.9
  129.3 7.2 %collective-permute-start.59 = (bf16[4,2,64,2048]{3,2,0,1:T(8,128)(2,1)}, bf16[4,2,64,2048]{3,2,0,1:T(8,128)(2,1)}, u32[]{:S(2)}, u32[]{:S(2)}) collective-permute-start(bf16[4,2,64,2048]{3,2,0,1:T(8,128)(2,1)} %bitcast.304), channel_id=1, source_target_pairs={{0,2},{4,6},{8,10},{12,14},{16,18},{20,22},{24,26},{28,30},{1,3},{... | collective-permute-start | bytes 6291464 | tf_op jit(solution)/shard_map/ppermute | solution.py:465
  137.4 10.1 %shard_map.337 = (f32[448,1024]{1,0:T(8,128)}, bf16[448,1024]{1,0:T(8,128)(2,1)}, bf16[448,1024]{1,0:T(8,128)(2,1)}, f32[3,1024]{1,0:T(4,128)}) custom-call(f32[448,1024]{1,0:T(8,128)} %get-tuple-element.53.g_own, bf16[448,1024]{1,0:T(8,128)(2,1)} %copy-done.12, f32[448,1024]{1,0:T(8,128)} %get-tuple-element.51.s1.stream1, ...), custom_call_target="tpu_custom_call" | custom-call | flops 939524096 | bytes 10000000 | tf_op jit(solution)/shard_map/pallas_call | solution.py:18
  147.5 25.8 %shard_map.338 = (bf16[448,1024]{1,0:T(8,128)(2,1)}, bf16[448,1024]{1,0:T(8,128)(2,1)}, bf16[448,1024]{1,0:T(8,128)(2,1)}, f32[3584,112]{1,0:T(8,128)}, f32[2,1024]{1,0:T(2,128)}) custom-call(bf16[3,448,1024]{2,1,0:T(8,128)(2,1)} %shard_map.332.refs_0_.refs_1_.refs_2_, bf16[3,448,1024]{2,1,0:T(8,128)(2,1)} %shard_map.332.refs_0_.refs_1_.refs_2_, ...), custom_call_target="tpu_custom_call" | custom-call | flops 2055208960 | bytes 10000000 | tf_op jit(solution)/shard_map/pallas_call | solution.py:18
  173.2 12.5 %shard_map.339 = (bf16[448,1024]{1,0:T(8,128)(2,1)}, bf16[448,1024]{1,0:T(8,128)(2,1)}, f32[2,1024]{1,0:T(2,128)}) custom-call(bf16[448,1024]{1,0:T(8,128)(2,1)} %get-tuple-element.58.dq, bf16[448,1024]{1,0:T(8,128)(2,1)} %get-tuple-element.59.dk, bf16[448,1024]{1,0:T(8,128)(2,1)} %get-tuple-element.60.dv, bf16[3,1024,512]{2,1,0:T(8,128)(2,1)} %bitcast.330, ...), custom_call_target="tpu_custom_call" | custom-call | flops 2818572288 | bytes 10000000 | tf_op jit(solution)/shard_map/pallas_call | solution.py:18
  185.8 14.7 %shard_map.340 = (f32[2,448,1024]{2,1,0:T(8,128)}, f32[4,1024]{1,0:T(4,128)}) custom-call(s32[1]{0:T(128)} %bitcast.t_ref, bf16[448,1024]{1,0:T(8,128)(2,1)} %get-tuple-element.62.g_s0.l_own, bf16[1024,1024]{1,0:T(8,128)(2,1)} %w_own.7, bf16[1024,1024]{1,0:T(8,128)(2,1)} %collective-permute-done.w_oth, bf16[2,448,1024]{2,1,0:T(8,128)(2,1)} %bitcast.322, ...), custom_call_target="tpu_custom_call" | custom-call | flops 1879048192 | bytes 10000000 | tf_op jit(solution)/shard_map/pallas_call | solution.py:18
  201.4 19.8 %shard_map.341 = f32[32,384]{1,0:T(8,128)} custom-call(s32[100,112]{1,0:T(8,128)} %pad.22.index, f32[3584,112]{1,0:T(8,128)} %get-tuple-element.67.sums), custom_call_target="tpu_custom_call" | custom-call | flops 629145600 | bytes 2000000 | tf_op jit(solution)/shard_map/pallas_call | solution.py:18
  222.3 5.3 constant_dynamic-slice_fusion.6
  245.1 3.5 collective-permute-start.12
  250.7 6.0 %reshape.740 = f32[2,4,112,2,512]{4,3,2,1,0:T(2,128)} reshape(f32[2,448,1024]{2,1,0:T(8,128)} %get-tuple-element.63) | data formatting | bytes 7340032 | tf_op jit(solution)/shard_map/reshape | solution.py:701
  258.6 3.8 copy.62
  267.8 7.2 %collective-permute-start.69 = (bf16[4,2,64,2048]{3,2,0,1:T(8,128)(2,1)}, bf16[4,2,64,2048]{3,2,0,1:T(8,128)(2,1)}, u32[]{:S(2)}, u32[]{:S(2)}) collective-permute-start(bf16[4,2,64,2048]{3,2,0,1:T(8,128)(2,1)} %bitcast.302), channel_id=1, source_target_pairs={{0,4},{2,6},{8,12},{10,14},{16,20},{18,22},{24,28},{26,30},{1,5},{... | collective-permute-start | bytes 6291464 | tf_op jit(solution)/shard_map/ppermute | solution.py:465
  278.3 7.8 %shard_map.342 = bf16[1024,1024]{1,0:T(8,128)(2,1)} custom-call(bf16[448,1024]{1,0:T(8,128)(2,1)} %get-tuple-element.62.g_s0.l_own, bf16[448,1024]{1,0:T(8,128)(2,1)} %collective-permute-done.13.l_sib, bf16[448,1024]{1,0:T(8,128)(2,1)} %get-tuple-element.71.r_own, bf16[448,1024]{1,0:T(8,128)(2,1)} %collective-permute-done.14.r_sib), custom_call_target="tpu_custom_call" | custom-call | flops 1879048192 | bytes 5767168 | tf_op jit(solution)/shard_map/pallas_call | solution.py:18
  291.5 5.6 %shard_map.343 = bf16[1024,512]{1,0:T(8,128)(2,1)} custom-call(bf16[448,1024]{1,0:T(8,128)(2,1)} %get-tuple-element.73.l_own, bf16[448,1024]{1,0:T(8,128)(2,1)} %copy-done.13, bf16[448,512]{1,0:T(8,128)(2,1)} %get-tuple-element.113.r_own, bf16[448,512]{1,0:T(8,128)(2,1)} %copy-done.15), custom_call_target="tpu_custom_call" | custom-call | flops 939524096 | bytes 3801088 | tf_op jit(solution)/shard_map/pallas_call | solution.py:18
  303.5 12.8 %collective-permute-done.70 = bf16[4,2,64,2048]{3,2,0,1:T(8,128)(2,1)} collective-permute-done((bf16[4,2,64,2048]{3,2,0,1:T(8,128)(2,1)}, bf16[4,2,64,2048]{3,2,0,1:T(8,128)(2,1)}, u32[]{:S(2)}, u32[]{:S(2)}) %collective-permute-start.70) | collective-permute-done | bytes 2097184 | tf_op jit(solution)/shard_map/ppermute | solution.py:465
  321.3 3.5 fusion.1
  326.0 6.2 %collective-permute-start.15 = (bf16[4,2,64,512]{3,2,0,1:T(8,128)(2,1)S(1)}, bf16[4,2,64,512]{3,2,0,1:T(8,128)(2,1)}, u32[]{:S(2)}, u32[]{:S(2)}) collective-permute-start(bf16[4,2,64,512]{3,2,0,1:T(8,128)(2,1)S(1)} %bitcast.336), channel_id=1, source_target_pairs={{0,2},{4,6},{8,10},{12,14},{16,18},{20,22},{24,26},{28,30},{1,3},{... | collective-permute-start | bytes 1572872 | tf_op jit(solution)/shard_map/ppermute | solution.py:465
  333.5 9.7 %shard_map.344 = bf16[1024,1536]{1,0:T(8,128)(2,1)} custom-call(bf16[448,1024]{1,0:T(8,128)(2,1)} %get-tuple-element.47.first.l_own, bf16[448,1024]{1,0:T(8,128)(2,1)} %collective-permute-done.37.l_sib, bf16[448,1536]{1,0:T(8,128)(2,1)} %pad_maximum_fusion.1.r_own, bf16[448,1536]{1,0:T(8,128)(2,1)} %collective-permute-done.38.r_sib), custom_call_target="tpu_custom_call" | custom-call | flops 2818572288 | bytes 7733248 | tf_op jit(solution)/shard_map/pallas_call | solution.py:18
  347.8 5.8 %collective-permute-start.61 = (bf16[4,64,2048]{2,1,0:T(8,128)(2,1)S(1)}, bf16[4,64,2048]{2,1,0:T(8,128)(2,1)S(1)}, u32[]{:S(2)}, u32[]{:S(2)}) collective-permute-start(bf16[4,64,2048]{2,1,0:T(8,128)(2,1)S(1)} %get-tuple-element.84), channel_id=1, source_target_pairs={{0,4},{2,6},{8,12},{10,14},{16,20},{18,22},{24,28},{26,30},{1,5},{... | collective-permute-start | bytes 3145736 | tf_op jit(solution)/shard_map/ppermute | solution.py:465
  357.7 4.6 collective-permute-start.27
  363.8 20.0 %collective-permute-done.28 = bf16[4,64,512]{2,1,0:T(8,128)(2,1)S(1)} collective-permute-done((bf16[4,64,512]{2,1,0:T(8,128)(2,1)S(1)}, bf16[4,64,512]{2,1,0:T(8,128)(2,1)S(1)}, u32[]{:S(2)}, u32[]{:S(2)}) %collective-permute-start.28) | collective-permute-done | bytes 262176 | tf_op jit(solution)/shard_map/ppermute | solution.py:465
  385.1 4.6 collective-permute-start.17
  397.2 4.4 collective-permute-start.19
  403.5 4.3 collective-permute-start.30
  409.6 4.3 collective-permute-start.20
  415.8 4.3 collective-permute-start.31
  422.2 7.9 %collective-permute-start.21 = (bf16[64,512]{1,0:T(8,128)(2,1)S(1)}, bf16[64,512]{1,0:T(8,128)(2,1)S(1)}, u32[]{:S(2)}, u32[]{:S(2)}) collective-permute-start(bf16[64,512]{1,0:T(8,128)(2,1)S(1)} %get-tuple-element.136), channel_id=1, source_target_pairs={{0,8},{2,10},{4,12},{6,14},{8,16},{10,18},{12,20},{14,22},{16,24},... | collective-permute-start | bytes 196616 | tf_op jit(solution)/shard_map/ppermute | solution.py:465
  438.6 4.7 collective-permute-start.49
  446.4 4.7 collective-permute-start.39
  453.1 5.3 collective-permute-start.63
  462.5 6.3 %collective-permute-done.39 = bf16[4,2,64,1024]{3,2,0,1:T(8,128)(2,1)S(1)} collective-permute-done((bf16[4,2,64,1024]{3,2,0,1:T(8,128)(2,1)S(1)}, bf16[4,2,64,1024]{3,2,0,1:T(8,128)(2,1)S(1)}, u32[]{:S(2)}, u32[]{:S(2)}) %collective-permute-start.39) | collective-permute-done | bytes 1048608 | tf_op jit(solution)/shard_map/ppermute | solution.py:465
  470.8 4.6 collective-permute-start.51
  475.5 5.1 collective-permute-start.64
  484.6 4.6 collective-permute-start.74
  494.0 5.0 collective-permute-start.65
  500.0 5.6 %collective-permute-start.75 = (bf16[64,2048]{1,0:T(8,128)(2,1)S(1)}, bf16[64,2048]{1,0:T(8,128)(2,1)S(1)}, u32[]{:S(2)}, u32[]{:S(2)}) collective-permute-start(bf16[64,2048]{1,0:T(8,128)(2,1)S(1)} %get-tuple-element.94), channel_id=1, source_target_pairs={{0,8},{2,10},{4,12},{6,14},{8,16},{10,18},{12,20},{14,22},{16,24},... | collective-permute-start | bytes 786440 | tf_op jit(solution)/shard_map/ppermute | solution.py:465
  505.6 4.6 collective-permute-start.53
  516.2 4.4 collective-permute-start.54
  524.0 4.4 collective-permute-start.44
  532.0 5.0 collective-permute-start.55
  538.6 5.2 collective-permute-start.45
  547.3 4.8 collective-permute-done.58
  (348 shorter events, 159.3 us)
Async XLA Ops:
  0.7 46.7 %collective-permute-start.2 = (bf16[3,1024,512]{2,1,0:T(8,128)(2,1)}, bf16[3,1024,512]{2,1,0:T(8,128)(2,1)}, u32[]{:S(2)}, u32[]{:S(2)}) collective-permute-start(bf16[3,1024,512]{2,1,0:T(8,128)(2,1)} %bitcast.328), channel_id=1, source_target_pairs={{0,1},{1,0},{2,3},{3,2},{4,5},{5,4},{6,7},{7,6},{8,9},{9,8},{10,11... | collective-permute-start | bytes 9437192 | tf_op jit(solution)/shard_map/ppermute | solution.py:438
  1.2 34.8 %collective-permute-start = (bf16[1024,1024]{1,0:T(8,128)(2,1)}, bf16[1024,1024]{1,0:T(8,128)(2,1)}, u32[]{:S(2)}, u32[]{:S(2)}) collective-permute-start(bf16[1024,1024]{1,0:T(8,128)(2,1)} %w_own.7), channel_id=1, source_target_pairs={{0,1},{1,0},{2,3},{3,2},{4,5},{5,4},{6,7},{7,6},{8,9},{9,8},{10,11... | collective-permute-start | bytes 6291464 | tf_op jit(solution)/shard_map/ppermute | solution.py:438
  4.1 65.7 %collective-permute-start.3 = (bf16[512,1024]{1,0:T(8,128)(2,1)}, bf16[512,1024]{1,0:T(8,128)(2,1)}, u32[]{:S(2)}, u32[]{:S(2)}) collective-permute-start(bf16[512,1024]{1,0:T(8,128)(2,1)} %w_own.6), channel_id=1, source_target_pairs={{0,1},{1,0},{2,3},{3,2},{4,5},{5,4},{6,7},{7,6},{8,9},{9,8},{10,11... | collective-permute-start | bytes 3145736 | tf_op jit(solution)/shard_map/ppermute | solution.py:438
  6.4 72.3 %collective-permute-start.5 = (bf16[2,448,512]{2,1,0:T(8,128)(2,1)}, bf16[2,448,512]{2,1,0:T(8,128)(2,1)}, u32[]{:S(2)}, u32[]{:S(2)}) collective-permute-start(bf16[2,448,512]{2,1,0:T(8,128)(2,1)} %bitcast.21.cot_own), channel_id=1, source_target_pairs={{0,1},{1,0},{2,3},{3,2},{4,5},{5,4},{6,7},{7,6},{8,9},{9,8},{10,11... | collective-permute-start | bytes 2752520 | tf_op jit(solution)/shard_map/ppermute | solution.py:438
  78.2 187.5 %collective-permute-start.14 = (bf16[448,1024]{1,0:T(8,128)(2,1)}, bf16[448,1024]{1,0:T(8,128)(2,1)}, u32[]{:S(2)}, u32[]{:S(2)}) collective-permute-start(bf16[448,1024]{1,0:T(8,128)(2,1)} %get-tuple-element.72), channel_id=1, source_target_pairs={{0,1},{1,0},{2,3},{3,2},{4,5},{5,4},{6,7},{7,6},{8,9},{9,8},{10,11... | collective-permute-start | bytes 2752520 | tf_op jit(solution)/shard_map/ppermute | solution.py:438
  116.8 19.7 %collective-permute-start.7 = (bf16[448,1024]{1,0:T(8,128)(2,1)}, bf16[448,1024]{1,0:T(8,128)(2,1)S(1)}, u32[]{:S(2)}, u32[]{:S(2)}) collective-permute-start(bf16[448,1024]{1,0:T(8,128)(2,1)} %get-tuple-element.54), channel_id=1, source_target_pairs={{0,1},{1,0},{2,3},{3,2},{4,5},{5,4},{6,7},{7,6},{8,9},{9,8},{10,11... | collective-permute-start | bytes 2752520 | tf_op jit(solution)/shard_map/ppermute | solution.py:438
  120.6 111.0 %collective-permute-start.6 = (bf16[2,448,512]{2,1,0:T(8,128)(2,1)}, bf16[2,448,512]{2,1,0:T(8,128)(2,1)}, u32[]{:S(2)}, u32[]{:S(2)}) collective-permute-start(bf16[2,448,512]{2,1,0:T(8,128)(2,1)} %fusion.23), channel_id=1, source_target_pairs={{0,1},{1,0},{2,3},{3,2},{4,5},{5,4},{6,7},{7,6},{8,9},{9,8},{10,11... | collective-permute-start | bytes 2752520 | tf_op jit(solution)/shard_map/ppermute | solution.py:438
  126.4 170.6 %collective-permute-start.60 = (bf16[4,2,64,2048]{3,2,0,1:T(8,128)(2,1)}, bf16[4,2,64,2048]{3,2,0,1:T(8,128)(2,1)}, u32[]{:S(2)}, u32[]{:S(2)}) collective-permute-start(bf16[4,2,64,2048]{3,2,0,1:T(8,128)(2,1)} %bitcast.303), channel_id=1, source_target_pairs={{2,0},{6,4},{10,8},{14,12},{18,16},{22,20},{26,24},{30,28},{3,1},{... | collective-permute-start | bytes 6291464 | tf_op jit(solution)/shard_map/ppermute | solution.py:465
  129.3 168.3 %collective-permute-start.59 = (bf16[4,2,64,2048]{3,2,0,1:T(8,128)(2,1)}, bf16[4,2,64,2048]{3,2,0,1:T(8,128)(2,1)}, u32[]{:S(2)}, u32[]{:S(2)}) collective-permute-start(bf16[4,2,64,2048]{3,2,0,1:T(8,128)(2,1)} %bitcast.304), channel_id=1, source_target_pairs={{0,2},{4,6},{8,10},{12,14},{16,18},{20,22},{24,26},{28,30},{1,3},{... | collective-permute-start | bytes 6291464 | tf_op jit(solution)/shard_map/ppermute | solution.py:465
  231.0 46.6 %collective-permute-start.13 = (bf16[448,1024]{1,0:T(8,128)(2,1)}, bf16[448,1024]{1,0:T(8,128)(2,1)}, u32[]{:S(2)}, u32[]{:S(2)}) collective-permute-start(bf16[448,1024]{1,0:T(8,128)(2,1)} %get-tuple-element.62.g_s0.l_own), channel_id=1, source_target_pairs={{0,1},{1,0},{2,3},{3,2},{4,5},{5,4},{6,7},{7,6},{8,9},{9,8},{10,11... | collective-permute-start | bytes 2752520 | tf_op jit(solution)/shard_map/ppermute | solution.py:438
  245.1 17.3 %collective-permute-start.12 = (f32[13968]{0:T(1024)S(1)}, f32[13968]{0:T(1024)}, u32[]{:S(2)}, u32[]{:S(2)}) collective-permute-start(f32[13968]{0:T(1024)S(1)} %add.405), channel_id=1, source_target_pairs={{0,16},{2,18},{4,20},{6,22},{8,24},{10,26},{12,28},{14,30},{16,0},... | collective-permute-start | bytes 167624 | tf_op jit(solution)/shard_map/ppermute | solution.py:501
  265.7 50.6 %collective-permute-start.70 = (bf16[4,2,64,2048]{3,2,0,1:T(8,128)(2,1)}, bf16[4,2,64,2048]{3,2,0,1:T(8,128)(2,1)}, u32[]{:S(2)}, u32[]{:S(2)}) collective-permute-start(bf16[4,2,64,2048]{3,2,0,1:T(8,128)(2,1)} %bitcast.301), channel_id=1, source_target_pairs={{4,0},{6,2},{12,8},{14,10},{20,16},{22,18},{28,24},{30,26},{5,1},{... | collective-permute-start | bytes 6291464 | tf_op jit(solution)/shard_map/ppermute | solution.py:465
  267.8 52.2 %collective-permute-start.69 = (bf16[4,2,64,2048]{3,2,0,1:T(8,128)(2,1)}, bf16[4,2,64,2048]{3,2,0,1:T(8,128)(2,1)}, u32[]{:S(2)}, u32[]{:S(2)}) collective-permute-start(bf16[4,2,64,2048]{3,2,0,1:T(8,128)(2,1)} %bitcast.302), channel_id=1, source_target_pairs={{0,4},{2,6},{8,12},{10,14},{16,20},{18,22},{24,28},{26,30},{1,5},{... | collective-permute-start | bytes 6291464 | tf_op jit(solution)/shard_map/ppermute | solution.py:465
  277.6 12.9 %collective-permute-start.35 = (bf16[448,1024]{1,0:T(8,128)(2,1)}, bf16[448,1024]{1,0:T(8,128)(2,1)S(1)}, u32[]{:S(2)}, u32[]{:S(2)}) collective-permute-start(bf16[448,1024]{1,0:T(8,128)(2,1)} %get-tuple-element.73.l_own), channel_id=1, source_target_pairs={{0,1},{1,0},{2,3},{3,2},{4,5},{5,4},{6,7},{7,6},{8,9},{9,8},{10,11... | collective-permute-start | bytes 2752520 | tf_op jit(solution)/shard_map/ppermute | solution.py:438
  290.5 35.5 %collective-permute-start.37 = (bf16[448,1024]{1,0:T(8,128)(2,1)}, bf16[448,1024]{1,0:T(8,128)(2,1)}, u32[]{:S(2)}, u32[]{:S(2)}) collective-permute-start(bf16[448,1024]{1,0:T(8,128)(2,1)} %get-tuple-element.47.first.l_own), channel_id=1, source_target_pairs={{0,1},{1,0},{2,3},{3,2},{4,5},{5,4},{6,7},{7,6},{8,9},{9,8},{10,11... | collective-permute-start | bytes 2752520 | tf_op jit(solution)/shard_map/ppermute | solution.py:438
  297.0 35.2 %collective-permute-start.38 = (bf16[448,1536]{1,0:T(8,128)(2,1)}, bf16[448,1536]{1,0:T(8,128)(2,1)}, u32[]{:S(2)}, u32[]{:S(2)}) collective-permute-start(bf16[448,1536]{1,0:T(8,128)(2,1)} %pad_maximum_fusion.2), channel_id=1, source_target_pairs={{0,1},{1,0},{2,3},{3,2},{4,5},{5,4},{6,7},{7,6},{8,9},{9,8},{10,11... | collective-permute-start | bytes 4128776 | tf_op jit(solution)/shard_map/ppermute | solution.py:438
  297.5 50.3 %collective-permute-start.26 = (bf16[4,2,64,512]{3,2,0,1:T(8,128)(2,1)}, bf16[4,2,64,512]{3,2,0,1:T(8,128)(2,1)}, u32[]{:S(2)}, u32[]{:S(2)}) collective-permute-start(bf16[4,2,64,512]{3,2,0,1:T(8,128)(2,1)} %bitcast.310), channel_id=1, source_target_pairs={{4,0},{6,2},{12,8},{14,10},{20,16},{22,18},{28,24},{30,26},{5,1},{... | collective-permute-start | bytes 1572872 | tf_op jit(solution)/shard_map/ppermute | solution.py:465
  316.4 37.2 %collective-permute-start.25 = (bf16[4,2,64,512]{3,2,0,1:T(8,128)(2,1)}, bf16[4,2,64,512]{3,2,0,1:T(8,128)(2,1)}, u32[]{:S(2)}, u32[]{:S(2)}) collective-permute-start(bf16[4,2,64,512]{3,2,0,1:T(8,128)(2,1)} %bitcast.311), channel_id=1, source_target_pairs={{0,4},{2,6},{8,12},{10,14},{16,20},{18,22},{24,28},{26,30},{1,5},{... | collective-permute-start | bytes 1572872 | tf_op jit(solution)/shard_map/ppermute | solution.py:465
  320.0 36.4 %collective-permute-start.16 = (bf16[4,2,64,512]{3,2,0,1:T(8,128)(2,1)}, bf16[4,2,64,512]{3,2,0,1:T(8,128)(2,1)}, u32[]{:S(2)}, u32[]{:S(2)}) collective-permute-start(bf16[4,2,64,512]{3,2,0,1:T(8,128)(2,1)} %bitcast.312), channel_id=1, source_target_pairs={{2,0},{6,4},{10,8},{14,12},{18,16},{22,20},{26,24},{30,28},{3,1},{... | collective-permute-start | bytes 1572872 | tf_op jit(solution)/shard_map/ppermute | solution.py:465
  326.0 31.6 %collective-permute-start.15 = (bf16[4,2,64,512]{3,2,0,1:T(8,128)(2,1)S(1)}, bf16[4,2,64,512]{3,2,0,1:T(8,128)(2,1)}, u32[]{:S(2)}, u32[]{:S(2)}) collective-permute-start(bf16[4,2,64,512]{3,2,0,1:T(8,128)(2,1)S(1)} %bitcast.336), channel_id=1, source_target_pairs={{0,2},{4,6},{8,10},{12,14},{16,18},{20,22},{24,26},{28,30},{1,3},{... | collective-permute-start | bytes 1572872 | tf_op jit(solution)/shard_map/ppermute | solution.py:465
  332.2 106.4 %collective-permute-start.62 = (bf16[4,64,2048]{2,1,0:T(8,128)(2,1)}, bf16[4,64,2048]{2,1,0:T(8,128)(2,1)}, u32[]{:S(2)}, u32[]{:S(2)}) collective-permute-start(bf16[4,64,2048]{2,1,0:T(8,128)(2,1)} %get-tuple-element.85), channel_id=1, source_target_pairs={{4,0},{6,2},{12,8},{14,10},{20,16},{22,18},{28,24},{30,26},{5,1},{... | collective-permute-start | bytes 3145736 | tf_op jit(solution)/shard_map/ppermute | solution.py:465
  347.8 95.5 %collective-permute-start.61 = (bf16[4,64,2048]{2,1,0:T(8,128)(2,1)S(1)}, bf16[4,64,2048]{2,1,0:T(8,128)(2,1)S(1)}, u32[]{:S(2)}, u32[]{:S(2)}) collective-permute-start(bf16[4,64,2048]{2,1,0:T(8,128)(2,1)S(1)} %get-tuple-element.84), channel_id=1, source_target_pairs={{0,4},{2,6},{8,12},{10,14},{16,20},{18,22},{24,28},{26,30},{1,5},{... | collective-permute-start | bytes 3145736 | tf_op jit(solution)/shard_map/ppermute | solution.py:465
  353.6 92.8 %collective-permute-start.72 = (bf16[4,64,2048]{2,1,0:T(8,128)(2,1)S(1)}, bf16[4,64,2048]{2,1,0:T(8,128)(2,1)S(1)}, u32[]{:S(2)}, u32[]{:S(2)}) collective-permute-start(bf16[4,64,2048]{2,1,0:T(8,128)(2,1)S(1)} %copy-done.11), channel_id=1, source_target_pairs={{2,0},{6,4},{10,8},{14,12},{18,16},{22,20},{26,24},{30,28},{3,1},{... | collective-permute-start | bytes 3145736 | tf_op jit(solution)/shard_map/ppermute | solution.py:465
  356.4 27.4 %collective-permute-start.28 = (bf16[4,64,512]{2,1,0:T(8,128)(2,1)S(1)}, bf16[4,64,512]{2,1,0:T(8,128)(2,1)S(1)}, u32[]{:S(2)}, u32[]{:S(2)}) collective-permute-start(bf16[4,64,512]{2,1,0:T(8,128)(2,1)S(1)} %get-tuple-element.131), channel_id=1, source_target_pairs={{2,0},{6,4},{10,8},{14,12},{18,16},{22,20},{26,24},{30,28},{3,1},{... | collective-permute-start | bytes 786440 | tf_op jit(solution)/shard_map/ppermute | solution.py:465
  357.7 27.4 %collective-permute-start.27 = (bf16[4,64,512]{2,1,0:T(8,128)(2,1)S(1)}, bf16[4,64,512]{2,1,0:T(8,128)(2,1)S(1)}, u32[]{:S(2)}, u32[]{:S(2)}) collective-permute-start(bf16[4,64,512]{2,1,0:T(8,128)(2,1)S(1)} %get-tuple-element.130), channel_id=1, source_target_pairs={{0,2},{4,6},{8,10},{12,14},{16,18},{20,22},{24,26},{28,30},{1,3},{... | collective-permute-start | bytes 786440 | tf_op jit(solution)/shard_map/ppermute | solution.py:465
  395.2 12.6 %collective-permute-start.32 = (bf16[64,512]{1,0:T(8,128)(2,1)S(1)}, bf16[64,512]{1,0:T(8,128)(2,1)S(1)}, u32[]{:S(2)}, u32[]{:S(2)}) collective-permute-start(bf16[64,512]{1,0:T(8,128)(2,1)S(1)} %get-tuple-element.143), channel_id=1, source_target_pairs={{24,16},{26,18},{28,20},{30,22},{25,17},{27,19},{29,21},{31,23}} | collective-permute-start | bytes 196616 | tf_op jit(solution)/shard_map/ppermute | solution.py:465
  432.0 21.0 %collective-permute-start.71 = (bf16[4,64,2048]{2,1,0:T(8,128)(2,1)S(1)}, bf16[4,64,2048]{2,1,0:T(8,128)(2,1)S(1)}, u32[]{:S(2)}, u32[]{:S(2)}) collective-permute-start(bf16[4,64,2048]{2,1,0:T(8,128)(2,1)S(1)} %get-tuple-element.82), channel_id=1, source_target_pairs={{0,2},{4,6},{8,10},{12,14},{16,18},{20,22},{24,26},{28,30},{1,3},{... | collective-permute-start | bytes 3145736 | tf_op jit(solution)/shard_map/ppermute | solution.py:465
  436.6 22.5 %collective-permute-start.50 = (bf16[4,2,64,1024]{3,2,0,1:T(8,128)(2,1)S(1)}, bf16[4,2,64,1024]{3,2,0,1:T(8,128)(2,1)S(1)}, u32[]{:S(2)}, u32[]{:S(2)}) collective-permute-start(bf16[4,2,64,1024]{3,2,0,1:T(8,128)(2,1)S(1)} %bitcast.335), channel_id=1, source_target_pairs={{4,0},{6,2},{12,8},{14,10},{20,16},{22,18},{28,24},{30,26},{5,1},{... | collective-permute-start | bytes 3145736 | tf_op jit(solution)/shard_map/ppermute | solution.py:465
  438.6 21.1 %collective-permute-start.49 = (bf16[4,2,64,1024]{3,2,0,1:T(8,128)(2,1)S(1)}, bf16[4,2,64,1024]{3,2,0,1:T(8,128)(2,1)S(1)}, u32[]{:S(2)}, u32[]{:S(2)}) collective-permute-start(bf16[4,2,64,1024]{3,2,0,1:T(8,128)(2,1)S(1)} %bitcast.334), channel_id=1, source_target_pairs={{0,4},{2,6},{8,12},{10,14},{16,20},{18,22},{24,28},{26,30},{1,5},{... | collective-permute-start | bytes 3145736 | tf_op jit(solution)/shard_map/ppermute | solution.py:465
  443.3 18.5 %collective-permute-start.40 = (bf16[4,2,64,1024]{3,2,0,1:T(8,128)(2,1)S(1)}, bf16[4,2,64,1024]{3,2,0,1:T(8,128)(2,1)S(1)}, u32[]{:S(2)}, u32[]{:S(2)}) collective-permute-start(bf16[4,2,64,1024]{3,2,0,1:T(8,128)(2,1)S(1)} %bitcast.333), channel_id=1, source_target_pairs={{2,0},{6,4},{10,8},{14,12},{18,16},{22,20},{26,24},{30,28},{3,1},{... | collective-permute-start | bytes 3145736 | tf_op jit(solution)/shard_map/ppermute | solution.py:465
  446.4 22.4 %collective-permute-start.39 = (bf16[4,2,64,1024]{3,2,0,1:T(8,128)(2,1)S(1)}, bf16[4,2,64,1024]{3,2,0,1:T(8,128)(2,1)S(1)}, u32[]{:S(2)}, u32[]{:S(2)}) collective-permute-start(bf16[4,2,64,1024]{3,2,0,1:T(8,128)(2,1)S(1)} %bitcast.332), channel_id=1, source_target_pairs={{0,2},{4,6},{8,10},{12,14},{16,18},{20,22},{24,26},{28,30},{1,3},{... | collective-permute-start | bytes 3145736 | tf_op jit(solution)/shard_map/ppermute | solution.py:465
  453.1 17.8 %collective-permute-start.63 = (bf16[64,2048]{1,0:T(8,128)(2,1)S(1)}, bf16[64,2048]{1,0:T(8,128)(2,1)S(1)}, u32[]{:S(2)}, u32[]{:S(2)}) collective-permute-start(bf16[64,2048]{1,0:T(8,128)(2,1)S(1)} %get-tuple-element.100), channel_id=1, source_target_pairs={{0,8},{2,10},{4,12},{6,14},{1,9},{3,11},{5,13},{7,15}} | collective-permute-start | bytes 786440 | tf_op jit(solution)/shard_map/ppermute | solution.py:465
  459.0 21.8 %collective-permute-start.66 = (bf16[64,2048]{1,0:T(8,128)(2,1)S(1)}, bf16[64,2048]{1,0:T(8,128)(2,1)S(1)}, u32[]{:S(2)}, u32[]{:S(2)}) collective-permute-start(bf16[64,2048]{1,0:T(8,128)(2,1)S(1)} %get-tuple-element.101), channel_id=1, source_target_pairs={{24,16},{26,18},{28,20},{30,22},{25,17},{27,19},{29,21},{31,23}} | collective-permute-start | bytes 786440 | tf_op jit(solution)/shard_map/ppermute | solution.py:465
  459.7 15.8 %collective-permute-start.73 = (bf16[64,2048]{1,0:T(8,128)(2,1)S(1)}, bf16[64,2048]{1,0:T(8,128)(2,1)S(1)}, u32[]{:S(2)}, u32[]{:S(2)}) collective-permute-start(bf16[64,2048]{1,0:T(8,128)(2,1)S(1)} %get-tuple-element.96), channel_id=1, source_target_pairs={{0,8},{2,10},{4,12},{6,14},{1,9},{3,11},{5,13},{7,15}} | collective-permute-start | bytes 786440 | tf_op jit(solution)/shard_map/ppermute | solution.py:465
  461.8 27.6 %collective-permute-start.76 = (bf16[64,2048]{1,0:T(8,128)(2,1)S(1)}, bf16[64,2048]{1,0:T(8,128)(2,1)S(1)}, u32[]{:S(2)}, u32[]{:S(2)}) collective-permute-start(bf16[64,2048]{1,0:T(8,128)(2,1)S(1)} %get-tuple-element.97), channel_id=1, source_target_pairs={{24,16},{26,18},{28,20},{30,22},{25,17},{27,19},{29,21},{31,23}} | collective-permute-start | bytes 786440 | tf_op jit(solution)/shard_map/ppermute | solution.py:465
  468.8 25.1 %collective-permute-start.52 = (bf16[4,64,1024]{2,1,0:T(8,128)(2,1)S(1)}, bf16[4,64,1024]{2,1,0:T(8,128)(2,1)S(1)}, u32[]{:S(2)}, u32[]{:S(2)}) collective-permute-start(bf16[4,64,1024]{2,1,0:T(8,128)(2,1)S(1)} %get-tuple-element.105), channel_id=1, source_target_pairs={{2,0},{6,4},{10,8},{14,12},{18,16},{22,20},{26,24},{30,28},{3,1},{... | collective-permute-start | bytes 1572872 | tf_op jit(solution)/shard_map/ppermute | solution.py:465
  470.8 28.1 %collective-permute-start.51 = (bf16[4,64,1024]{2,1,0:T(8,128)(2,1)S(1)}, bf16[4,64,1024]{2,1,0:T(8,128)(2,1)S(1)}, u32[]{:S(2)}, u32[]{:S(2)}) collective-permute-start(bf16[4,64,1024]{2,1,0:T(8,128)(2,1)S(1)} %get-tuple-element.104), channel_id=1, source_target_pairs={{0,2},{4,6},{8,10},{12,14},{16,18},{20,22},{24,26},{28,30},{1,3},{... | collective-permute-start | bytes 1572872 | tf_op jit(solution)/shard_map/ppermute | solution.py:465
  480.8 19.2 %collective-permute-start.42 = (bf16[4,64,1024]{2,1,0:T(8,128)(2,1)S(1)}, bf16[4,64,1024]{2,1,0:T(8,128)(2,1)S(1)}, u32[]{:S(2)}, u32[]{:S(2)}) collective-permute-start(bf16[4,64,1024]{2,1,0:T(8,128)(2,1)S(1)} %get-tuple-element.103), channel_id=1, source_target_pairs={{4,0},{6,2},{12,8},{14,10},{20,16},{22,18},{28,24},{30,26},{5,1},{... | collective-permute-start | bytes 1572872 | tf_op jit(solution)/shard_map/ppermute | solution.py:465
  489.4 16.2 %collective-permute-start.41 = (bf16[4,64,1024]{2,1,0:T(8,128)(2,1)S(1)}, bf16[4,64,1024]{2,1,0:T(8,128)(2,1)S(1)}, u32[]{:S(2)}, u32[]{:S(2)}) collective-permute-start(bf16[4,64,1024]{2,1,0:T(8,128)(2,1)S(1)} %get-tuple-element.102), channel_id=1, source_target_pairs={{0,4},{2,6},{8,12},{10,14},{16,20},{18,22},{24,28},{26,30},{1,5},{... | collective-permute-start | bytes 1572872 | tf_op jit(solution)/shard_map/ppermute | solution.py:465
  493.1 17.4 %collective-permute-start.67 = (bf16[64,2048]{1,0:T(8,128)(2,1)S(1)}, bf16[64,2048]{1,0:T(8,128)(2,1)S(1)}, u32[]{:S(2)}, u32[]{:S(2)}) collective-permute-start(bf16[64,2048]{1,0:T(8,128)(2,1)S(1)} %get-tuple-element.99), channel_id=1, source_target_pairs={{16,8},{18,10},{20,12},{22,14},{24,16},{26,18},{28,20},{30,22},{17... | collective-permute-start | bytes 786440 | tf_op jit(solution)/shard_map/ppermute | solution.py:465
  494.0 38.0 %collective-permute-start.65 = (bf16[64,2048]{1,0:T(8,128)(2,1)S(1)}, bf16[64,2048]{1,0:T(8,128)(2,1)S(1)}, u32[]{:S(2)}, u32[]{:S(2)}) collective-permute-start(bf16[64,2048]{1,0:T(8,128)(2,1)S(1)} %get-tuple-element.98), channel_id=1, source_target_pairs={{0,8},{2,10},{4,12},{6,14},{8,16},{10,18},{12,20},{14,22},{16,24},... | collective-permute-start | bytes 786440 | tf_op jit(solution)/shard_map/ppermute | solution.py:465
  500.0 38.6 %collective-permute-start.75 = (bf16[64,2048]{1,0:T(8,128)(2,1)S(1)}, bf16[64,2048]{1,0:T(8,128)(2,1)S(1)}, u32[]{:S(2)}, u32[]{:S(2)}) collective-permute-start(bf16[64,2048]{1,0:T(8,128)(2,1)S(1)} %get-tuple-element.94), channel_id=1, source_target_pairs={{0,8},{2,10},{4,12},{6,14},{8,16},{10,18},{12,20},{14,22},{16,24},... | collective-permute-start | bytes 786440 | tf_op jit(solution)/shard_map/ppermute | solution.py:465
  512.7 15.8 %collective-permute-start.46 = (bf16[64,1024]{1,0:T(8,128)(2,1)S(1)}, bf16[64,1024]{1,0:T(8,128)(2,1)S(1)}, u32[]{:S(2)}, u32[]{:S(2)}) collective-permute-start(bf16[64,1024]{1,0:T(8,128)(2,1)S(1)} %get-tuple-element.123), channel_id=1, source_target_pairs={{24,16},{26,18},{28,20},{30,22},{25,17},{27,19},{29,21},{31,23}} | collective-permute-start | bytes 393224 | tf_op jit(solution)/shard_map/ppermute | solution.py:465
  520.7 16.3 %collective-permute-start.68 = (bf16[64,2048]{1,0:T(8,128)(2,1)S(1)}, bf16[64,2048]{1,0:T(8,128)(2,1)S(1)}, u32[]{:S(2)}, u32[]{:S(2)}) collective-permute-start(bf16[64,2048]{1,0:T(8,128)(2,1)S(1)} %fusion.31), channel_id=1, source_target_pairs={{8,0},{10,2},{12,4},{14,6},{16,8},{18,10},{20,12},{22,14},{24,16},... | collective-permute-start | bytes 786440 | tf_op jit(solution)/shard_map/ppermute | solution.py:465
  528.5 15.3 %collective-permute-start.78 = (bf16[64,2048]{1,0:T(8,128)(2,1)S(1)}, bf16[64,2048]{1,0:T(8,128)(2,1)S(1)}, u32[]{:S(2)}, u32[]{:S(2)}) collective-permute-start(bf16[64,2048]{1,0:T(8,128)(2,1)S(1)} %fusion.25), channel_id=1, source_target_pairs={{8,0},{10,2},{12,4},{14,6},{16,8},{18,10},{20,12},{22,14},{24,16},... | collective-permute-start | bytes 786440 | tf_op jit(solution)/shard_map/ppermute | solution.py:465
  531.2 13.4 %collective-permute-start.57 = (bf16[64,1024]{1,0:T(8,128)(2,1)S(1)}, bf16[64,1024]{1,0:T(8,128)(2,1)S(1)}, u32[]{:S(2)}, u32[]{:S(2)}) collective-permute-start(bf16[64,1024]{1,0:T(8,128)(2,1)S(1)} %get-tuple-element.125), channel_id=1, source_target_pairs={{16,8},{18,10},{20,12},{22,14},{24,16},{26,18},{28,20},{30,22},{17... | collective-permute-start | bytes 393224 | tf_op jit(solution)/shard_map/ppermute | solution.py:465
  532.0 15.4 %collective-permute-start.55 = (bf16[64,1024]{1,0:T(8,128)(2,1)S(1)}, bf16[64,1024]{1,0:T(8,128)(2,1)S(1)}, u32[]{:S(2)}, u32[]{:S(2)}) collective-permute-start(bf16[64,1024]{1,0:T(8,128)(2,1)S(1)} %get-tuple-element.124), channel_id=1, source_target_pairs={{0,8},{2,10},{4,12},{6,14},{8,16},{10,18},{12,20},{14,22},{16,24},... | collective-permute-start | bytes 393224 | tf_op jit(solution)/shard_map/ppermute | solution.py:465
  538.6 13.7 %collective-permute-start.45 = (bf16[64,1024]{1,0:T(8,128)(2,1)S(1)}, bf16[64,1024]{1,0:T(8,128)(2,1)S(1)}, u32[]{:S(2)}, u32[]{:S(2)}) collective-permute-start(bf16[64,1024]{1,0:T(8,128)(2,1)S(1)} %get-tuple-element.120), channel_id=1, source_target_pairs={{0,8},{2,10},{4,12},{6,14},{8,16},{10,18},{12,20},{14,22},{16,24},... | collective-permute-start | bytes 393224 | tf_op jit(solution)/shard_map/ppermute | solution.py:465
  (68 other events, 536.0 us)

commit v2 on v1

--- a/solution.py
+++ b/solution.py
@@ -11,7 +11,8 @@
 VMEM = pl.BlockSpec(memory_space=pltpu.VMEM)
 SMEM = pl.BlockSpec(memory_space=pltpu.SMEM)
 PAD = 112
-LIMIT = 56 * 1024 * 1024
+LIMIT = 60 * 1024 * 1024
+MESH = pl.DeviceIdType.MESH
 
 
 def call(body, out, ins, scratch=(), flops=0, nbytes=0, **more):
@@ -442,65 +443,208 @@
     return lax.dynamic_index_in_dim(value, index, 0, keepdims=False)
 
 
-class Grid:
-    def __init__(self, count):
-        side = 1
-        while 4 * (side + 1) * (side + 1) <= count:
-            side += 1
-        self.sizes = {"z": count // (side * side), "y": side, "x": side}
-        self.strides = {"z": side * side, "y": side, "x": 1}
-        self.count = count
-
-    def place(self, axis):
-        me = lax.axis_index("win")
-        return (me // self.strides[axis]) % self.sizes[axis]
-
-    def shift(self, value, axis, delta, senders):
-        stride, size = self.strides[axis], self.sizes[axis]
-        pairs = []
-        for w in range(self.count):
-            c = (w // stride) % size
-            if c in senders:
-                pairs.append((w, w + delta * stride))
-        return lax.ppermute(value, "win", pairs)
-
-    def chain(self, value, axis):
-        size = self.sizes[axis]
-        c = self.place(axis)
-        right = left = None
-        for s in range(1, size):
-            go_right = take(value, jnp.clip(size - s + c, 0, size - 1))
-            go_left = take(value, jnp.clip(c - 1 - (size - 1 - s), 0, size - 1))
-            if s > 1:
-                go_right = (go_right.astype(F32) + right.astype(F32)).astype(BF16)
-                go_left = (go_left.astype(F32) + left.astype(F32)).astype(BF16)
-            right = self.shift(go_right, axis, 1, range(0, min(s, size - 1)))
-            left = self.shift(go_left, axis, -1, range(max(size - s, 1), size))
-        return take(value, c).astype(F32) + right.astype(F32) + left.astype(F32)
-
-    def scatter(self, value, order):
-        sizes = self.sizes
-        v = value.reshape(sizes["z"], sizes["y"], sizes["x"], -1, value.shape[1])
-        left = ["z", "y", "x"]
-        for step, axis in enumerate(order):
-            v = self.chain(jnp.moveaxis(v, left.index(axis), 0), axis)
-            left.remove(axis)
-            if step < 2:
-                v = v.astype(BF16)
-        return v
-
-    def total(self, value):
-        for axis in ("x", "y", "z"):
-            size, stride = self.sizes[axis], self.strides[axis]
-            hop = 1
-            while hop < size:
-                pairs = []
-                for w in range(self.count):
-                    c = (w // stride) % size
-                    pairs.append((w, w + ((c ^ hop) - c) * stride))
-                value = value + lax.ppermute(value, "win", pairs)
-                hop *= 2
-        return value
+def win_sizes(count):
+    side = 1
+    while 4 * (side + 1) * (side + 1) <= count:
+        side += 1
+    return count // (side * side), side, side
+
+
+def my_place(sizes):
+    me = lax.axis_index("win")
+    _, ny, nx = sizes
+    return lax.div(me, ny * nx), lax.rem(lax.div(me, nx), ny), lax.rem(me, nx)
+
+
+def wins_along(sizes, place, axis):
+    z, y, x = place
+    strides = (sizes[1] * sizes[2], sizes[2], 1)
+    base = z * strides[0] + y * strides[1] + x
+    found = []
+    for d in range(1, sizes[axis]):
+        c = lax.rem(place[axis] + d, sizes[axis])
+        found.append((d, c, base + (c - place[axis]) * strides[axis]))
+    return found
+
+
+def enter(sizes, place):
+    barrier = pltpu.get_barrier_semaphore()
+    tp = lax.axis_index("tp")
+    peers = [(lax.axis_index("win"), 1 - tp)]
+    for axis in range(3):
+        peers += [(w, tp) for _, _, w in wins_along(sizes, place, axis)]
+    for peer in peers:
+        pl.semaphore_signal(barrier, inc=1, device_id=peer, device_id_type=MESH)
+    pl.semaphore_wait(barrier, len(peers))
+
+
+class Scatter:
+    def __init__(self, sizes, place, order, src, bufs, sends, recvs, unit):
+        self.sizes, self.place, self.order = sizes, place, order
+        self.src, self.bufs, self.sends, self.recvs, self.unit = src, bufs, sends, recvs, unit
+
+    def pick(self, step, c):
+        if step == 0:
+            return self.src.at[:, :, c] if self.order[0] == 2 else self.src.at[:, c]
+        before = self.bufs[step - 1].at[0]
+        if step == 1:
+            return before.at[:, c]
+        return before.at[c]
+
+    def copies(self, step):
+        axis = self.order[step]
+        tp = lax.axis_index("tp")
+        made = []
+        for d, c, w in wins_along(self.sizes, self.place, axis):
+            made.append(
+                pltpu.make_async_remote_copy(
+                    src_ref=self.pick(step, c),
+                    dst_ref=self.bufs[step].at[d - 1],
+                    send_sem=self.sends.at[self.unit, step, d - 1],
+                    recv_sem=self.recvs.at[self.unit, step, d - 1],
+                    device_id=(w, tp),
+                    device_id_type=MESH,
+                )
+            )
+        return made
+
+    def start(self, step):
+        for copy in self.copies(step):
+            copy.start()
+
+    def wait_sent(self, step):
+        for copy in self.copies(step):
+            copy.wait_send()
+
+    def finish(self, step, out=None):
+        copies = self.copies(step)
+        for copy in copies:
+            copy.wait_recv()
+        mine = self.pick(step, self.place[self.order[step]])
+        buf = self.bufs[step]
+        lead = mine.shape[:-2]
+        rows, n = mine.shape[-2:]
+        width = min(n, 512)
+        if step == 2:
+            for b in range(n // width):
+                at = pl.ds(b * width, width)
+                total = mine[:, at].astype(F32)
+                for d in range(len(copies)):
+                    total += buf[d, :, at].astype(F32)
+                out[:, at] = total
+            return
+        count = 1
+        for size in lead:
+            count *= size
+
+        @pl.loop(0, count)
+        def _(i):
+            where = (i,) if len(lead) == 1 else (lax.div(i, lead[1]), lax.rem(i, lead[1]))
+            for b in range(n // width):
+                at = pl.ds(b * width, width)
+                total = mine[(*where, slice(None), at)].astype(F32)
+                for d in range(len(copies)):
+                    total += buf[(d, *where, slice(None), at)].astype(F32)
+                buf[(0, *where, slice(None), at)] = total.astype(BF16)
+
+
+def scatter_buffers(sizes, order, rows, n):
+    left = [0, 1, 2]
+    shapes = []
+    for axis in order:
+        left.remove(axis)
+        shapes.append(
+            pltpu.VMEM((sizes[axis] - 1, *[sizes[a] for a in left], rows, n), BF16)
+        )
+    return shapes
+
+
+X_FIRST, Y_FIRST = (2, 1, 0), (1, 2, 0)
+
+
+def all_sum(sizes, place, src, bufs, sends, recvs):
+    tp = lax.axis_index("tp")
+    for step, axis in enumerate((2, 1, 0)):
+        copies = []
+        for d, c, w in wins_along(sizes, place, axis):
+            copies.append(
+                pltpu.make_async_remote_copy(
+                    src_ref=src.at[step],
+                    dst_ref=bufs.at[step, d - 1],
+                    send_sem=sends.at[step, d - 1],
+                    recv_sem=recvs.at[step, d - 1],
+                    device_id=(w, tp),
+                    device_id_type=MESH,
+                )
+            )
+        for copy in copies:
+            copy.start()
+        total = src[step]
+        for d, copy in enumerate(copies):
+            copy.wait()
+            total += bufs[step, d]
+        src[step + 1] = total
+
+
+def sums_body(sizes, orders, n_units, *refs):
+    srcs, vec = refs[:n_units], refs[n_units]
+    outs, vec_out = refs[n_units + 1 : 2 * n_units + 1], refs[2 * n_units + 1]
+    scratch = refs[2 * n_units + 2 :]
+    bufs = [scratch[3 * u : 3 * u + 3] for u in range(n_units)]
+    sends, recvs, vsrc, vbuf, vsends, vrecvs = scratch[3 * n_units :]
+    place = my_place(sizes)
+    enter(sizes, place)
+    units = [
+        Scatter(sizes, place, orders[u], srcs[u], bufs[u], sends, recvs, u)
+        for u in range(n_units)
+    ]
+    for unit in units:
+        unit.start(0)
+    for unit in units:
+        unit.finish(0)
+        unit.start(1)
+    vsrc[0] = vec[...]
+    all_sum(sizes, place, vsrc, vbuf, vsends, vrecvs)
+    vec_out[...] = vsrc[3]
+    for unit in units:
+        unit.finish(1)
+        unit.start(2)
+    for unit, out in zip(units, outs):
+        unit.finish(2, out)
+    for unit in units:
+        for step in range(3):
+            unit.wait_sent(step)
+
+
+def sums_over_win(count, units, vec):
+    sizes = win_sizes(count)
+    rows = units[0][0].shape[0] // count
+    most = max(sizes) - 1
+    scratch = []
+    for value, order in units:
+        scratch += scatter_buffers(sizes, order, rows, value.shape[1])
+    dma = pltpu.SemaphoreType.DMA
+    scratch += [
+        dma((len(units), 3, most)), dma((len(units), 3, most)),
+        pltpu.VMEM((4, *vec.shape), F32), pltpu.VMEM((3, most, *vec.shape), F32),
+        dma((3, most)), dma((3, most)),
+    ]
+
+    def body(*refs):
+        sums_body(sizes, [order for _, order in units], len(units), *refs)
+
+    ins = [value.reshape(*sizes, rows, value.shape[1]) for value, _ in units] + [vec]
+    outs = [shape((rows, value.shape[1])) for value, _ in units] + [shape(vec.shape)]
+    return pl.pallas_call(
+        body,
+        out_shape=outs,
+        in_specs=[VMEM] * len(ins),
+        out_specs=[VMEM] * len(outs),
+        scratch_shapes=scratch,
+        compiler_params=pltpu.CompilerParams(
+            vmem_limit_bytes=LIMIT, collective_id=1, has_side_effects=True
+        ),
+    )(*ins)
 
 
 def solution(mesh):
@@ -511,7 +655,6 @@
         qkv_bias, rel_table, proj_weight, proj_bias, norm2_gain, norm2_shift, fc1_weight,
         fc1_bias, fc2_weight, fc2_bias, rel_index, keep, cotangent,
     ):
-        grid = Grid(count)
         t = lax.axis_index("tp")
         t_arr = t.reshape(1).astype(jnp.int32)
         wins, height, _, channels = pixels.shape
@@ -646,8 +789,6 @@
         feed_recv = swap(feed[1].astype(BF16))
         out = keep_rows * (feed[0] + feed_recv.astype(F32) + fc2_bias)
         out = out.reshape(2 * wins, PAD, half)[:, :area].reshape(2 * wins * area, half).astype(BF16)
-        fc1_grad = grid.scatter(wg1, ("x", "y", "z"))
-        fc2_grad = grid.scatter(wg2, ("y", "x", "z")).T
 
         d_s1, g_att, g_attended, vec2 = whole(
             norm2_back_body,
@@ -703,16 +844,6 @@
             .transpose(1, 2, 4, 3, 0, 5)
             .reshape(pixels.shape)
         )
-        a_part = jnp.concatenate([proj_part, qkv_part[:, :half]], 1)
-        b_part = qkv_part[:, half:]
-        a_sum = grid.scatter(a_part, ("x", "y", "z"))
-        b_sum = grid.scatter(b_part, ("y", "x", "z"))
-        ma_sum = grid.scatter(merge_part[:, :half], ("x", "y", "z"))
-        mb_sum = grid.scatter(merge_part[:, half:], ("y", "x", "z"))
-        proj_grad = a_sum[:, :half].T
-        qkv_grad = jnp.stack([a_sum[:, half:], b_sum[:, :half], b_sum[:, half:]], 1)
-        merge_grad = jnp.concatenate([ma_sum, mb_sum], 1).T
-
         def sides(v):
             both = jnp.stack([v[..., :half], v[..., half:]])
             return take(both, t), take(both, 1 - t)
@@ -727,7 +858,16 @@
         ]
         back = swap(jnp.concatenate([v.reshape(-1) for v in leavers]))
         mine = jnp.concatenate([v.reshape(-1) for v in keepers]) + back
-        vectors = grid.total(jnp.concatenate([mine, gb1.reshape(-1), gb2.reshape(-1)]))
+        vector = jnp.concatenate([mine, gb1.reshape(-1), gb2.reshape(-1)])
+        vector = jnp.pad(vector, (0, -vector.size % 1024)).reshape(-1, 128)
+        units = [(wg1, X_FIRST), (wg2, Y_FIRST), (qkv_part, X_FIRST), (proj_part, Y_FIRST),
+                 (merge_part, Y_FIRST)]
+        fc1_grad, fc2_grad, qkv_grad, proj_grad, merge_grad, vectors = sums_over_win(
+            count, units, vector
+        )
+        vectors = vectors.reshape(-1)
+        fc2_grad, proj_grad, merge_grad = fc2_grad.T, proj_grad.T, merge_grad.T
+        qkv_grad = qkv_grad.reshape(-1, 3, half)
         parts, at = [], 0
         for v in keepers + [gb1, gb2]:
             parts.append(vectors[at : at + v.size].reshape(v.shape))

time: 564 us -> 486 us (0.86); the launches traced: 556 us -> 485 us
  Pallas kernels: 200 us -> 420 us
  starting transfers between devices: 180 us -> 3.97 us
  waiting for transfers between devices: 76 us -> 1.57 us
  other arithmetic: 28.6 us -> 8.22 us
  local copies, waits for them, and re-layouts: 68.5 us -> 50.5 us
    pallas_call x0 -> x1, Pallas kernels: none -> 220 us  [sums_over_win(): pl.pallas_call(body, out_shape=outs, in_specs=[VMEM] * len(ins), out_spec...]
    ppermute x64 -> x0, starting transfers between devices: 175 us -> none  [the longest x60 167 us: shift(): return lax.ppermute(value, 'win', pairs)]
    ppermute x64 -> x0, waiting for transfers between devices: 75 us -> none  [the longest x60 70.6 us: shift(): return lax.ppermute(value, 'win', pairs)]
    another operation x19 -> x0, local copies, waits for them, and re-layouts: 19.4 us -> none
    convert_element_type x30 -> x0, other arithmetic: 15.1 us -> none  [the longest x12 14.1 us: scatter(): v = v.astype(BF16)]
  transfers between devices with their start and end apart: 79 -> 15, of which waited for: 25 -> 1; matrix products, arithmetic and copies ran while one was open for 16% -> 8% of each run, Pallas kernels for 36% -> 32%
where the time goes in v2:
time: 486 us; the launch traced here: 485 us
  Pallas kernels  420 us (86%)
  local copies, waits for them, and re-layouts  50.5 us (10%)
  other arithmetic  8.22 us (2%)
    pallas_call x1, Pallas kernels, sums_over_win(): pl.pallas_call(body, out_shape=outs, in_specs=[VMEM] * len(ins), out_spec...  220 us
    pallas_call x14, Pallas kernels, call(): pl.pallas_call(body, out_shape=out, scratch_shapes=list(scratch), compile...  200 us
  transfers between devices with their start and end apart: 15, of which 1 were waited for; matrix products, arithmetic and copies ran while one was open for 8% of the time, Pallas kernels for 32%

profile of v2, /device:TPU:0, one launch (start us, length us, event | category | flops | bytes accessed | tf_op | source)
XLA Modules:
  0.0 485.2 jit_solution(14234199694552112633)
XLA Ops:
  1.2 0.8 reshape.587
  2.7 0.9 concatenate.196
  4.2 1.3 reshape.591
  5.4 1.0 pad.28
  6.9 3.1 copy.59
  10.0 1.0 reshape.584
  11.1 1.5 pad.25
  16.2 17.4 %shard_map.333.refs_3_.refs_4_ = f32[3584,112]{1,0:T(8,128)} custom-call(s32[100,112]{1,0:T(8,128)} %pad.26.index, bf16[64,384]{1,0:T(8,128)(2,1)} %pad_maximum_fusion.2.table), custom_call_target="tpu_custom_call" | custom-call | flops 629145600 | bytes 2000000 | tf_op jit(solution)/shard_map/pallas_call | solution.py:19
  36.0 11.2 %shard_map.331 = (f32[448,1024]{1,0:T(8,128)}, bf16[448,1024]{1,0:T(8,128)(2,1)}, bf16[448,1024]{1,0:T(8,128)(2,1)}, bf16[448,1024]{1,0:T(8,128)(2,1)}) custom-call(s32[1]{0:T(128)} %bitcast.t_ref, bf16[2,448,1024]{2,1,0:T(8,128)(2,1)} %bitcast.100, bf16[1024,1024]{1,0:T(8,128)(2,1)} %w_own.7, bf16[1024,1024]{1,0:T(8,128)(2,1)} %collective-permute-done.w_oth, ...), custom_call_target="tpu_custom_call" | custom-call | flops 1879048192 | bytes 10000000 | tf_op jit(solution)/shard_map/pallas_call | solution.py:19
  47.2 9.6 %shard_map.332.refs_0_.refs_1_.refs_2_ = bf16[3,448,1024]{2,1,0:T(8,128)(2,1)} custom-call(bf16[448,1024]{1,0:T(8,128)(2,1)} %get-tuple-element.53.first.l_own, bf16[3,1024,512]{2,1,0:T(8,128)(2,1)} %bitcast.109, bf16[3,1024,512]{2,1,0:T(8,128)(2,1)} %collective-permute-done.2.w_oth, f32[3,1,1024]{2,1,0:T(1,128)} %reshape.589.bias), custom_call_target="tpu_custom_call" | custom-call | flops 2818572288 | bytes 10000000 | tf_op jit(solution)/shard_map/pallas_call | solution.py:19
  56.8 12.8 %shard_map.334 = (bf16[448,1024]{1,0:T(8,128)(2,1)}, f32[8,16,112]{2,1,0:T(8,128)}) custom-call(bf16[3,448,1024]{2,1,0:T(8,128)(2,1)} %shard_map.332.refs_0_.refs_1_.refs_2_, bf16[3,448,1024]{2,1,0:T(8,128)(2,1)} %shard_map.332.refs_0_.refs_1_.refs_2_, bf16[3,448,1024]{2,1,0:T(8,128)(2,1)} %shard_map.332.refs_0_.refs_1_.refs_2_, ...), custom_call_target="tpu_custom_call" | custom-call | flops 822083584 | bytes 6000000 | tf_op jit(solution)/shard_map/pallas_call | solution.py:19
  69.7 7.2 %shard_map.335 = (f32[448,1024]{1,0:T(8,128)}, bf16[448,1024]{1,0:T(8,128)(2,1)}) custom-call(bf16[448,1024]{1,0:T(8,128)(2,1)} %get-tuple-element.54.att, bf16[512,1024]{1,0:T(8,128)(2,1)} %w_own.6, bf16[512,1024]{1,0:T(8,128)(2,1)} %collective-permute-done.3.w_oth, f32[1,1024]{1,0:T(1,128)} %get-tuple-element.166.pb, ...), custom_call_target="tpu_custom_call" | custom-call | flops 939524096 | bytes 8000000 | tf_op jit(solution)/shard_map/pallas_call | solution.py:19
  77.0 1.0 reshape.621.keep
  78.0 1.5 collective-permute-done.4.sec_sib
  79.5 0.9 copy-done.29
  80.5 36.2 %shard_map.336 = (bf16[1024,2048]{1,0:T(8,128)(2,1)}, bf16[1024,2048]{1,0:T(8,128)(2,1)}, f32[1,2048]{1,0:T(1,128)}, f32[1,512]{1,0:T(1,128)}, f32[2,2,448,512]{...) custom-call(s32[1]{0:T(128)} %bitcast.t_ref, ...), custom_call_target="tpu_custom_call" | custom-call | flops 22548578304 | bytes 30000000 | tf_op jit(solution)/shard_map/pallas_call | solution.py:19
  117.3 1.0 fusion.11
  118.4 2.6 fusion.3
  121.3 0.9 copy-done.4
  122.2 9.7 %shard_map.337 = (f32[448,1024]{1,0:T(8,128)}, bf16[448,1024]{1,0:T(8,128)(2,1)}, bf16[448,1024]{1,0:T(8,128)(2,1)}, f32[3,1024]{1,0:T(4,128)}) custom-call(f32[448,1024]{1,0:T(8,128)} %get-tuple-element.59.g_own, bf16[448,1024]{1,0:T(8,128)(2,1)} %copy-done.4, f32[448,1024]{1,0:T(8,128)} %get-tuple-element.57.s1.stream1, ...), custom_call_target="tpu_custom_call" | custom-call | flops 939524096 | bytes 10000000 | tf_op jit(solution)/shard_map/pallas_call | solution.py:19
  131.9 1.3 slice_bitcast_fusion.1
  133.2 25.7 %shard_map.338 = (bf16[448,1024]{1,0:T(8,128)(2,1)}, bf16[448,1024]{1,0:T(8,128)(2,1)}, bf16[448,1024]{1,0:T(8,128)(2,1)}, f32[3584,112]{1,0:T(8,128)}, f32[2,1024]{1,0:T(2,128)}) custom-call(bf16[3,448,1024]{2,1,0:T(8,128)(2,1)} %shard_map.332.refs_0_.refs_1_.refs_2_, bf16[3,448,1024]{2,1,0:T(8,128)(2,1)} %shard_map.332.refs_0_.refs_1_.refs_2_, ...), custom_call_target="tpu_custom_call" | custom-call | flops 2055208960 | bytes 10000000 | tf_op jit(solution)/shard_map/pallas_call | solution.py:19
  158.9 1.4 fusion.12
  160.7 12.6 %shard_map.339 = (bf16[448,1024]{1,0:T(8,128)(2,1)}, bf16[448,1024]{1,0:T(8,128)(2,1)}, f32[2,1024]{1,0:T(2,128)}) custom-call(bf16[448,1024]{1,0:T(8,128)(2,1)} %get-tuple-element.64.dq, bf16[448,1024]{1,0:T(8,128)(2,1)} %get-tuple-element.65.dk, bf16[448,1024]{1,0:T(8,128)(2,1)} %get-tuple-element.66.dv, bf16[3,1024,512]{2,1,0:T(8,128)(2,1)} %bitcast.110, ...), custom_call_target="tpu_custom_call" | custom-call | flops 2818572288 | bytes 10000000 | tf_op jit(solution)/shard_map/pallas_call | solution.py:19
  173.4 14.7 %shard_map.340 = (f32[2,448,1024]{2,1,0:T(8,128)}, f32[4,1024]{1,0:T(4,128)}) custom-call(s32[1]{0:T(128)} %bitcast.t_ref, bf16[448,1024]{1,0:T(8,128)(2,1)} %get-tuple-element.68.g_s0.l_own, bf16[1024,1024]{1,0:T(8,128)(2,1)} %w_own.7, bf16[1024,1024]{1,0:T(8,128)(2,1)} %collective-permute-done.w_oth, bf16[2,448,1024]{2,1,0:T(8,128)(2,1)} %bitcast.101, ...), custom_call_target="tpu_custom_call" | custom-call | flops 1879048192 | bytes 10000000 | tf_op jit(solution)/shard_map/pallas_call | solution.py:19
  188.1 0.8 slice_bitcast_fusion
  188.9 20.0 %shard_map.344 = f32[32,384]{1,0:T(8,128)} custom-call(s32[100,112]{1,0:T(8,128)} %pad.26.index, f32[3584,112]{1,0:T(8,128)} %get-tuple-element.78.sums), custom_call_target="tpu_custom_call" | custom-call | flops 629145600 | bytes 2000000 | tf_op jit(solution)/shard_map/pallas_call | solution.py:19
  209.1 1.2 pad_maximum_fusion.1
  211.8 5.9 %reshape.596 = f32[2,4,112,2,512]{4,3,2,1,0:T(2,128)} reshape(f32[2,448,1024]{2,1,0:T(8,128)} %get-tuple-element.69) | data formatting | bytes 7340032 | tf_op jit(solution)/shard_map/reshape | solution.py:842
  217.8 1.9 slice-done
  219.7 3.8 copy.45
  223.7 1.5 fusion.2
  225.2 1.0 convert_element_type.39
  226.4 1.2 pad_maximum_fusion.r_own
  228.3 5.6 %shard_map.342 = bf16[1024,512]{1,0:T(8,128)(2,1)} custom-call(bf16[448,1024]{1,0:T(8,128)(2,1)} %get-tuple-element.72.l_own, bf16[448,1024]{1,0:T(8,128)(2,1)} %collective-permute-done.10.l_sib, bf16[448,512]{1,0:T(8,128)(2,1)} %get-tuple-element.125.r_own, bf16[448,512]{1,0:T(8,128)(2,1)} %collective-permute-done.11.r_sib), custom_call_target="tpu_custom_call" | custom-call | flops 939524096 | bytes 3801088 | tf_op jit(solution)/shard_map/pallas_call | solution.py:19
  233.8 7.7 %shard_map.343 = bf16[1024,1024]{1,0:T(8,128)(2,1)} custom-call(bf16[448,1024]{1,0:T(8,128)(2,1)} %get-tuple-element.68.g_s0.l_own, bf16[448,1024]{1,0:T(8,128)(2,1)} %collective-permute-done.12.l_sib, bf16[448,1024]{1,0:T(8,128)(2,1)} %get-tuple-element.73.r_own, bf16[448,1024]{1,0:T(8,128)(2,1)} %collective-permute-done.13.r_sib), custom_call_target="tpu_custom_call" | custom-call | flops 1879048192 | bytes 5767168 | tf_op jit(solution)/shard_map/pallas_call | solution.py:19
  241.5 9.8 %shard_map.341 = bf16[1024,1536]{1,0:T(8,128)(2,1)} custom-call(bf16[448,1024]{1,0:T(8,128)(2,1)} %get-tuple-element.53.first.l_own, bf16[448,1024]{1,0:T(8,128)(2,1)} %collective-permute-done.8.l_sib, bf16[448,1536]{1,0:T(8,128)(2,1)} %pad_maximum_fusion.r_own, bf16[448,1536]{1,0:T(8,128)(2,1)} %collective-permute-done.9.r_sib), custom_call_target="tpu_custom_call" | custom-call | flops 2818572288 | bytes 7733248 | tf_op jit(solution)/shard_map/pallas_call | solution.py:19
  251.3 219.6 %shard_map.345 = (f32[64,2048]{1,0:T(8,128)}, f32[64,2048]{1,0:T(8,128)}, f32[64,1536]{1,0:T(8,128)}, f32[64,512]{1,0:T(8,128)}, f32[64,1024]{1,0:T(8,128)}, /*index=5*/f32[112,128]{1,0:T(8,128)}) custom-call(bf16[4,2,2,64,2048]{4,3,2,1,0:T(8,128)(2,1)} %bitcast.103, bf16[4,2,2,64,2048]{4,3,2,1,0:T(8,128)(2,1)} %bitcast.104, ...), custom_call_target="tpu_custom_call" | custom-call | tf_op jit(solution)/shard_map/pallas_call | solution.py:638
  470.9 1.4 fusion.16
  472.3 0.7 slice.217
  473.1 1.5 fusion.15
  474.5 1.4 slice.221
  475.9 1.3 slice_bitcast_fusion.10
  477.2 1.8 copy.60
  480.3 1.7 copy.68
  482.0 1.6 copy.69
  483.6 0.8 copy.70
  484.4 0.8 copy.71
  (140 shorter events, 13.9 us)
Async XLA Ops:
  0.7 6.3 %copy-start.14 = (f32[2,512]{1,0:T(2,128)S(1)}, f32[2,512]{1,0:T(2,128)}, u32[]{:S(2)}) copy-start(f32[2,512]{1,0:T(2,128)} %param.27) | copy-start | bytes 12292
  0.7 46.6 %collective-permute-start.2 = (bf16[3,1024,512]{2,1,0:T(8,128)(2,1)}, bf16[3,1024,512]{2,1,0:T(8,128)(2,1)}, u32[]{:S(2)}, u32[]{:S(2)}) collective-permute-start(bf16[3,1024,512]{2,1,0:T(8,128)(2,1)} %bitcast.108), channel_id=1, source_target_pairs={{0,1},{1,0},{2,3},{3,2},{4,5},{5,4},{6,7},{7,6},{8,9},{9,8},{10,11... | collective-permute-start | bytes 9437192 | tf_op jit(solution)/shard_map/ppermute | solution.py:439
  3.6 9.9 %collective-permute-start.1 = (f32[11408]{0:T(1024)S(1)}, f32[11408]{0:T(1024)S(1)}, u32[]{:S(2)}, u32[]{:S(2)}) collective-permute-start(f32[11408]{0:T(1024)S(1)} %concatenate.196), channel_id=1, source_target_pairs={{0,1},{1,0},{2,3},{3,2},{4,5},{5,4},{6,7},{7,6},{8,9},{9,8},{10,11... | collective-permute-start | bytes 136904 | tf_op jit(solution)/shard_map/ppermute | solution.py:439
  3.6 32.4 %collective-permute-start = (bf16[1024,1024]{1,0:T(8,128)(2,1)}, bf16[1024,1024]{1,0:T(8,128)(2,1)}, u32[]{:S(2)}, u32[]{:S(2)}) collective-permute-start(bf16[1024,1024]{1,0:T(8,128)(2,1)} %w_own.7), channel_id=1, source_target_pairs={{0,1},{1,0},{2,3},{3,2},{4,5},{5,4},{6,7},{7,6},{8,9},{9,8},{10,11... | collective-permute-start | bytes 6291464 | tf_op jit(solution)/shard_map/ppermute | solution.py:439
  4.1 65.6 %collective-permute-start.3 = (bf16[512,1024]{1,0:T(8,128)(2,1)}, bf16[512,1024]{1,0:T(8,128)(2,1)}, u32[]{:S(2)}, u32[]{:S(2)}) collective-permute-start(bf16[512,1024]{1,0:T(8,128)(2,1)} %w_own.6), channel_id=1, source_target_pairs={{0,1},{1,0},{2,3},{3,2},{4,5},{5,4},{6,7},{7,6},{8,9},{9,8},{10,11... | collective-permute-start | bytes 3145736 | tf_op jit(solution)/shard_map/ppermute | solution.py:439
  6.5 71.5 %collective-permute-start.5 = (bf16[2,448,512]{2,1,0:T(8,128)(2,1)}, bf16[2,448,512]{2,1,0:T(8,128)(2,1)}, u32[]{:S(2)}, u32[]{:S(2)}) collective-permute-start(bf16[2,448,512]{2,1,0:T(8,128)(2,1)} %bitcast.21.cot_own), channel_id=1, source_target_pairs={{0,1},{1,0},{2,3},{3,2},{4,5},{5,4},{6,7},{7,6},{8,9},{9,8},{10,11... | collective-permute-start | bytes 2752520 | tf_op jit(solution)/shard_map/ppermute | solution.py:439
  11.1 1.5 copy-start.8
  11.1 2.6 copy-start.18
  11.1 3.2 copy-start.7
  11.1 3.9 copy-start.19
  12.6 21.0 %copy-start.20 = (f32[512]{0:T(512)S(1)}, f32[512]{0:T(512)}, u32[]{:S(2)}) copy-start(f32[512]{0:T(512)} %param.31) | copy-start | bytes 6148
  12.6 21.6 %copy-start.15 = (f32[1024]{0:T(1024)S(1)}, f32[1024]{0:T(1024)}, u32[]{:S(2)}) copy-start(f32[1024]{0:T(1024)} %param.21) | copy-start | bytes 12292
  12.6 22.2 %copy-start.16 = (f32[1024]{0:T(1024)S(1)}, f32[1024]{0:T(1024)}, u32[]{:S(2)}) copy-start(f32[1024]{0:T(1024)} %param.22) | copy-start | bytes 12292
  12.6 22.8 %copy-start.21 = (f32[512]{0:T(512)S(1)}, f32[512]{0:T(512)}, u32[]{:S(2)}) copy-start(f32[512]{0:T(512)} %param.30) | copy-start | bytes 6148
  12.6 22.8 %copy-start.22 = (f32[512]{0:T(512)S(1)}, f32[512]{0:T(512)}, u32[]{:S(2)}) copy-start(f32[512]{0:T(512)} %param.32) | copy-start | bytes 6148
  69.7 7.3 %copy-start.25 = (s32[800]{0:T(1024)S(1)}, s32[800]{0:T(1024)}, u32[]{:S(2)}) copy-start(s32[800]{0:T(1024)} %param.38) | copy-start | bytes 9604
  76.9 2.7 collective-permute-start.4
  77.0 2.5 copy-start.10
  79.5 0.9 copy-start.29
  80.5 36.8 %copy-start.2 = (bf16[448,1024]{1,0:T(8,128)(2,1)S(1)}, bf16[448,1024]{1,0:T(8,128)(2,1)}, u32[]{:S(2)}) copy-start(bf16[448,1024]{1,0:T(8,128)(2,1)} %get-tuple-element.54.att) | copy-start | bytes 2752516
  116.7 4.6 collective-permute-start.7
  116.9 117.0 %collective-permute-start.13 = (bf16[448,1024]{1,0:T(8,128)(2,1)}, bf16[448,1024]{1,0:T(8,128)(2,1)}, u32[]{:S(2)}, u32[]{:S(2)}) collective-permute-start(bf16[448,1024]{1,0:T(8,128)(2,1)} %get-tuple-element.74), channel_id=1, source_target_pairs={{0,1},{1,0},{2,3},{3,2},{4,5},{5,4},{6,7},{7,6},{8,9},{9,8},{10,11... | collective-permute-start | bytes 2752520 | tf_op jit(solution)/shard_map/ppermute | solution.py:439
  118.2 92.5 %collective-permute-start.11 = (bf16[448,512]{1,0:T(8,128)(2,1)}, bf16[448,512]{1,0:T(8,128)(2,1)}, u32[]{:S(2)}, u32[]{:S(2)}) collective-permute-start(bf16[448,512]{1,0:T(8,128)(2,1)} %get-tuple-element.124), channel_id=1, source_target_pairs={{0,1},{1,0},{2,3},{3,2},{4,5},{5,4},{6,7},{7,6},{8,9},{9,8},{10,11... | collective-permute-start | bytes 1376264 | tf_op jit(solution)/shard_map/ppermute | solution.py:439
  120.9 90.3 %collective-permute-start.6 = (bf16[2,448,512]{2,1,0:T(8,128)(2,1)}, bf16[2,448,512]{2,1,0:T(8,128)(2,1)}, u32[]{:S(2)}, u32[]{:S(2)}) collective-permute-start(bf16[2,448,512]{2,1,0:T(8,128)(2,1)} %fusion.3), channel_id=1, source_target_pairs={{0,1},{1,0},{2,3},{3,2},{4,5},{5,4},{6,7},{7,6},{8,9},{9,8},{10,11... | collective-permute-start | bytes 2752520 | tf_op jit(solution)/shard_map/ppermute | solution.py:439
  121.3 0.9 copy-start.4
  158.9 1.5 copy-start
  158.9 1.7 copy-start.1
  188.9 21.8 %copy-start.24 = (f32[2,1024]{1,0:T(2,128)S(1)}, f32[2,1024]{1,0:T(2,128)}, u32[]{:S(2)}) copy-start(f32[2,1024]{1,0:T(2,128)} %get-tuple-element.76) | copy-start | bytes 24580
  188.9 21.8 %copy-start.23 = (f32[2,1024]{1,0:T(2,128)S(1)}, f32[2,1024]{1,0:T(2,128)}, u32[]{:S(2)}) copy-start(f32[2,1024]{1,0:T(2,128)} %get-tuple-element.77) | copy-start | bytes 24580
  188.9 21.8 %copy-start.12 = (f32[1,3,512]{2,1,0:T(4,128)S(1)}, f32[1,3,512]{2,1,0:T(4,128)}, u32[]{:S(2)}) copy-start(f32[1,3,512]{2,1,0:T(4,128)} %get-tuple-element.155) | copy-start | bytes 18436
  188.9 21.8 %copy-start.13 = (f32[1,3,512]{2,1,0:T(4,128)S(1)}, f32[1,3,512]{2,1,0:T(4,128)}, u32[]{:S(2)}) copy-start(f32[1,3,512]{2,1,0:T(4,128)} %get-tuple-element.156) | copy-start | bytes 18436
  209.0 1.7 copy-start.9
  209.0 2.6 copy-start.11
  209.0 19.3 %collective-permute-start.10 = (bf16[448,1024]{1,0:T(8,128)(2,1)}, bf16[448,1024]{1,0:T(8,128)(2,1)}, u32[]{:S(2)}, u32[]{:S(2)}) collective-permute-start(bf16[448,1024]{1,0:T(8,128)(2,1)} %get-tuple-element.72.l_own), channel_id=1, source_target_pairs={{0,1},{1,0},{2,3},{3,2},{4,5},{5,4},{6,7},{7,6},{8,9},{9,8},{10,11... | collective-permute-start | bytes 2752520 | tf_op jit(solution)/shard_map/ppermute | solution.py:439
  210.3 31.2 %collective-permute-start.9 = (bf16[448,1536]{1,0:T(8,128)(2,1)}, bf16[448,1536]{1,0:T(8,128)(2,1)}, u32[]{:S(2)}, u32[]{:S(2)}) collective-permute-start(bf16[448,1536]{1,0:T(8,128)(2,1)} %pad_maximum_fusion.1), channel_id=1, source_target_pairs={{0,1},{1,0},{2,3},{3,2},{4,5},{5,4},{6,7},{7,6},{8,9},{9,8},{10,11... | collective-permute-start | bytes 4128776 | tf_op jit(solution)/shard_map/ppermute | solution.py:439
  210.8 23.1 %collective-permute-start.12 = (bf16[448,1024]{1,0:T(8,128)(2,1)}, bf16[448,1024]{1,0:T(8,128)(2,1)}, u32[]{:S(2)}, u32[]{:S(2)}) collective-permute-start(bf16[448,1024]{1,0:T(8,128)(2,1)} %get-tuple-element.68.g_s0.l_own), channel_id=1, source_target_pairs={{0,1},{1,0},{2,3},{3,2},{4,5},{5,4},{6,7},{7,6},{8,9},{9,8},{10,11... | collective-permute-start | bytes 2752520 | tf_op jit(solution)/shard_map/ppermute | solution.py:439
  211.2 12.3 %collective-permute-start.14 = (f32[11408]{0:T(1024)S(1)}, f32[11408]{0:T(1024)S(1)}, u32[]{:S(2)}, u32[]{:S(2)}) collective-permute-start(f32[11408]{0:T(1024)S(1)} %concatenate.230), channel_id=1, source_target_pairs={{0,1},{1,0},{2,3},{3,2},{4,5},{5,4},{6,7},{7,6},{8,9},{9,8},{10,11... | collective-permute-start | bytes 136904 | tf_op jit(solution)/shard_map/ppermute | solution.py:439
  217.8 1.9 slice-start
  219.7 3.8 copy-start.28
  219.7 4.0 copy-start.3
  219.7 4.0 copy-start.26
  223.5 18.0 %collective-permute-start.8 = (bf16[448,1024]{1,0:T(8,128)(2,1)S(1)}, bf16[448,1024]{1,0:T(8,128)(2,1)}, u32[]{:S(2)}, u32[]{:S(2)}) collective-permute-start(bf16[448,1024]{1,0:T(8,128)(2,1)S(1)} %copy-done.28), channel_id=1, source_target_pairs={{0,1},{1,0},{2,3},{3,2},{4,5},{5,4},{6,7},{7,6},{8,9},{9,8},{10,11... | collective-permute-start | bytes 2752520 | tf_op jit(solution)/shard_map/ppermute | solution.py:439
  225.2 2.3 copy-start.17
  225.2 2.3 copy-start.27
  470.9 12.6 %copy-start.6 = (f32[64,2048]{1,0:T(8,128)S(1)}, f32[64,2048]{1,0:T(8,128)}, u32[]{:S(2)}) copy-start(f32[64,2048]{1,0:T(8,128)} %get-tuple-element.199) | copy-start | bytes 1572868
  470.9 13.4 %copy-start.5 = (f32[64,2048]{1,0:T(8,128)S(1)}, f32[64,2048]{1,0:T(8,128)}, u32[]{:S(2)}) copy-start(f32[64,2048]{1,0:T(8,128)} %get-tuple-element.87) | copy-start | bytes 1572868

commit v3 on v0

v3 whole, which is shorter than its diff:
```python
from types import SimpleNamespace

import jax
import jax.numpy as jnp
from jax import lax
from jax.experimental import pallas as pl
from jax.experimental.pallas import tpu as pltpu
from jax.sharding import PartitionSpec as P

EPS = 1e-05
F32 = jnp.float32
BF16 = jnp.bfloat16
MESH = pl.DeviceIdType.MESH
PAD = 112
LIMIT = 63 * 1024 * 1024


def shape(dims, dtype=F32):
    return jax.ShapeDtypeStruct(tuple(dims), dtype)


def kernel_call(body, small, large, outs, scratch, large_outs, collective=None):
    names = [*small, *large, *outs, *scratch]
    free, vmem = pl.BlockSpec(memory_space=pl.ANY), pl.BlockSpec(memory_space=pltpu.VMEM)
    more = {} if collective is None else dict(collective_id=collective, has_side_effects=True)

    def run(*refs):
        body(SimpleNamespace(**dict(zip(names, refs, strict=True))))

    results = pl.pallas_call(
        run,
        out_shape=tuple(outs.values()),
        in_specs=[vmem] * len(small) + [free] * len(large),
        out_specs=tuple(free if n in large_outs else vmem for n in outs),
        scratch_shapes=list(scratch.values()),
        compiler_params=pltpu.CompilerParams(vmem_limit_bytes=LIMIT, **more),
    )(*small.values(), *large.values())
    return SimpleNamespace(**dict(zip(outs, results)))


def dot(a, b):
    return jnp.dot(a, b, preferred_element_type=F32)


def dot_nt(a, b):
    return lax.dot_general(a, b, (((1,), (1,)), ((), ())), preferred_element_type=F32)


def dot_tn(a, b):
    return lax.dot_general(a, b, (((0,), (0,)), ((), ())), preferred_element_type=F32)


def stats(x, width):
    mean = jnp.sum(x, 1, keepdims=True) * (1.0 / width)
    second = jnp.sum(x * x, 1, keepdims=True) * (1.0 / width)
    return mean, lax.rsqrt(second - mean * mean + EPS)


def norm_back(e, x, gain, width):
    mean, scale = stats(x, width)
    xhat = (x - mean) * scale
    scaled = e * gain
    first = jnp.sum(scaled, 1, keepdims=True) * (1.0 / width)
    cross = jnp.sum(scaled * xhat, 1, keepdims=True) * (1.0 / width)
    return scale * (scaled - first - xhat * cross), e * xhat


def steps(total, size, fn):
    @pl.loop(0, total // size)
    def _(step):
        fn(pl.ds(pl.multiple_of(step * size, size), size))


def add_to(ref, row, value):
    ref[row : row + 1, :] += jnp.sum(value, 0, keepdims=True)


def spread(rows, tokens, windows):
    row = lax.broadcasted_iota(jnp.int32, (rows, tokens), 0)
    col = lax.broadcasted_iota(jnp.int32, (rows, tokens), 1)
    area = tokens // windows
    w = row // PAD
    k = row - w * PAD
    real = k < area
    return (
        jnp.logical_and(real, w * area + k == col),
        jnp.logical_and(real, k * windows + w == col),
    )


def gather_rows(rows, tokens, windows):
    row = lax.broadcasted_iota(jnp.int32, (tokens, rows), 1)
    col = lax.broadcasted_iota(jnp.int32, (tokens, rows), 0)
    area = tokens // windows
    w = row // PAD
    k = row - w * PAD
    real = k < area
    return (
        jnp.logical_and(real, w * area + k == col),
        jnp.logical_and(real, k * windows + w == col),
    )


def ones(mask):
    return jnp.where(mask, 1.0, 0.0).astype(BF16)


class Link:
    def __init__(self, sends, recvs):
        self.sends, self.recvs = sends, recvs

    def copy(self, k, src, dst):
        return pltpu.make_async_remote_copy(
            src_ref=src,
            dst_ref=dst,
            send_sem=self.sends.at[k],
            recv_sem=self.recvs.at[k],
            device_id=(lax.axis_index("win"), 1 - lax.axis_index("tp")),
            device_id_type=MESH,
        )


def head_masks(rows, width, dim):
    lane = lax.broadcasted_iota(jnp.int32, (rows, width), 1) // dim
    return [lane == h for h in range(width // dim)]


def stacked(block, masks):
    return jnp.concatenate([jnp.where(m, block, 0.0).astype(BF16) for m in masks], 0)


def diagonal(a, b):
    zero = jnp.zeros((PAD, 128), BF16)
    rest = jnp.zeros((128 - PAD, 256), BF16)
    return jnp.concatenate(
        [jnp.concatenate([a, zero], 1), rest, jnp.concatenate([zero, b], 1), rest], 0
    )


def bias_of(bias, heads, g, per):
    return [bias[pl.ds(g * per + h, PAD, stride=heads), :] for h in range(per)]


def attention_forward(dim, heads, g, r):
    per = 128 // dim
    windows = r.qkvb.shape[1] // PAD
    scale = dim ** (-0.5)
    masks = head_masks(PAD, 128, dim)
    lanes = pl.ds(pl.multiple_of(g * 128, 128), 128)
    bias = bias_of(r.biasb, heads, g, per)
    done, sums = [], []
    for w in range(0, windows, 2):
        at = [pl.ds((w + u) * PAD, PAD) for u in range(2)]
        q, k, v = ([r.qkvb[s, a, lanes] for a in at] for s in range(3))
        both = dot_nt(
            jnp.concatenate([stacked(k[0], masks), stacked(k[1], masks)], 1),
            diagonal(q[0], q[1]),
        )
        for u in range(2):
            vt = v[u].T
            parts = []
            for h in range(per):
                s = both[h * PAD : (h + 1) * PAD, u * 128 : (u + 1) * 128] * scale + bias[h]
                top = jnp.max(s, 0, keepdims=True)
                e = jnp.exp(s - top)
                total = jnp.sum(e, 0, keepdims=True)
                p = (e * (1.0 / total)).astype(BF16)
                sums.append(top + jnp.log(total))
                parts.append(dot(vt[h * dim : (h + 1) * dim], p))
            done.append(jnp.concatenate(parts, 0).T[:PAD].astype(BF16))
    for w in range(windows):
        r.attb[pl.ds(w * PAD, PAD), lanes] = done[w]
    r.lse[g] = jnp.concatenate(sums, 0)


def attention_back(dim, heads, g, r):
    per = 128 // dim
    windows = r.qkvb.shape[1] // PAD
    scale = dim ** (-0.5)
    masks = head_masks(PAD, 128, dim)
    lanes = pl.ds(pl.multiple_of(g * 128, 128), 128)
    bias = bias_of(r.biasb, heads, g, per)
    totals, done = [None] * per, []
    for w in range(windows):
        at = pl.ds(w * PAD, PAD)
        q, k, v = r.qkvb[0, at, lanes], r.qkvb[1, at, lanes], r.qkvb[2, at, lanes]
        go = r.ex[0, at, lanes]
        both = dot_nt(
            jnp.concatenate([stacked(k, masks), stacked(v, masks)], 1), diagonal(q, go)
        )
        kt = k.T
        p_parts, g_parts, dqs = [], [], []
        for h in range(per):
            here = slice(h * PAD, (h + 1) * PAD)
            p = jnp.exp(
                both[here, :128] * scale + bias[h] - r.lse[g, pl.ds(w * per + h, 1), :]
            )
            dp = both[here, 128:]
            gs = (p * (dp - jnp.sum(dp * p, 0, keepdims=True))).astype(BF16)
            wide = gs.astype(F32)
            totals[h] = wide if w == 0 else totals[h] + wide
            p_parts.append(p.astype(BF16))
            g_parts.append(gs)
            dqs.append(dot(kt[h * dim : (h + 1) * dim], gs))
        back = dot(
            jnp.concatenate([jnp.concatenate(p_parts, 0), jnp.concatenate(g_parts, 0)], 1),
            diagonal(go, q),
        )
        dv, dk = back[:PAD, :128], back[:PAD, 128:]
        for h in range(1, per):
            here = slice(h * PAD, (h + 1) * PAD)
            dv = jnp.where(masks[h], back[here, :128], dv)
            dk = jnp.where(masks[h], back[here, 128:], dk)
        dq = jnp.concatenate(dqs, 0).T[:PAD] * scale
        done.append((dq.astype(BF16), (dk * scale).astype(BF16), dv.astype(BF16)))
    q_sum = jnp.zeros((1, 128), F32)
    v_sum = jnp.zeros((1, 128), F32)
    for w in range(windows):
        for s in range(3):
            r.qkvb[s, pl.ds(w * PAD, PAD), lanes] = done[w][s]
        q_sum += jnp.sum(done[w][0].astype(F32), 0, keepdims=True)
        v_sum += jnp.sum(done[w][2].astype(F32), 0, keepdims=True)
    for h in range(per):
        r.sums[pl.ds(g * per + h, PAD, stride=heads), :] = totals[h]
    r.vq[0:1, lanes] = q_sum
    r.vq[1:2, lanes] = v_sum


PAIRS = 4


def onehot_of(index, first, entries):
    rows = [index[pl.ds(first + u, 1), :] for u in range(PAIRS)]
    ids = lax.broadcasted_iota(jnp.int32, (entries, rows[0].shape[1]), 0)
    return jnp.concatenate([ones(ids == row) for row in rows], 1)


def bias_spread(area, heads, table, index, out):
    entries = table.shape[1]
    top = table.astype(BF16)
    both = jnp.concatenate([top, (table - top.astype(F32)).astype(BF16)], 0)

    @pl.loop(0, area // PAIRS)
    def _(i):
        value = dot(both, onehot_of(index, i * PAIRS, entries))
        value = value[:heads] + value[heads:]
        for u in range(PAIRS):
            at = pl.ds(pl.multiple_of((i * PAIRS + u) * heads, heads), heads)
            out[at, :] = value[:, u * 128 : (u + 1) * 128]

    out[pl.ds(area * heads, (PAD - area) * heads), :] = jnp.full(
        ((PAD - area) * heads, out.shape[1]), -1e30, F32
    )


def rel_sum(area, heads, index, sums, rel):
    entries = rel.shape[1]
    rel[...] = jnp.zeros_like(rel)

    @pl.loop(0, area // PAIRS)
    def _(i):
        hot = onehot_of(index, i * PAIRS, entries)
        s = jnp.concatenate(
            [
                sums[pl.ds(pl.multiple_of((i * PAIRS + u) * heads, heads), heads), :]
                for u in range(PAIRS)
            ],
            1,
        )
        top = s.astype(BF16)
        low = (s - top.astype(F32)).astype(BF16)
        both = dot_nt(jnp.concatenate([top, low], 0), hot)
        rel[...] += both[:heads] + both[heads:]


def win_sizes(count):
    side = 1
    while 4 * (side + 1) * (side + 1) <= count:
        side += 1
    return count // (side * side), side, side


def my_place(sizes):
    me = lax.axis_index("win")
    _, ny, nx = sizes
    return lax.div(me, ny * nx), lax.rem(lax.div(me, nx), ny), lax.rem(me, nx)


def wins_along(sizes, place, axis):
    z, y, x = place
    strides = (sizes[1] * sizes[2], sizes[2], 1)
    base = z * strides[0] + y * strides[1] + x
    found = []
    for d in range(1, sizes[axis]):
        c = lax.rem(place[axis] + d, sizes[axis])
        found.append((d, c, base + (c - place[axis]) * strides[axis]))
    return found


def enter(sizes=None, place=None):
    barrier = pltpu.get_barrier_semaphore()
    tp = lax.axis_index("tp")
    peers = [(lax.axis_index("win"), 1 - tp)]
    if sizes is not None:
        for axis in range(3):
            peers += [(w, tp) for _, _, w in wins_along(sizes, place, axis)]
    for peer in peers:
        pl.semaphore_signal(barrier, inc=1, device_id=peer, device_id_type=MESH)
    pl.semaphore_wait(barrier, len(peers))


class Scatter:
    def __init__(self, sizes, place, order, src, bufs, sends, recvs, unit):
        self.sizes, self.place, self.order = sizes, place, order
        self.src, self.bufs, self.sends, self.recvs, self.unit = src, bufs, sends, recvs, unit

    def pick(self, step, c):
        if step == 0:
            return self.src.at[:, :, c] if self.order[0] == 2 else self.src.at[:, c]
        before = self.bufs[step - 1].at[0]
        if step == 1:
            return before.at[:, c]
        return before.at[c]

    def copies(self, step):
        axis = self.order[step]
        tp = lax.axis_index("tp")
        made = []
        for d, c, w in wins_along(self.sizes, self.place, axis):
            made.append(
                pltpu.make_async_remote_copy(
                    src_ref=self.pick(step, c),
                    dst_ref=self.bufs[step].at[d - 1],
                    send_sem=self.sends.at[self.unit, step, d - 1],
                    recv_sem=self.recvs.at[self.unit, step, d - 1],
                    device_id=(w, tp),
                    device_id_type=MESH,
                )
            )
        return made

    def start(self, step):
        for copy in self.copies(step):
            copy.start()

    def wait_sent(self, step):
        for copy in self.copies(step):
            copy.wait_send()

    def finish(self, step, out=None):
        copies = self.copies(step)
        for copy in copies:
            copy.wait_recv()
        mine = self.pick(step, self.place[self.order[step]])
        buf = self.bufs[step]
        lead = mine.shape[:-2]
        rows, n = mine.shape[-2:]
        width = min(n, 512)
        if step == 2:
            for b in range(n // width):
                at = pl.ds(b * width, width)
                total = mine[:, at].astype(F32)
                for d in range(len(copies)):
                    total += buf[d, :, at].astype(F32)
                out[:, at] = total
            return
        count = 1
        for size in lead:
            count *= size

        @pl.loop(0, count)
        def _(i):
            where = (i,) if len(lead) == 1 else (lax.div(i, lead[1]), lax.rem(i, lead[1]))
            for b in range(n // width):
                at = pl.ds(b * width, width)
                total = mine[(*where, slice(None), at)].astype(F32)
                for d in range(len(copies)):
                    total += buf[(d, *where, slice(None), at)].astype(F32)
                buf[(0, *where, slice(None), at)] = total.astype(BF16)


X_FIRST, Y_FIRST = (2, 1, 0), (1, 2, 0)


def all_sum(sizes, place, src, bufs, sends, recvs):
    tp = lax.axis_index("tp")
    for step, axis in enumerate((2, 1, 0)):
        copies = []
        for d, c, w in wins_along(sizes, place, axis):
            copies.append(
                pltpu.make_async_remote_copy(
                    src_ref=src.at[step],
                    dst_ref=bufs.at[step, d - 1],
                    send_sem=sends.at[step, d - 1],
                    recv_sem=recvs.at[step, d - 1],
                    device_id=(w, tp),
                    device_id_type=MESH,
                )
            )
        for copy in copies:
            copy.start()
        total = src[step]
        for d, copy in enumerate(copies):
            copy.wait()
            total += bufs[step, d]
        src[step + 1] = total


def front_body(dim, heads, area, r):
    enter()
    t = lax.axis_index("tp")
    who = (t, 1 - t)
    rows, model = r.firstb.shape
    half = model // 2
    windows = rows // PAD
    tokens = windows * area
    link = Link(r.xsend, r.xrecv)
    own_cols = pl.ds(pl.multiple_of(t * half, half), half)
    oth_cols = pl.ds(pl.multiple_of((1 - t) * half, half), half)

    def load(k, src, dst):
        return pltpu.make_async_copy(src, dst, r.lsem.at[k])

    c_wm = link.copy(0, r.wm, r.wmb.at[1])
    c_wm.start()
    loads = [load(k, r.pixels.at[:, k % 2, :, k // 2], r.pix.at[k]) for k in range(4)]
    loads += [load(4, r.cot, r.cotb.at[0]), load(5, r.wm, r.wmb.at[0])]
    for one in loads:
        one.start()
    vx = r.vx
    vx[0] = jnp.zeros(vx.shape[1:], F32)
    for k, ref in enumerate((r.mg, r.ms)):
        for j in range(2):
            vx[0, 2 * k + j : 2 * k + j + 1, :] = ref[:, j * half : (j + 1) * half]
    for k, ref in enumerate((r.n1g, r.n1s, r.pb, r.n2g, r.n2s)):
        vx[0, 4 + k : 5 + k, :] = ref[...]
    vx[0, 9:11, :] = r.qb[...]
    vx[0, 16 : 16 + heads // 2, 0 : r.table.shape[1]] = r.table[...]
    c_vec = link.copy(1, vx.at[0], vx.at[1])
    c_vec.start()
    c_cot = link.copy(2, r.cot, r.cotb.at[1])
    c_cot.start()
    c_wq = link.copy(3, r.wqkv, r.wqb.at[1])
    c_wq.start()
    c_wp = link.copy(4, r.wp, r.wpb.at[pl.ds(half, half), :])
    c_wp.start()
    late = [load(6, r.wqkv, r.wqb.at[0]), load(7, r.wp, r.wpb.at[pl.ds(0, half), :])]
    for one in late:
        one.start()
    stores = []

    def store(src, dst):
        one = pltpu.make_async_copy(src, dst, r.ssem.at[len(stores)])
        stores.append(one)
        one.start()

    token_rows, pixel_rows = spread(rows, tokens, windows)
    pixel_rows = ones(pixel_rows)
    for k in range(4):
        loads[k].wait()
        r.xb[k] = dot(
            pixel_rows, r.pix[k].astype(F32).reshape(tokens, half).astype(BF16)
        ).astype(BF16)
    store(r.xb, r.x)

    c_vec.wait()
    mgo, nat = r.mgo, r.nat
    for side in range(2):
        for j in range(2):
            mgo[side, :, j * half : (j + 1) * half] = vx[side, j : j + 1, :]
            r.mso[side, :, j * half : (j + 1) * half] = vx[side, 2 + j : 3 + j, :]
        nat[0:5, (own_cols, oth_cols)[side]] = vx[side, 4:9, :]
    width = 2 * model

    def norm0(at):
        xs = [
            [r.xb[2 * who[i] + j, at, :].astype(F32) for j in range(2)] for i in range(2)
        ]

        def both(fn):
            return sum(jnp.sum(fn(x), 1, keepdims=True) for pair in xs for x in pair)

        mean = both(lambda x: x) * (1.0 / width)
        scale = lax.rsqrt(both(lambda x: x * x) * (1.0 / width) - mean * mean + EPS)
        for i in range(2):
            for j in range(2):
                cols = pl.ds(j * half, half)
                value = (xs[i][j] - mean) * scale * mgo[i, :, cols] + r.mso[i, :, cols]
                r.mnb[i, at, cols] = value.astype(BF16)

    steps(rows, 64, norm0)
    c_mn = link.copy(6, r.mnb.at[1], r.mn_sib)
    c_mn.start()
    store(r.mnb.at[0], r.mn_own)

    entries = r.tableb.shape[1]
    for side in range(2):
        r.tableb[side * (heads // 2) : (side + 1) * (heads // 2), :] = vx[
            side, 16 : 16 + heads // 2, 0:entries
        ]
    bias_spread(area, heads, r.tableb[...], r.index, r.biasb)
    store(r.biasb, r.bias)

    loads[4].wait()
    c_cot.wait()
    total = jnp.zeros((1, half), F32)
    for side in range(2):
        at = pl.ds(pl.multiple_of(who[side] * tokens, tokens), tokens)
        pick = ones(jnp.logical_and(token_rows, r.keep[who[side]] > 0))
        mine = dot(pick, r.cotb[0, at, :])
        total += jnp.sum(mine, 0, keepdims=True)
        here = pl.ds(side * rows, rows)
        r.gfb[here, own_cols] = mine.astype(BF16)
        r.gfb[here, oth_cols] = dot(pick, r.cotb[1, at, :]).astype(BF16)
    r.gb2[...] = total
    store(r.gfb, r.gf)

    loads[5].wait()

    def own_part(at):
        r.s0b[:, at] = dot(r.mnb[0], r.wmb[0, :, at])

    steps(model, 512, own_part)
    c_wm.wait()
    store(r.wmb.at[1], r.wm_oth)

    def oth_part(at):
        r.s0b[:, at] += dot(r.mnb[1], r.wmb[1, :, at])

    steps(model, 512, oth_part)
    store(r.s0b, r.stream0)

    def norm1(at):
        x = r.s0b[at, :]
        mean, scale = stats(x, model)
        r.firstb[at, :] = ((x - mean) * scale * nat[0:1, :] + nat[1:2, :]).astype(BF16)

    steps(rows, 112, norm1)
    c_first = link.copy(5, r.firstb, r.first_sib)
    c_first.start()
    store(r.firstb, r.first_own)

    late[0].wait()
    for side in range(2):
        if side == 1:
            c_wq.wait()
            store(r.wqb.at[1], r.wqkv_oth)
        for s in range(3):
            cols = pl.ds(side * half, half)
            value = dot(r.firstb[...], r.wqb[side, s])
            if s != 1:
                value += vx[side, 9 + s // 2 : 10 + s // 2, :]
            r.qkvb[s, :, cols] = value.astype(BF16)
    store(r.qkvb, r.qkv)

    @pl.loop(0, model // 128)
    def _(g):
        attention_forward(dim, heads, g, r)

    c_att = link.copy(7, r.attb.at[:, pl.ds(half, half)], r.att_sib)
    c_att.start()
    store(r.attb.at[:, pl.ds(0, half)], r.att_own)

    late[1].wait()
    c_wp.wait()
    store(r.wpb.at[pl.ds(half, half), :], r.wp_oth)

    def project(at):
        value = dot(r.attb[...], r.wpb[:, at]) + nat[2:3, at]
        r.s1b[:, at] = r.s0b[:, at] + value

    steps(model, 512, project)
    store(r.s1b, r.stream1)

    def norm2(at):
        x = r.s1b[at, :]
        mean, scale = stats(x, model)
        r.secb[at, :] = ((x - mean) * scale * nat[3:4, :] + nat[4:5, :]).astype(BF16)

    steps(rows, 112, norm2)
    store(r.secb, r.second)
    for one in (c_mn, c_first, c_att):
        one.wait()
    for one in stores:
        one.wait()


def front(dim, heads, area, windows, small, large):
    rows, tokens = windows * PAD, windows * area
    model = large["wm"].shape[1]
    half = model // 2
    side = large["pixels"].shape[0:3:2]
    slots = -(-small["table"].shape[1] // 128) * 128
    vm, dma = pltpu.VMEM, pltpu.SemaphoreType.DMA
    big = dict(
        x=shape((4, rows, half), BF16), gf=shape((2 * rows, model), BF16),
        stream0=shape((rows, model)), stream1=shape((rows, model)),
        second=shape((rows, model), BF16), qkv=shape((3, rows, model), BF16),
        bias=shape((PAD * heads, 128)), first_own=shape((rows, model), BF16),
        first_sib=shape((rows, model), BF16), mn_own=shape((rows, model), BF16),
        mn_sib=shape((rows, model), BF16), att_own=shape((rows, half), BF16),
        att_sib=shape((rows, half), BF16), wm_oth=shape((model, model), BF16),
        wqkv_oth=shape((3, model, half), BF16), wp_oth=shape((half, model), BF16),
    )
    outs = dict(
        big, gb2=shape((1, half)), nat=shape((8, model)), mgo=shape((2, 1, model)),
        lse=shape((model // 128, windows * 128 // dim, 128)),
    )
    scratch = dict(
        wmb=vm((2, model, model), BF16), wqb=vm((2, 3, model, half), BF16),
        wpb=vm((model, model), BF16), pix=vm((4, *side, windows, half), BF16),
        xb=vm((4, rows, half), BF16), cotb=vm((2, 2 * tokens, half), BF16),
        gfb=vm((2 * rows, model), BF16), mnb=vm((2, rows, model), BF16),
        s0b=vm((rows, model), F32), s1b=vm((rows, model), F32), firstb=vm((rows, model), BF16),
        qkvb=vm((3, rows, model), BF16), biasb=vm((PAD * heads, 128), F32),
        attb=vm((rows, model), BF16), secb=vm((rows, model), BF16),
        vx=vm((2, 32, half), F32), mso=vm((2, 1, model), F32), tableb=vm((heads, slots), F32),
        lsem=dma((8,)), ssem=dma((16,)), xsend=dma((8,)), xrecv=dma((8,)),
    )

    def body(r):
        front_body(dim, heads, area, r)

    return kernel_call(body, small, large, outs, scratch, big, collective=2)


CHUNK = 512


def back_body(sizes, dim, heads, area, r):
    place = my_place(sizes)
    t = lax.axis_index("tp")
    who = (t, 1 - t)
    sec, gf, facc, gacc, st, ex = r.sec, r.gfb, r.facc, r.gacc, r.st, r.ex
    w1b, w2b, cotb, qkvb = r.w1b, r.w2b, r.cotb, r.qkvb
    rows, model = st.shape
    half = model // 2
    hidden = r.fc1.shape[1]
    chunks = hidden // CHUNK
    windows = rows // PAD
    tokens = windows * area
    mine, theirs = pl.ds(0, rows), pl.ds(rows, rows)
    left, right = pl.ds(0, half), pl.ds(half, half)
    link = Link(r.xsend, r.xrecv)
    own_cols = pl.ds(pl.multiple_of(t * half, half), half)
    oth_cols = pl.ds(pl.multiple_of((1 - t) * half, half), half)
    part = model // (sizes[0] * sizes[1] * sizes[2])

    def load(k, src, dst):
        return pltpu.make_async_copy(src, dst, r.lsem.at[k])

    def unit(u, order):
        slot = u % 8 if isinstance(u, int) else lax.rem(u, 8)
        bufs = [buf.at[u] for buf in (r.buf0, r.buf1, r.buf2)]
        return Scatter(sizes, place, order, r.src.at[slot], bufs, r.rsend, r.rrecv, u)

    def pair(k):
        return unit(2 * k, X_FIRST), unit(2 * k + 1, Y_FIRST)

    def finish(k, step):
        for one in pair(k):
            one.finish(step)
            one.start(step + 1)

    def put(slot, value):
        r.src[slot] = value.astype(BF16).reshape(*sizes, part, CHUNK)

    enter(sizes, place)
    c_sec = link.copy(0, r.second, sec.at[theirs])
    c_sec.start()
    loads = [
        load(0, r.second, sec.at[mine]), load(1, r.gf, gf), load(3, r.stream1, st),
        load(4, r.qkv, qkvb),
    ]
    for one in loads:
        one.start()

    def weights(c):
        slot = lax.rem(c, 2)
        cols = pl.ds(pl.multiple_of(c * CHUNK, CHUNK), CHUNK)
        return (
            pltpu.make_async_copy(r.fc1.at[:, cols], w1b.at[slot], r.wsem.at[0, slot]),
            pltpu.make_async_copy(r.fc2.at[cols, :], w2b.at[slot], r.wsem.at[1, slot]),
        )

    for one in weights(0):
        one.start()
    for one in loads[0:2]:
        one.wait()
    c_sec.wait()

    blocks = CHUNK // 128
    hid, dact, act, gh = r.sums, r.biasb, r.act, r.gh

    @pl.loop(0, chunks)
    def _(c):
        slot = lax.rem(c, 2)
        for one in weights(c):
            one.wait()

        @pl.when(c + 1 < chunks)
        def _():
            for one in weights(c + 1):
                one.start()

        of = pl.ds(pl.multiple_of(c * CHUNK, CHUNK), CHUNK)
        value = dot(sec[...], w1b[slot]) + r.b1[:, of]
        for b in range(blocks):
            hid[b * 2 * rows : (b + 1) * 2 * rows, :] = value[:, b * 128 : (b + 1) * 128]
        value = dot_nt(gf[...], w2b[slot])
        for b in range(blocks):
            dact[b * 2 * rows : (b + 1) * 2 * rows, :] = value[:, b * 128 : (b + 1) * 128]
        for b in range(blocks):
            lanes = pl.ds(b * 128, 128)

            def gelu(at):
                here = pl.ds(pl.multiple_of(b * 2 * rows + at.start, 128), at.size)
                x = hid[here, :]
                cdf = 0.5 * (1.0 + lax.erf(x * 0.7071067811865476))
                pdf = jnp.exp(x * x * -0.5) * 0.3989422804014327
                act[at, lanes] = (x * cdf).astype(BF16)
                gh[at, lanes] = (dact[here, :] * (cdf + x * pdf)).astype(BF16)

            steps(2 * rows, 128, gelu)
        r.gb1[:, of] = jnp.sum(gh[...].astype(F32), 0, keepdims=True)
        put(lax.rem(2 * c, 8), dot_tn(sec[...], gh[...]))
        unit(2 * c, X_FIRST).start(0)
        put(lax.rem(2 * c + 1, 8), dot_tn(gf[...], act[...]))
        unit(2 * c + 1, Y_FIRST).start(0)

        @pl.when(c == 0)
        def _():
            facc[...] = dot(act[...], w2b[slot])
            gacc[...] = dot_nt(gh[...], w1b[slot])

        @pl.when(c > 0)
        def _():
            facc[...] += dot(act[...], w2b[slot])
            gacc[...] += dot_nt(gh[...], w1b[slot])

        @pl.when(c >= 2)
        def _():
            finish(c - 2, 0)

    load(5, r.bias, r.biasb).start()
    for k, src in enumerate((r.wp_own, r.wp_oth)):
        load(8 + k, src, w2b.at[k]).start()
    ex[0] = gacc[theirs].astype(BF16)
    c_g2 = link.copy(1, ex.at[0], ex.at[1])
    c_g2.start()
    load(3, r.stream1, st).wait()
    fsend, fland = r.fsend, r.fland
    fsend[0] = facc[theirs, oth_cols].astype(BF16)
    fsend[1] = (facc[mine, oth_cols] + st[:, oth_cols]).astype(BF16)
    c_feed = link.copy(2, fsend, fland)
    c_feed.start()
    v2 = r.v2
    v2[...] = jnp.zeros_like(v2)
    c_g2.wait()

    def norm2(at):
        e = gacc[at, :] + ex[1, at, :].astype(F32)
        dv, hat = norm_back(e, st[at, :], r.nat[3:4, :], model)
        d = gf[at, :].astype(F32) + dv
        gacc[at, :] = d
        low = d.astype(BF16)
        sec[at, :] = low
        add_to(v2, 0, hat)
        add_to(v2, 1, e)
        add_to(v2, 2, low.astype(F32))

    steps(rows, 112, norm2)
    c_att = link.copy(3, sec.at[mine], sec.at[theirs])
    c_att.start()
    load(10, r.first_own, gf.at[mine]).start()
    load(11, r.first_sib, gf.at[theirs]).start()
    for k, src in enumerate((r.wp_own, r.wp_oth)):
        load(8 + k, src, w2b.at[k]).wait()
        ex[0, :, (left, right)[k]] = dot_nt(sec[mine, :], w2b[k]).astype(BF16)

    c_feed.wait()
    token_rows = gather_rows(rows, tokens, windows)[0]
    outs = []
    for side in range(2):
        value = facc[side * rows : (side + 1) * rows, own_cols] + fland[side].astype(F32)
        if side == 0:
            value += st[:, own_cols]
        pick = ones(jnp.logical_and(token_rows, r.keep[who[side]] > 0))
        fsend[side, 0:tokens, :] = dot(pick, (value + r.b2[...]).astype(BF16)).astype(BF16)
        at = pl.ds(pl.multiple_of(who[side] * tokens, tokens), tokens)
        outs.append(load(14 + side, fsend.at[side, pl.ds(0, tokens), :], r.out.at[at, :]))
        outs[-1].start()
    load(6, r.att_own, fland.at[0]).start()
    load(7, r.att_sib, fland.at[1]).start()
    load(12, r.stream0, st).start()

    load(4, r.qkv, qkvb).wait()
    load(5, r.bias, r.biasb).wait()

    @pl.loop(0, model // 128)
    def _(g):
        attention_back(dim, heads, g, r)

        @pl.when(lax.rem(g, 4) == 0)
        def _():
            finish(chunks - 2 + lax.div(g, 4), 0)

        @pl.when(lax.rem(g, 2) == 1)
        def _():
            finish(lax.div(g, 2), 1)

    dland = cotb.at[pl.ds(0, 3)]
    c_qkv = link.copy(4, qkvb.at[:, :, right], dland)
    c_qkv.start()

    def slice_of(k):
        return (r.wqkv_own, r.wqkv_oth)[k // 3].at[k % 3]

    load(16, slice_of(0), w1b.at[0]).start()

    first_unit = 2 * chunks

    def free(u):
        unit(u - 8, X_FIRST if u % 2 == 0 else Y_FIRST).wait_sent(0)

    u_qkv = [first_unit, first_unit + 1, first_unit + 2]
    u_proj, u_merge = first_unit + 3, [first_unit + 4, first_unit + 5]
    c_att.wait()
    load(6, r.att_own, fland.at[0]).wait()
    load(7, r.att_sib, fland.at[1]).wait()
    free(u_proj)
    put(u_proj % 8, dot_tn(sec[mine, :], fland[0]) + dot_tn(sec[theirs, :], fland[1]))
    unit(u_proj, Y_FIRST).start(0)

    for k in range(6):
        load(16 + k % 2, slice_of(k), w1b.at[k % 2]).wait()
        if k + 1 < 6:
            load(16 + (k + 1) % 2, slice_of(k + 1), w1b.at[(k + 1) % 2]).start()
        value = dot_nt(qkvb[k % 3, :, (left, right)[k // 3]], w1b[k % 2])
        if k == 0:
            facc[theirs, :] = value
        else:
            facc[theirs, :] += value
    load(12, r.stream0, st).wait()
    v1 = r.v1
    v1[...] = jnp.zeros_like(v1)

    def norm1(at):
        e = facc[pl.ds(pl.multiple_of(rows + at.start, 16), at.size), :]
        dv, hat = norm_back(e, st[at, :], r.nat[0:1, :], model)
        sec[at, :] = (gacc[at, :] + dv).astype(BF16)
        add_to(v1, 0, hat)
        add_to(v1, 1, e)

    steps(rows, 112, norm1)
    c_s0 = link.copy(5, sec.at[mine], ex.at[1])
    c_s0.start()

    load(10, r.first_own, gf.at[mine]).wait()
    load(11, r.first_sib, gf.at[theirs]).wait()
    for k in range(2):
        load(8 + k, r.wm_own.at[(left, right)[k], :], w2b.at[k]).start()
    c_qkv.wait()
    for s in range(3):
        free(u_qkv[s])
        put(u_qkv[s] % 8, dot_tn(gf[mine, :], qkvb[s, :, left]) + dot_tn(gf[theirs, :], dland[s]))
        unit(u_qkv[s], X_FIRST if s % 2 == 0 else Y_FIRST).start(0)
    load(1, r.x, cotb).start()
    load(10, r.mn_own, gf.at[mine]).start()
    load(11, r.mn_sib, gf.at[theirs]).start()

    c_s0.wait()
    load(10, r.mn_own, gf.at[mine]).wait()
    load(11, r.mn_sib, gf.at[theirs]).wait()
    for k in range(2):
        cols = (left, right)[k]
        free(u_merge[k])
        put(u_merge[k] % 8, dot_tn(sec[mine, :], gf[mine, cols]) + dot_tn(ex[1], gf[theirs, cols]))
        unit(u_merge[k], (X_FIRST, Y_FIRST)[k]).start(0)
    last = chunks + 2
    finish(chunks + 1, 0)
    finish(chunks, 0)

    rel_sum(area, heads, r.index, r.sums, r.rel)
    finish(chunks + 1, 1)
    finish(chunks, 1)
    finish(last, 0)

    for k in range(4):
        load(8 + k % 2, (r.wm_own, r.wm_oth)[k // 2].at[(left, right)[k % 2], :],
             w2b.at[k % 2]).wait()
        facc[k // 2 * rows : (k // 2 + 1) * rows, (left, right)[k % 2]] = dot_nt(
            sec[mine, :], w2b[k % 2]
        )
        if k < 2:
            load(8 + k, r.wm_oth.at[(left, right)[k], :], w2b.at[k]).start()
    load(1, r.x, cotb).wait()
    v0 = r.v0
    v0[...] = jnp.zeros_like(v0)
    width = 2 * model

    def norm0(at):
        def both(fn):
            return sum(jnp.sum(fn(i, j), 1, keepdims=True) for i in range(2) for j in range(2))

        def cols(j):
            return (left, right)[j]

        def here(i):
            return pl.ds(pl.multiple_of(i * rows + at.start, 16), at.size)

        xs = [[cotb[2 * who[i] + j, at, :].astype(F32) for j in range(2)] for i in range(2)]
        es = [[facc[here(i), cols(j)] for j in range(2)] for i in range(2)]
        sc = [[es[i][j] * r.mgo[i, :, cols(j)] for j in range(2)] for i in range(2)]
        mean = both(lambda i, j: xs[i][j]) * (1.0 / width)
        second = both(lambda i, j: xs[i][j] * xs[i][j]) * (1.0 / width)
        scale = lax.rsqrt(second - mean * mean + EPS)
        hats = [[(xs[i][j] - mean) * scale for j in range(2)] for i in range(2)]
        low = both(lambda i, j: sc[i][j]) * (1.0 / width)
        cross = both(lambda i, j: sc[i][j] * hats[i][j]) * (1.0 / width)
        for i in range(2):
            for j in range(2):
                d = scale * (sc[i][j] - low - hats[i][j] * cross)
                qkvb[i, at, cols(j)] = d.astype(BF16)
                v0[2 * i : 2 * i + 1, cols(j)] += jnp.sum(es[i][j] * hats[i][j], 0, keepdims=True)
                v0[2 * i + 1 : 2 * i + 2, cols(j)] += jnp.sum(es[i][j], 0, keepdims=True)

    steps(rows, 64, norm0)
    finish(last, 1)

    vs, vx = r.vs, r.vx
    heads_here = heads // 2
    for side, dst in ((0, vs.at[0]), (1, vx.at[0])):
        cols = (own_cols, oth_cols)[side]
        dst[...] = jnp.zeros(dst.shape, F32)
        for i in range(2):
            for j in range(2):
                dst[2 * i + j : 2 * i + j + 1, :] = v0[
                    2 * side + i : 2 * side + i + 1, j * half : (j + 1) * half
                ]
        dst[4:6, :] = v1[:, cols]
        dst[6:8, :] = r.vq[:, (left, right)[side]]
        dst[8:11, :] = v2[0:3, cols]
        if side == 0:
            dst[11:12, :] = r.gb2[...]
            for j in range(hidden // half):
                dst[12 + j : 13 + j, :] = r.gb1[:, j * half : (j + 1) * half]
        dst[16 : 16 + heads_here, 0 : r.rel.shape[1]] = r.rel[
            side * heads_here : (side + 1) * heads_here, :
        ]
    c_vec = link.copy(6, vx.at[0], vx.at[1])
    c_vec.start()

    pixel_rows = ones(gather_rows(rows, tokens, windows)[1])
    for b in range(2):
        for a in range(2):
            value = dot(pixel_rows, qkvb[b, :, (left, right)[a]])
            if b == 1:
                outs[2 + a].wait()
            r.pix[a] = value.reshape(*r.pix.shape[1:])
            outs.append(load(2 * b + a, r.pix.at[a], r.pixels_grad.at[:, a, :, who[b]]))
            outs[-1].start()
    c_vec.wait()
    vs[0] += vx[1]
    all_sum(sizes, place, vs, r.vbuf, r.vsend, r.vrecv)
    v = vs.at[3]
    for i in range(2):
        for j in range(2):
            (r.o_mg, r.o_ms)[i][:, j * half : (j + 1) * half] = v[2 * i + j : 2 * i + j + 1, :]
    for k, ref in enumerate((r.o_n1g, r.o_n1s)):
        ref[...] = v[4 + k : 5 + k, :]
    r.o_qb[...] = v[6:8, :]
    for k, ref in enumerate((r.o_n2g, r.o_n2s, r.o_pb, r.o_b2)):
        ref[...] = v[8 + k : 9 + k, :]
    for j in range(hidden // half):
        r.o_b1[:, j * half : (j + 1) * half] = v[12 + j : 13 + j, :]
    r.o_rel[...] = v[16 : 16 + heads_here, 0 : r.o_rel.shape[1]]

    for k in range(chunks):
        at = pl.ds(k * CHUNK, CHUNK)
        unit(2 * k, X_FIRST).finish(2, r.o_fc1.at[:, at])
        unit(2 * k + 1, Y_FIRST).finish(2, r.o_fc2.at[:, at])
    for s in range(3):
        unit(u_qkv[s], X_FIRST if s % 2 == 0 else Y_FIRST).finish(2, r.o_qkv.at[s])
    unit(u_proj, Y_FIRST).finish(2, r.o_proj)
    for k in range(2):
        unit(u_merge[k], (X_FIRST, Y_FIRST)[k]).finish(2, r.o_merge.at[:, (left, right)[k]])
    for one in outs[:2] + outs[4:]:
        one.wait()
    for u in range(first_unit + 6):
        one = unit(u, X_FIRST if u % 2 == 0 else Y_FIRST)
        for step in range(3):
            if step > 0 or u >= first_unit + 6 - 8:
                one.wait_sent(step)


def back(count, dim, heads, area, windows, entries, small, large):
    sizes = win_sizes(count)
    rows, tokens = windows * PAD, windows * area
    hidden = large["fc1"].shape[1]
    model = large["fc1"].shape[0]
    half = model // 2
    side = int(area**0.5)
    slots = -(-entries // 128) * 128
    n_units = 2 * (hidden // CHUNK) + 6
    part = model // count
    most = max(sizes) - 1
    nz, ny, nx = sizes
    big = dict(
        out=shape((2 * tokens, half), BF16),
        pixels_grad=shape((side, 2, side, 2, windows, half)),
    )
    outs = dict(
        big, o_mg=shape((1, model)), o_ms=shape((1, model)),
        o_n1g=shape((1, half)), o_n1s=shape((1, half)), o_qb=shape((2, half)),
        o_n2g=shape((1, half)), o_n2s=shape((1, half)), o_pb=shape((1, half)),
        o_b1=shape((1, hidden)), o_b2=shape((1, half)), o_rel=shape((heads // 2, entries)),
        o_fc1=shape((part, hidden)), o_fc2=shape((part, hidden)), o_qkv=shape((3, part, half)),
        o_proj=shape((part, half)), o_merge=shape((part, model)),
    )
    vm, dma = pltpu.VMEM, pltpu.SemaphoreType.DMA
    scratch = dict(
        sec=vm((2 * rows, model), BF16), gfb=vm((2 * rows, model), BF16),
        facc=vm((2 * rows, model), F32), gacc=vm((2 * rows, model), F32),
        st=vm((rows, model), F32), ex=vm((2, rows, model), BF16),
        w1b=vm((2, model, CHUNK), BF16), w2b=vm((2, CHUNK, model), BF16),
        cotb=vm((4, rows, half), BF16), qkvb=vm((3, rows, model), BF16),
        biasb=vm((PAD * heads, 128), F32), sums=vm((PAD * heads, 128), F32),
        act=vm((2 * rows, CHUNK), BF16), gh=vm((2 * rows, CHUNK), BF16),
        fsend=vm((2, rows, half), BF16), fland=vm((2, rows, half), BF16),
        pix=vm((2, side, side, windows, half), F32),
        src=vm((8, nz, ny, nx, part, CHUNK), BF16),
        buf0=vm((n_units, nx - 1, nz, ny, part, CHUNK), BF16),
        buf1=vm((n_units, ny - 1, nz, part, CHUNK), BF16),
        buf2=vm((n_units, nz - 1, part, CHUNK), BF16),
        v0=vm((4, model), F32), v1=vm((2, model), F32), v2=vm((3, model), F32),
        vq=vm((2, model), F32), rel=vm((heads, slots), F32), gb1=vm((1, hidden), F32),
        vs=vm((4, 32, half), F32), vx=vm((2, 32, half), F32), vbuf=vm((3, most, 32, half), F32),
        lsem=dma((18,)), wsem=dma((2, 2)), xsend=dma((8,)), xrecv=dma((8,)),
        rsend=dma((n_units, 3, most)), rrecv=dma((n_units, 3, most)),
        vsend=dma((3, most)), vrecv=dma((3, most)),
    )

    def body(r):
        back_body(sizes, dim, heads, area, r)

    return kernel_call(body, small, large, outs, scratch, big, collective=1)


def hand_on(arrays):
    names = list(arrays)

    free = pl.BlockSpec(memory_space=pl.ANY)
    n = len(names)

    def run(*refs):
        given, taken, held, sem = refs[:n], refs[n : 2 * n], refs[2 * n : 3 * n], refs[3 * n]
        ins = [pltpu.make_async_copy(given[k], held[k], sem.at[0, k]) for k in range(n)]
        outs = [pltpu.make_async_copy(held[k], taken[k], sem.at[1, k]) for k in range(n)]
        for one in ins:
            one.start()
        for one, other in zip(ins, outs):
            one.wait()
            other.start()
        for one in outs:
            one.wait()

    results = pl.pallas_call(
        run,
        out_shape=tuple(shape(a.shape, a.dtype) for a in arrays.values()),
        in_specs=[free] * n,
        out_specs=(free,) * n,
        scratch_shapes=[pltpu.VMEM(a.shape, a.dtype) for a in arrays.values()]
        + [pltpu.SemaphoreType.DMA((2, n))],
    )(*arrays.values())
    return SimpleNamespace(**dict(zip(names, results)))


def solution(mesh):
    count = mesh.shape["win"]

    def shards(
        pixels, merge_gain, merge_shift, merge_weight, norm1_gain, norm1_shift, qkv_weight,
        qkv_bias, rel_table, proj_weight, proj_bias, norm2_gain, norm2_shift, fc1_weight,
        fc1_bias, fc2_weight, fc2_bias, rel_index, keep, cotangent,
    ):
        wins, height, _, channels = pixels.shape
        side = height // 2
        area = side * side
        rows = wins * PAD
        model = merge_weight.shape[1]
        half = model // 2
        heads = 2 * rel_table.shape[1]
        dim = half // rel_table.shape[1]
        hidden = fc1_weight.shape[1]

        def row(v):
            return v.reshape(1, -1)

        index = jnp.pad(rel_index.T, ((0, 0), (0, 128 - area)))
        kept = keep.reshape(2, 1, wins * area)
        kept_rows = jnp.pad(
            keep.reshape(2 * wins, area), ((0, 0), (0, PAD - area))
        ).reshape(2, 1, rows)
        wqkv = qkv_weight.transpose(1, 0, 2)
        a = front(
            dim, heads, area, wins,
            dict(
                mg=row(merge_gain), ms=row(merge_shift), n1g=row(norm1_gain),
                n1s=row(norm1_shift), pb=row(proj_bias), n2g=row(norm2_gain),
                n2s=row(norm2_shift), qb=qkv_bias, table=rel_table.T, index=index, keep=kept,
            ),
            dict(
                pixels=pixels.transpose(1, 2, 0, 3).reshape(side, 2, side, 2, wins, channels),
                wm=merge_weight, wqkv=wqkv, wp=proj_weight, cot=cotangent,
            ),
        )
        b = back(
            count, dim, heads, area, wins, rel_table.shape[0],
            dict(
                keep=kept_rows, b1=row(fc1_bias), b2=row(fc2_bias), nat=a.nat, mgo=a.mgo,
                lse=a.lse, index=index, gb2=a.gb2,
            ),
            dict(
                second=a.second, gf=a.gf, stream1=a.stream1, stream0=a.stream0,
                fc1=fc1_weight, fc2=fc2_weight, wp_own=proj_weight, wp_oth=a.wp_oth,
                wqkv_own=wqkv, wqkv_oth=a.wqkv_oth, wm_own=merge_weight, wm_oth=a.wm_oth,
                att_own=a.att_own, att_sib=a.att_sib, qkv=a.qkv, bias=a.bias,
                first_own=a.first_own, first_sib=a.first_sib, mn_own=a.mn_own, mn_sib=a.mn_sib,
                x=a.x,
            ),
        )
        f = hand_on(vars(b))

        def flat(v):
            return v.reshape(-1)

        pixels_grad = f.pixels_grad.reshape(height, height, wins, channels)
        return (
            f.out, pixels_grad.transpose(2, 0, 1, 3), flat(f.o_mg), flat(f.o_ms), f.o_merge.T,
            flat(f.o_n1g), flat(f.o_n1s), f.o_qkv.transpose(1, 0, 2), f.o_qb, f.o_rel.T,
            f.o_proj.T, flat(f.o_pb), flat(f.o_n2g), flat(f.o_n2s), f.o_fc1, flat(f.o_b1),
            f.o_fc2.T, flat(f.o_b2),
        )

    in_specs = (
        P(("win", "tp"), None, None, None), P("tp"), P("tp"), P("tp", None), P("tp"), P("tp"),
        P(None, None, "tp"), P(None, "tp"), P(None, "tp"), P("tp", None), P("tp"), P("tp"),
        P("tp"), P(None, "tp"), P("tp"), P("tp", None), P("tp"), P(), P("win"), P("win", "tp"),
    )
    out_specs = (
        P("win", "tp"), P(("win", "tp"), None, None, None), P("tp"), P("tp"), P("tp", "win"),
        P("tp"), P("tp"), P("win", None, "tp"), P(None, "tp"), P(None, "tp"), P("tp", "win"),
        P("tp"), P("tp"), P("tp"), P("win", "tp"), P("tp"), P("tp", "win"), P("tp"),
    )
    return jax.shard_map(shards, mesh=mesh, in_specs=in_specs, out_specs=out_specs, check_vma=False)
```

time: 1000 us -> 217 us (0.22)
  waiting for transfers between devices: 606 us -> 0 us
  Pallas kernels: 0 us -> 211 us
  matrix products: 143 us -> 0 us
  blocking collectives: 106 us -> 0 us
  local copies, waits for them, and re-layouts: 76.1 us -> 4.34 us
  other arithmetic: 47.2 us -> 0 us
  between operations: 14.7 us -> 0.86 us
    reduce_scatter x10 -> x0, waiting for transfers between devices: 583 us -> none  [the longest x1 183 us: shards(): lax.psum_scatter(fc1_weight_grad, 'win', scatter_dimension=0, tiled=True)]
    pallas_call x0 -> x3, Pallas kernels: none -> 211 us  [the longest x2 206 us: kernel_call(): pl.pallas_call(run, out_shape=tuple(outs.values()), in_specs=[vmem] * len...]
    dot_general x23 -> x0, matrix products: 143 us -> none  [the longest x5 43.4 us: times_transposed(): lax.dot_general(left, right, (((1,), (1,)), ((), ())), preferred_element_...]
    psum x7 -> x0, blocking collectives: 94.4 us -> none  [the longest x1 79.4 us: shards(): lax.psum((merge_gain_grad, merge_shift_grad, norm1_gain_grad, norm1_shift...]
    reduce_sum x10 -> x0, other arithmetic: 24.7 us -> none  [the longest x2 5.13 us: norm_grads(): return (scaled, local, jnp.sum(grad * centred, 0), jnp.sum(grad, 0))]
    all_gather x5 -> x0, waiting for transfers between devices: 23.4 us -> none  [the longest x3 15.2 us: gather_grad(): return lax.all_gather(grad_low, 'tp', axis=1, tiled=True)]
    convert_element_type x6 -> x0, local copies, waits for them, and re-layouts: 22.5 us -> none  [the longest x2 11.4 us: shards(): g_qkv = jnp.stack([d_query, d_key, d_value], 2).reshape(tokens, 3 * local...]
    reshape x6 -> x3, local copies, waits for them, and re-layouts: 24.3 us -> 2.79 us  [the longest x1 1.36 us: shards(): kept = keep.reshape(2, 1, wins * area)]
  transfers between devices with their start and end apart: 15 -> 0, of which waited for: 11 -> 0; matrix products, arithmetic and copies ran while one was open for 11% -> 0% of each run, Pallas kernels for 0% -> 0%
where the time goes in v3:
time: 217 us; the launch traced here: 216 us
  Pallas kernels  211 us (97%)
  local copies, waits for them, and re-layouts  4.34 us (2%)
    pallas_call x2, Pallas kernels, kernel_call(): pl.pallas_call(run, out_shape=tuple(outs.values()), in_specs=[vmem] * len...  206 us
    pallas_call x1, Pallas kernels, hand_on(): pl.pallas_call(run, out_shape=tuple((shape(a.shape, a.dtype) for a in arr...  5.05 us

profile of v3, /device:TPU:0, one launch (start us, length us, event | category | flops | bytes accessed | tf_op | source)
XLA Modules:
  0.0 216.3 jit_solution(17486887014197309170)
XLA Ops:
  0.7 1.4 reshape.116.refs_10_
  2.0 0.8 reshape.105
  2.8 0.7 reshape.106.refs_0_
  3.5 0.9 copy.38
  4.4 0.6 pad.9.refs_9_.refs_6_
  5.0 31.1 %shard_map.331 = (bf16[4,448,512]{2,1,0:T(8,128)(2,1)}, bf16[896,1024]{1,0:T(8,128)(2,1)}, f32[448,1024]{1,0:T(8,128)}, f32[448,1024]{1,0:T(8,128)}, bf16[448,10...) custom-call(f32[1,1024]{1,0:T(1,128)} %bitcast.38, ...), custom_call_target="tpu_custom_call" | custom-call | tf_op jit(solution)/shard_map/pallas_call | solution.py:30
  36.1 175.0 %shard_map.332 = (bf16[800,512]{1,0:T(8,128)(2,1)}, f32[10,2,10,2,4,512]{5,4,3,2,1,0:T(4,128)}, f32[1,1024]{1,0:T(1,128)}, f32[1,1024]{1,0:T(1,128)}, f32[1,512]...) custom-call(s32[2,1,448]{2,1,0:T(1,128)} %reshape.106.refs_0_, ...), custom_call_target="tpu_custom_call" | custom-call | tf_op jit(solution)/shard_map/pallas_call | solution.py:30
  211.1 5.1 %shard_map.333 = (bf16[800,512]{1,0:T(8,128)(2,1)}, f32[10,2,10,2,4,512]{5,4,3,2,1,0:T(4,128)}, f32[1,1024]{1,0:T(1,128)}, f32[1,1024]{1,0:T(1,128)}, f32[1,512]...) custom-call(bf16[800,512]{1,0:T(8,128)(2,1)} %get-tuple-element.94.r, ...), custom_call_target="tpu_custom_call" | custom-call | tf_op jit(solution)/shard_map/pallas_call | solution.py:1068
  (1 shorter events, 0.0 us)

commit v4 on v3

--- a/solution.py
+++ b/solution.py
@@ -253,11 +253,10 @@
     )
 
 
-def rel_sum(area, heads, index, sums, rel):
+def rel_sum(first, last, heads, index, sums, rel):
     entries = rel.shape[1]
-    rel[...] = jnp.zeros_like(rel)
-
-    @pl.loop(0, area // PAIRS)
+
+    @pl.loop(first, last)
     def _(i):
         hot = onehot_of(index, i * PAIRS, entries)
         s = jnp.concatenate(
@@ -273,141 +272,83 @@
         rel[...] += both[:heads] + both[heads:]
 
 
-def win_sizes(count):
+def win_bits(count):
+    total = count.bit_length() - 1
     side = 1
     while 4 * (side + 1) * (side + 1) <= count:
         side += 1
-    return count // (side * side), side, side
-
-
-def my_place(sizes):
-    me = lax.axis_index("win")
-    _, ny, nx = sizes
-    return lax.div(me, ny * nx), lax.rem(lax.div(me, nx), ny), lax.rem(me, nx)
-
-
-def wins_along(sizes, place, axis):
-    z, y, x = place
-    strides = (sizes[1] * sizes[2], sizes[2], 1)
-    base = z * strides[0] + y * strides[1] + x
-    found = []
-    for d in range(1, sizes[axis]):
-        c = lax.rem(place[axis] + d, sizes[axis])
-        found.append((d, c, base + (c - place[axis]) * strides[axis]))
-    return found
-
-
-def enter(sizes=None, place=None):
+    wide = side.bit_length() - 1
+    axes = [range(wide), range(wide, 2 * wide), range(2 * wide, total)]
+    near = [axis[0] for axis in axes if len(axis)]
+    far = [bit for axis in axes for bit in axis[1:]]
+    return near, far
+
+
+def orders_of(count, n_units):
+    near, far = win_bits(count)
+    x, y, z = near
+    turns = [(x, y, z), (y, x, z), (z, x, y), (x, z, y), (y, z, x), (z, y, x)]
+    later = [(x, y, z), (y, x, z), (z, x, y), (x, y, z), (y, x, z), (z, y, x)]
+    return [(*(turns if u < 6 else later)[u % 6], *far) for u in range(n_units)]
+
+
+def my_bit(bit):
+    return lax.rem(lax.div(lax.axis_index("win"), 1 << bit), 2)
+
+
+def partner(bit):
+    return lax.axis_index("win") + (1 - 2 * my_bit(bit)) * (1 << bit), lax.axis_index("tp")
+
+
+def enter(bits):
     barrier = pltpu.get_barrier_semaphore()
-    tp = lax.axis_index("tp")
-    peers = [(lax.axis_index("win"), 1 - tp)]
-    if sizes is not None:
-        for axis in range(3):
-            peers += [(w, tp) for _, _, w in wins_along(sizes, place, axis)]
+    peers = [(lax.axis_index("win"), 1 - lax.axis_index("tp"))]
+    peers += [partner(bit) for bit in range(bits)]
     for peer in peers:
         pl.semaphore_signal(barrier, inc=1, device_id=peer, device_id_type=MESH)
     pl.semaphore_wait(barrier, len(peers))
 
 
 class Scatter:
-    def __init__(self, sizes, place, order, src, bufs, sends, recvs, unit):
-        self.sizes, self.place, self.order = sizes, place, order
-        self.src, self.bufs, self.sends, self.recvs, self.unit = src, bufs, sends, recvs, unit
-
-    def pick(self, step, c):
-        if step == 0:
-            return self.src.at[:, :, c] if self.order[0] == 2 else self.src.at[:, c]
-        before = self.bufs[step - 1].at[0]
-        if step == 1:
-            return before.at[:, c]
-        return before.at[c]
-
-    def copies(self, step):
-        axis = self.order[step]
-        tp = lax.axis_index("tp")
-        made = []
-        for d, c, w in wins_along(self.sizes, self.place, axis):
-            made.append(
-                pltpu.make_async_remote_copy(
-                    src_ref=self.pick(step, c),
-                    dst_ref=self.bufs[step].at[d - 1],
-                    send_sem=self.sends.at[self.unit, step, d - 1],
-                    recv_sem=self.recvs.at[self.unit, step, d - 1],
-                    device_id=(w, tp),
-                    device_id_type=MESH,
-                )
-            )
-        return made
-
-    def start(self, step):
-        for copy in self.copies(step):
-            copy.start()
-
-    def wait_sent(self, step):
-        for copy in self.copies(step):
-            copy.wait_send()
+    def __init__(self, order, src, bufs, sends, recvs, unit):
+        self.order, self.held = order, [src, *bufs]
+        self.sends, self.recvs, self.unit = sends, recvs, unit
+
+    def pick(self, step, value):
+        left = [b for b in range(len(self.order)) if b not in self.order[:step]]
+        dim = len(left) - 1 - left.index(self.order[step])
+        return self.held[step].at[(*([slice(None)] * dim), value)]
+
+    def copy(self, step):
+        bit = self.order[step]
+        return pltpu.make_async_remote_copy(
+            src_ref=self.pick(step, 1 - my_bit(bit)),
+            dst_ref=self.held[step + 1],
+            send_sem=self.sends.at[self.unit, step],
+            recv_sem=self.recvs.at[self.unit, step],
+            device_id=partner(bit),
+            device_id_type=MESH,
+        )
 
     def finish(self, step, out=None):
-        copies = self.copies(step)
-        for copy in copies:
-            copy.wait_recv()
-        mine = self.pick(step, self.place[self.order[step]])
-        buf = self.bufs[step]
-        lead = mine.shape[:-2]
-        rows, n = mine.shape[-2:]
-        width = min(n, 512)
-        if step == 2:
-            for b in range(n // width):
-                at = pl.ds(b * width, width)
-                total = mine[:, at].astype(F32)
-                for d in range(len(copies)):
-                    total += buf[d, :, at].astype(F32)
-                out[:, at] = total
+        self.copy(step).wait_recv()
+        mine = self.pick(step, my_bit(self.order[step]))
+        got = self.held[step + 1]
+        lead = got.shape[:-2]
+        if not lead:
+            out[...] = mine[...].astype(F32) + got[...].astype(F32)
             return
-        count = 1
-        for size in lead:
-            count *= size
-
-        @pl.loop(0, count)
+
+        @pl.loop(0, 1 << len(lead))
         def _(i):
-            where = (i,) if len(lead) == 1 else (lax.div(i, lead[1]), lax.rem(i, lead[1]))
-            for b in range(n // width):
-                at = pl.ds(b * width, width)
-                total = mine[(*where, slice(None), at)].astype(F32)
-                for d in range(len(copies)):
-                    total += buf[(d, *where, slice(None), at)].astype(F32)
-                buf[(0, *where, slice(None), at)] = total.astype(BF16)
-
-
-X_FIRST, Y_FIRST = (2, 1, 0), (1, 2, 0)
-
-
-def all_sum(sizes, place, src, bufs, sends, recvs):
-    tp = lax.axis_index("tp")
-    for step, axis in enumerate((2, 1, 0)):
-        copies = []
-        for d, c, w in wins_along(sizes, place, axis):
-            copies.append(
-                pltpu.make_async_remote_copy(
-                    src_ref=src.at[step],
-                    dst_ref=bufs.at[step, d - 1],
-                    send_sem=sends.at[step, d - 1],
-                    recv_sem=recvs.at[step, d - 1],
-                    device_id=(w, tp),
-                    device_id_type=MESH,
-                )
-            )
-        for copy in copies:
-            copy.start()
-        total = src[step]
-        for d, copy in enumerate(copies):
-            copy.wait()
-            total += bufs[step, d]
-        src[step + 1] = total
+            at = tuple(lax.rem(lax.div(i, 1 << k), 2) for k in reversed(range(len(lead))))
+            got[at] = (mine[at].astype(F32) + got[at].astype(F32)).astype(BF16)
+
+        self.copy(step + 1).start()
 
 
 def front_body(dim, heads, area, r):
-    enter()
+    enter(0)
     t = lax.axis_index("tp")
     who = (t, 1 - t)
     rows, model = r.firstb.shape
@@ -625,10 +566,42 @@
 
 
 CHUNK = 512
-
-
-def back_body(sizes, dim, heads, area, r):
-    place = my_place(sizes)
+PLAN = {
+    2: ((0, 0), (1, 0)),
+    3: ((2, 0),),
+    7: ((3, 0),),
+    9: ((4, 0),),
+    11: ((1, 1),),
+    12: ((5, 0),),
+    13: ((0, 1),),
+    15: ((3, 1),),
+    17: ((6, 0),),
+    19: ((4, 1),),
+    20: ((7, 0), (1, 2)),
+    21: ((2, 1),),
+    25: ((5, 1), (4, 2)),
+    27: ((3, 2),),
+    29: ((7, 1), (8, 0)),
+    30: ((6, 1), (5, 2)),
+    31: ((0, 2),),
+    32: ((2, 2),),
+    33: ((1, 3),),
+    34: ((4, 3), (3, 3)),
+    35: ((7, 2), (9, 0)),
+    36: ((10, 0),),
+    37: ((8, 1),),
+    40: (
+        (11, 0), (6, 2), (-1, 0), (13, 0), (5, 3), (-1, 1),
+        (12, 0), (0, 3), (-1, 2), (9, 1), (2, 3), (-1, 3),
+        (8, 2), (10, 1), (-1, 4), (7, 3), (6, 3), (11, 1),
+        (13, 1), (9, 2), (8, 3), (11, 2), (10, 2), (12, 1),
+        (13, 2), (9, 3), (11, 3), (10, 3), (12, 2), (13, 3),
+        (12, 3),
+    ),
+}
+
+
+def back_body(bits, orders, dim, heads, area, r):
     t = lax.axis_index("tp")
     who = (t, 1 - t)
     sec, gf, facc, gacc, st, ex = r.sec, r.gfb, r.facc, r.gacc, r.st, r.ex
@@ -644,28 +617,70 @@
     link = Link(r.xsend, r.xrecv)
     own_cols = pl.ds(pl.multiple_of(t * half, half), half)
     oth_cols = pl.ds(pl.multiple_of((1 - t) * half, half), half)
-    part = model // (sizes[0] * sizes[1] * sizes[2])
+    part = model // (1 << bits)
 
     def load(k, src, dst):
         return pltpu.make_async_copy(src, dst, r.lsem.at[k])
 
-    def unit(u, order):
-        slot = u % 8 if isinstance(u, int) else lax.rem(u, 8)
-        bufs = [buf.at[u] for buf in (r.buf0, r.buf1, r.buf2)]
-        return Scatter(sizes, place, order, r.src.at[slot], bufs, r.rsend, r.rrecv, u)
-
-    def pair(k):
-        return unit(2 * k, X_FIRST), unit(2 * k + 1, Y_FIRST)
-
-    def finish(k, step):
-        for one in pair(k):
-            one.finish(step)
-            one.start(step + 1)
-
-    def put(slot, value):
-        r.src[slot] = value.astype(BF16).reshape(*sizes, part, CHUNK)
-
-    enter(sizes, place)
+    def unit(u):
+        bufs = [buf.at[u] for buf in r.bufs]
+        return Scatter(orders[u], r.src.at[u % 8], bufs, r.rsend, r.rrecv, u)
+
+    def put(u, value):
+        if u >= 8:
+            unit(u - 8).copy(0).wait_send()
+        r.src[u % 8] = value.astype(BF16).reshape(*([2] * bits), part, CHUNK)
+        unit(u).copy(0).start()
+
+    def held(u):
+        return st.at[u // 2 * part : (u // 2 + 1) * part, (left, right)[u % 2]]
+
+    def result(u):
+        if u < 2 * chunks:
+            return (r.o_fc1, r.o_fc2)[u % 2].at[:, pl.ds(u // 2 * CHUNK, CHUNK)]
+        u -= 2 * chunks
+        if u == 0:
+            return r.o_proj
+        if u < 4:
+            return r.o_qkv.at[u - 1]
+        return r.o_merge.at[:, (left, right)[u - 4]]
+
+    last_step = bits - 1
+    copies = [
+        pltpu.make_async_remote_copy(
+            src_ref=r.vs.at[bit],
+            dst_ref=r.vbuf.at[bit],
+            send_sem=r.vsend.at[bit],
+            recv_sem=r.vrecv.at[bit],
+            device_id=partner(bit),
+            device_id_type=MESH,
+        )
+        for bit in range(bits)
+    ]
+
+    def vectors(step):
+        if step == 0:
+            link.copy(6, r.vx.at[0], r.vx.at[1]).wait()
+            r.vs[0] += r.vx[1]
+        else:
+            copies[step - 1].wait()
+            r.vs[step] = r.vs[step - 1] + r.vbuf[step - 1]
+        if step < bits:
+            copies[step].start()
+
+    def pump(place):
+        for u, step in PLAN.get(place, ()):
+            if u < 0:
+                vectors(step)
+                continue
+            unit(u).finish(step, held(u))
+            if step == last_step:
+                write(u).start()
+
+    def write(u):
+        return pltpu.make_async_copy(held(u), result(u), r.osem.at[u])
+
+    enter(bits)
     c_sec = link.copy(0, r.second, sec.at[theirs])
     c_sec.start()
     loads = [
@@ -723,10 +738,19 @@
 
             steps(2 * rows, 128, gelu)
         r.gb1[:, of] = jnp.sum(gh[...].astype(F32), 0, keepdims=True)
-        put(lax.rem(2 * c, 8), dot_tn(sec[...], gh[...]))
-        unit(2 * c, X_FIRST).start(0)
-        put(lax.rem(2 * c + 1, 8), dot_tn(gf[...], act[...]))
-        unit(2 * c + 1, Y_FIRST).start(0)
+        for k, value in enumerate((dot_tn(sec[...], gh[...]), dot_tn(gf[...], act[...]))):
+            r.src[2 * c + k] = value.astype(BF16).reshape(*([2] * bits), part, CHUNK)
+            for j in range(chunks):
+
+                @pl.when(c == j)
+                def _():
+                    unit(2 * j + k).copy(0).start()
+
+        for j in range(chunks):
+
+            @pl.when(c == j)
+            def _():
+                pump(j)
 
         @pl.when(c == 0)
         def _():
@@ -738,22 +762,37 @@
             facc[...] += dot(act[...], w2b[slot])
             gacc[...] += dot_nt(gh[...], w1b[slot])
 
-        @pl.when(c >= 2)
-        def _():
-            finish(c - 2, 0)
+        for j in range(chunks):
+
+            @pl.when(c == j)
+            def _():
+                pump(chunks + j)
 
     load(5, r.bias, r.biasb).start()
+    load(6, r.att_own, act.at[mine]).start()
+    load(7, r.att_sib, act.at[theirs]).start()
     for k, src in enumerate((r.wp_own, r.wp_oth)):
         load(8 + k, src, w2b.at[k]).start()
     ex[0] = gacc[theirs].astype(BF16)
     c_g2 = link.copy(1, ex.at[0], ex.at[1])
     c_g2.start()
     load(3, r.stream1, st).wait()
-    fsend, fland = r.fsend, r.fland
-    fsend[0] = facc[theirs, oth_cols].astype(BF16)
-    fsend[1] = (facc[mine, oth_cols] + st[:, oth_cols]).astype(BF16)
-    c_feed = link.copy(2, fsend, fland)
-    c_feed.start()
+    fsend, fland = gh, cotb.at[pl.ds(3, 2)]
+    fsend[mine, :] = facc[theirs, oth_cols].astype(BF16)
+    fsend[theirs, :] = (facc[mine, oth_cols] + st[:, oth_cols]).astype(BF16)
+    c_feed = [
+        link.copy(k, fsend.at[(mine, theirs)[k - 7]], fland.at[k - 7]) for k in (7, 8)
+    ]
+    for one in c_feed:
+        one.start()
+
+    def fold(at):
+        own = facc[at, own_cols] + st[at, own_cols]
+        oth = facc[pl.ds(pl.multiple_of(rows + at.start, 16), at.size), own_cols]
+        facc[at, left] = own
+        facc[at, right] = oth
+
+    pump(8)
     v2 = r.v2
     v2[...] = jnp.zeros_like(v2)
     c_g2.wait()
@@ -774,26 +813,26 @@
     c_att.start()
     load(10, r.first_own, gf.at[mine]).start()
     load(11, r.first_sib, gf.at[theirs]).start()
+    pump(9)
+    steps(rows, 112, fold)
+    pump(10)
     for k, src in enumerate((r.wp_own, r.wp_oth)):
         load(8 + k, src, w2b.at[k]).wait()
         ex[0, :, (left, right)[k]] = dot_nt(sec[mine, :], w2b[k]).astype(BF16)
 
-    c_feed.wait()
-    token_rows = gather_rows(rows, tokens, windows)[0]
-    outs = []
-    for side in range(2):
-        value = facc[side * rows : (side + 1) * rows, own_cols] + fland[side].astype(F32)
-        if side == 0:
-            value += st[:, own_cols]
-        pick = ones(jnp.logical_and(token_rows, r.keep[who[side]] > 0))
-        fsend[side, 0:tokens, :] = dot(pick, (value + r.b2[...]).astype(BF16)).astype(BF16)
-        at = pl.ds(pl.multiple_of(who[side] * tokens, tokens), tokens)
-        outs.append(load(14 + side, fsend.at[side, pl.ds(0, tokens), :], r.out.at[at, :]))
-        outs[-1].start()
-    load(6, r.att_own, fland.at[0]).start()
-    load(7, r.att_sib, fland.at[1]).start()
-    load(12, r.stream0, st).start()
-
+    pump(11)
+
+    first_unit = 2 * chunks
+    u_proj, u_qkv = first_unit, first_unit + 1
+    u_merge = first_unit + 4
+    load(6, r.att_own, act.at[mine]).wait()
+    load(7, r.att_sib, act.at[theirs]).wait()
+    c_att.wait()
+    put(u_proj, dot_tn(sec[...], act[...]))
+    pump(12)
+
+    s0 = facc.at[theirs]
+    load(12, r.stream0, s0).start()
     load(4, r.qkv, qkvb).wait()
     load(5, r.bias, r.biasb).wait()
 
@@ -801,13 +840,11 @@
     def _(g):
         attention_back(dim, heads, g, r)
 
-        @pl.when(lax.rem(g, 4) == 0)
-        def _():
-            finish(chunks - 2 + lax.div(g, 4), 0)
-
-        @pl.when(lax.rem(g, 2) == 1)
-        def _():
-            finish(lax.div(g, 2), 1)
+        for k in range(8):
+
+            @pl.when(g == k)
+            def _():
+                pump(13 + k)
 
     dland = cotb.at[pl.ds(0, 3)]
     c_qkv = link.copy(4, qkvb.at[:, :, right], dland)
@@ -817,20 +854,6 @@
         return (r.wqkv_own, r.wqkv_oth)[k // 3].at[k % 3]
 
     load(16, slice_of(0), w1b.at[0]).start()
-
-    first_unit = 2 * chunks
-
-    def free(u):
-        unit(u - 8, X_FIRST if u % 2 == 0 else Y_FIRST).wait_sent(0)
-
-    u_qkv = [first_unit, first_unit + 1, first_unit + 2]
-    u_proj, u_merge = first_unit + 3, [first_unit + 4, first_unit + 5]
-    c_att.wait()
-    load(6, r.att_own, fland.at[0]).wait()
-    load(7, r.att_sib, fland.at[1]).wait()
-    free(u_proj)
-    put(u_proj % 8, dot_tn(sec[mine, :], fland[0]) + dot_tn(sec[theirs, :], fland[1]))
-    unit(u_proj, Y_FIRST).start(0)
 
     for k in range(6):
         load(16 + k % 2, slice_of(k), w1b.at[k % 2]).wait()
@@ -838,16 +861,17 @@
             load(16 + (k + 1) % 2, slice_of(k + 1), w1b.at[(k + 1) % 2]).start()
         value = dot_nt(qkvb[k % 3, :, (left, right)[k // 3]], w1b[k % 2])
         if k == 0:
-            facc[theirs, :] = value
+            gacc[theirs, :] = value
         else:
-            facc[theirs, :] += value
-    load(12, r.stream0, st).wait()
+            gacc[theirs, :] += value
+        pump(21 + k)
+    load(12, r.stream0, s0).wait()
     v1 = r.v1
     v1[...] = jnp.zeros_like(v1)
 
     def norm1(at):
-        e = facc[pl.ds(pl.multiple_of(rows + at.start, 16), at.size), :]
-        dv, hat = norm_back(e, st[at, :], r.nat[0:1, :], model)
+        e = gacc[pl.ds(pl.multiple_of(rows + at.start, 16), at.size), :]
+        dv, hat = norm_back(e, s0[at, :], r.nat[0:1, :], model)
         sec[at, :] = (gacc[at, :] + dv).astype(BF16)
         add_to(v1, 0, hat)
         add_to(v1, 1, e)
@@ -861,11 +885,10 @@
     for k in range(2):
         load(8 + k, r.wm_own.at[(left, right)[k], :], w2b.at[k]).start()
     c_qkv.wait()
+    pump(27)
     for s in range(3):
-        free(u_qkv[s])
-        put(u_qkv[s] % 8, dot_tn(gf[mine, :], qkvb[s, :, left]) + dot_tn(gf[theirs, :], dland[s]))
-        unit(u_qkv[s], X_FIRST if s % 2 == 0 else Y_FIRST).start(0)
-    load(1, r.x, cotb).start()
+        put(u_qkv + s, dot_tn(gf[mine, :], qkvb[s, :, left]) + dot_tn(gf[theirs, :], dland[s]))
+        pump(28 + s)
     load(10, r.mn_own, gf.at[mine]).start()
     load(11, r.mn_sib, gf.at[theirs]).start()
 
@@ -874,17 +897,27 @@
     load(11, r.mn_sib, gf.at[theirs]).wait()
     for k in range(2):
         cols = (left, right)[k]
-        free(u_merge[k])
-        put(u_merge[k] % 8, dot_tn(sec[mine, :], gf[mine, cols]) + dot_tn(ex[1], gf[theirs, cols]))
-        unit(u_merge[k], (X_FIRST, Y_FIRST)[k]).start(0)
-    last = chunks + 2
-    finish(chunks + 1, 0)
-    finish(chunks, 0)
-
-    rel_sum(area, heads, r.index, r.sums, r.rel)
-    finish(chunks + 1, 1)
-    finish(chunks, 1)
-    finish(last, 0)
+        put(u_merge + k, dot_tn(sec[mine, :], gf[mine, cols]) + dot_tn(ex[1], gf[theirs, cols]))
+        pump(31 + k)
+
+    for one in c_feed:
+        one.wait()
+    token_rows = gather_rows(rows, tokens, windows)[0]
+    outs = []
+    for side in range(2):
+        value = facc[mine, (left, right)[side]] + fland[side].astype(F32)
+        pick = ones(jnp.logical_and(token_rows, r.keep[who[side]] > 0))
+        fsend[side * rows : side * rows + tokens, :] = dot(pick, (value + r.b2[...]).astype(BF16)).astype(BF16)
+        at = pl.ds(pl.multiple_of(who[side] * tokens, tokens), tokens)
+        outs.append(load(14 + side, fsend.at[pl.ds(side * rows, tokens), :], r.out.at[at, :]))
+        outs[-1].start()
+    load(1, r.x, cotb.at[pl.ds(0, 4)]).start()
+    pump(33)
+
+    r.rel[...] = jnp.zeros_like(r.rel)
+    for k in range(2):
+        rel_sum(k * 12, (area // PAIRS if k else 12), heads, r.index, r.sums, r.rel)
+        pump(34 + k)
 
     for k in range(4):
         load(8 + k % 2, (r.wm_own, r.wm_oth)[k // 2].at[(left, right)[k % 2], :],
@@ -894,7 +927,8 @@
         )
         if k < 2:
             load(8 + k, r.wm_oth.at[(left, right)[k], :], w2b.at[k]).start()
-    load(1, r.x, cotb).wait()
+    pump(36)
+    load(1, r.x, cotb.at[pl.ds(0, 4)]).wait()
     v0 = r.v0
     v0[...] = jnp.zeros_like(v0)
     width = 2 * model
@@ -926,7 +960,7 @@
                 v0[2 * i + 1 : 2 * i + 2, cols(j)] += jnp.sum(es[i][j], 0, keepdims=True)
 
     steps(rows, 64, norm0)
-    finish(last, 1)
+    pump(37)
 
     vs, vx = r.vs, r.vx
     heads_here = heads // 2
@@ -948,22 +982,21 @@
         dst[16 : 16 + heads_here, 0 : r.rel.shape[1]] = r.rel[
             side * heads_here : (side + 1) * heads_here, :
         ]
-    c_vec = link.copy(6, vx.at[0], vx.at[1])
-    c_vec.start()
-
+    link.copy(6, vx.at[0], vx.at[1]).start()
+    pump(38)
+
+    outs[0].wait()
     pixel_rows = ones(gather_rows(rows, tokens, windows)[1])
     for b in range(2):
         for a in range(2):
             value = dot(pixel_rows, qkvb[b, :, (left, right)[a]])
-            if b == 1:
-                outs[2 + a].wait()
-            r.pix[a] = value.reshape(*r.pix.shape[1:])
-            outs.append(load(2 * b + a, r.pix.at[a], r.pixels_grad.at[:, a, :, who[b]]))
+            outs[-1].wait()
+            r.pix[...] = value.reshape(*r.pix.shape)
+            outs.append(load(2 * b + a, r.pix, r.pixels_grad.at[:, a, :, who[b]]))
             outs[-1].start()
-    c_vec.wait()
-    vs[0] += vx[1]
-    all_sum(sizes, place, vs, r.vbuf, r.vsend, r.vrecv)
-    v = vs.at[3]
+    pump(39)
+    pump(40)
+    v = vs.at[bits]
     for i in range(2):
         for j in range(2):
             (r.o_mg, r.o_ms)[i][:, j * half : (j + 1) * half] = v[2 * i + j : 2 * i + j + 1, :]
@@ -976,26 +1009,16 @@
         r.o_b1[:, j * half : (j + 1) * half] = v[12 + j : 13 + j, :]
     r.o_rel[...] = v[16 : 16 + heads_here, 0 : r.o_rel.shape[1]]
 
-    for k in range(chunks):
-        at = pl.ds(k * CHUNK, CHUNK)
-        unit(2 * k, X_FIRST).finish(2, r.o_fc1.at[:, at])
-        unit(2 * k + 1, Y_FIRST).finish(2, r.o_fc2.at[:, at])
-    for s in range(3):
-        unit(u_qkv[s], X_FIRST if s % 2 == 0 else Y_FIRST).finish(2, r.o_qkv.at[s])
-    unit(u_proj, Y_FIRST).finish(2, r.o_proj)
-    for k in range(2):
-        unit(u_merge[k], (X_FIRST, Y_FIRST)[k]).finish(2, r.o_merge.at[:, (left, right)[k]])
-    for one in outs[:2] + outs[4:]:
-        one.wait()
+    outs[-1].wait()
     for u in range(first_unit + 6):
-        one = unit(u, X_FIRST if u % 2 == 0 else Y_FIRST)
-        for step in range(3):
+        write(u).wait()
+        for step in range(bits):
             if step > 0 or u >= first_unit + 6 - 8:
-                one.wait_sent(step)
+                unit(u).copy(step).wait_send()
 
 
 def back(count, dim, heads, area, windows, entries, small, large):
-    sizes = win_sizes(count)
+    bits = count.bit_length() - 1
     rows, tokens = windows * PAD, windows * area
     hidden = large["fc1"].shape[1]
     model = large["fc1"].shape[0]
@@ -1004,19 +1027,18 @@
     slots = -(-entries // 128) * 128
     n_units = 2 * (hidden // CHUNK) + 6
     part = model // count
-    most = max(sizes) - 1
-    nz, ny, nx = sizes
+    orders = orders_of(count, n_units)
     big = dict(
         out=shape((2 * tokens, half), BF16),
         pixels_grad=shape((side, 2, side, 2, windows, half)),
+        o_fc1=shape((part, hidden)), o_fc2=shape((part, hidden)), o_qkv=shape((3, part, half)),
+        o_proj=shape((part, half)), o_merge=shape((part, model)),
     )
     outs = dict(
         big, o_mg=shape((1, model)), o_ms=shape((1, model)),
         o_n1g=shape((1, half)), o_n1s=shape((1, half)), o_qb=shape((2, half)),
         o_n2g=shape((1, half)), o_n2s=shape((1, half)), o_pb=shape((1, half)),
         o_b1=shape((1, hidden)), o_b2=shape((1, half)), o_rel=shape((heads // 2, entries)),
-        o_fc1=shape((part, hidden)), o_fc2=shape((part, hidden)), o_qkv=shape((3, part, half)),
-        o_proj=shape((part, half)), o_merge=shape((part, model)),
     )
     vm, dma = pltpu.VMEM, pltpu.SemaphoreType.DMA
     scratch = dict(
@@ -1024,25 +1046,22 @@
         facc=vm((2 * rows, model), F32), gacc=vm((2 * rows, model), F32),
         st=vm((rows, model), F32), ex=vm((2, rows, model), BF16),
         w1b=vm((2, model, CHUNK), BF16), w2b=vm((2, CHUNK, model), BF16),
-        cotb=vm((4, rows, half), BF16), qkvb=vm((3, rows, model), BF16),
+        cotb=vm((5, rows, half), BF16), qkvb=vm((3, rows, model), BF16),
         biasb=vm((PAD * heads, 128), F32), sums=vm((PAD * heads, 128), F32),
         act=vm((2 * rows, CHUNK), BF16), gh=vm((2 * rows, CHUNK), BF16),
-        fsend=vm((2, rows, half), BF16), fland=vm((2, rows, half), BF16),
-        pix=vm((2, side, side, windows, half), F32),
-        src=vm((8, nz, ny, nx, part, CHUNK), BF16),
-        buf0=vm((n_units, nx - 1, nz, ny, part, CHUNK), BF16),
-        buf1=vm((n_units, ny - 1, nz, part, CHUNK), BF16),
-        buf2=vm((n_units, nz - 1, part, CHUNK), BF16),
+        pix=vm((side, side, windows, half), F32),
+        src=vm((8, *([2] * bits), part, CHUNK), BF16),
+        bufs=[vm((n_units, *([2] * k), part, CHUNK), BF16) for k in reversed(range(bits))],
         v0=vm((4, model), F32), v1=vm((2, model), F32), v2=vm((3, model), F32),
         vq=vm((2, model), F32), rel=vm((heads, slots), F32), gb1=vm((1, hidden), F32),
-        vs=vm((4, 32, half), F32), vx=vm((2, 32, half), F32), vbuf=vm((3, most, 32, half), F32),
-        lsem=dma((18,)), wsem=dma((2, 2)), xsend=dma((8,)), xrecv=dma((8,)),
-        rsend=dma((n_units, 3, most)), rrecv=dma((n_units, 3, most)),
-        vsend=dma((3, most)), vrecv=dma((3, most)),
+        vs=vm((bits + 1, 32, half), F32), vx=vm((2, 32, half), F32), vbuf=vm((bits, 32, half), F32),
+        lsem=dma((18,)), wsem=dma((2, 2)), xsend=dma((9,)), xrecv=dma((9,)), osem=dma((n_units,)),
+        rsend=dma((n_units, bits)), rrecv=dma((n_units, bits)),
+        vsend=dma((bits,)), vrecv=dma((bits,)),
     )
 
     def body(r):
-        back_body(sizes, dim, heads, area, r)
+        back_body(bits, orders, dim, heads, area, r)
 
     return kernel_call(body, small, large, outs, scratch, big, collective=1)
 

time: 217 us -> 187 us (0.86)
  Pallas kernels: 211 us -> 181 us
    pallas_call x2, Pallas kernels: 206 us -> 176 us  [kernel_call(): pl.pallas_call(run, out_shape=tuple(outs.values()), in_specs=[vmem] * len...]
where the time goes in v4:
time: 187 us; the launch traced here: 186 us
  Pallas kernels  181 us (97%)
  local copies, waits for them, and re-layouts  4.34 us (2%)
    pallas_call x2, Pallas kernels, kernel_call(): pl.pallas_call(run, out_shape=tuple(outs.values()), in_specs=[vmem] * len...  176 us
    pallas_call x1, Pallas kernels, hand_on(): pl.pallas_call(run, out_shape=tuple((shape(a.shape, a.dtype) for a in arr...  5.03 us

profile of v4, /device:TPU:0, one launch (start us, length us, event | category | flops | bytes accessed | tf_op | source)
XLA Modules:
  0.0 186.1 jit_solution(17557745158286274312)
XLA Ops:
  0.7 1.4 reshape.116.refs_10_
  2.0 0.8 reshape.105
  2.8 0.7 reshape.106.refs_0_
  3.5 0.9 copy.38
  4.4 0.6 pad.9.refs_9_.refs_6_
  5.0 31.1 %shard_map.331 = (bf16[4,448,512]{2,1,0:T(8,128)(2,1)}, bf16[896,1024]{1,0:T(8,128)(2,1)}, f32[448,1024]{1,0:T(8,128)}, f32[448,1024]{1,0:T(8,128)}, bf16[448,10...) custom-call(f32[1,1024]{1,0:T(1,128)} %bitcast.38, ...), custom_call_target="tpu_custom_call" | custom-call | tf_op jit(solution)/shard_map/pallas_call | solution.py:30
  36.1 144.9 %shard_map.332 = (bf16[800,512]{1,0:T(8,128)(2,1)}, f32[10,2,10,2,4,512]{5,4,3,2,1,0:T(4,128)}, f32[64,2048]{1,0:T(8,128)}, f32[64,2048]{1,0:T(8,128)}, f32[3,64...) custom-call(s32[2,1,448]{2,1,0:T(1,128)} %reshape.106.refs_0_, ...), custom_call_target="tpu_custom_call" | custom-call | tf_op jit(solution)/shard_map/pallas_call | solution.py:30
  180.9 5.0 %shard_map.333 = (bf16[800,512]{1,0:T(8,128)(2,1)}, f32[10,2,10,2,4,512]{5,4,3,2,1,0:T(4,128)}, f32[64,2048]{1,0:T(8,128)}, f32[64,2048]{1,0:T(8,128)}, f32[3,64...) custom-call(bf16[800,512]{1,0:T(8,128)(2,1)} %get-tuple-element.94.r, ...), custom_call_target="tpu_custom_call" | custom-call | tf_op jit(solution)/shard_map/pallas_call | solution.py:1087
  (1 shorter events, 0.0 us)

commit v5 on v4

--- a/solution.py
+++ b/solution.py
@@ -138,7 +138,8 @@
 
 
 def bias_of(bias, heads, g, per):
-    return [bias[pl.ds(g * per + h, PAD, stride=heads), :] for h in range(per)]
+    first = lax.rem(g * per + lax.axis_index("tp") * (heads // 2), heads)
+    return [bias[pl.ds(first + h, PAD, stride=heads), :] for h in range(per)]
 
 
 def attention_forward(dim, heads, g, r):
@@ -157,17 +158,16 @@
             diagonal(q[0], q[1]),
         )
         for u in range(2):
-            vt = v[u].T
             parts = []
             for h in range(per):
                 s = both[h * PAD : (h + 1) * PAD, u * 128 : (u + 1) * 128] * scale + bias[h]
                 top = jnp.max(s, 0, keepdims=True)
                 e = jnp.exp(s - top)
                 total = jnp.sum(e, 0, keepdims=True)
-                p = (e * (1.0 / total)).astype(BF16)
+                parts.append((e * (1.0 / total)).astype(BF16))
                 sums.append(top + jnp.log(total))
-                parts.append(dot(vt[h * dim : (h + 1) * dim], p))
-            done.append(jnp.concatenate(parts, 0).T[:PAD].astype(BF16))
+            value = dot_tn(jnp.concatenate(parts, 0), stacked(v[u], masks))
+            done.append(value[:PAD].astype(BF16))
     for w in range(windows):
         r.attb[pl.ds(w * PAD, PAD), lanes] = done[w]
     r.lse[g] = jnp.concatenate(sums, 0)
@@ -235,22 +235,19 @@
     return jnp.concatenate([ones(ids == row) for row in rows], 1)
 
 
-def bias_spread(area, heads, table, index, out):
+def bias_spread(first, count, heads, table, index, out):
     entries = table.shape[1]
     top = table.astype(BF16)
     both = jnp.concatenate([top, (table - top.astype(F32)).astype(BF16)], 0)
 
-    @pl.loop(0, area // PAIRS)
-    def _(i):
+    @pl.loop(0, count)
+    def _(k):
+        i = first + k
         value = dot(both, onehot_of(index, i * PAIRS, entries))
         value = value[:heads] + value[heads:]
         for u in range(PAIRS):
             at = pl.ds(pl.multiple_of((i * PAIRS + u) * heads, heads), heads)
             out[at, :] = value[:, u * 128 : (u + 1) * 128]
-
-    out[pl.ds(area * heads, (PAD - area) * heads), :] = jnp.full(
-        ((PAD - area) * heads, out.shape[1]), -1e30, F32
-    )
 
 
 def rel_sum(first, last, heads, index, sums, rel):
@@ -284,12 +281,13 @@
     return near, far
 
 
-def orders_of(count, n_units):
+TURNS = (((0,1,2,3),(1,0,2,3),(2,0,1,3),(0,2,1,3),(1,2,0,3),(2,1,0,3),(0,1,2,3),(1,0,2,3),(2,0,1,3),(0,1,2,3),(1,0,2,3),(2,1,0,3),(0,1,2,3),(0,1,2,3),(1,0,2,3),(1,0,2,3)))
+
+
+def orders_of(count):
     near, far = win_bits(count)
-    x, y, z = near
-    turns = [(x, y, z), (y, x, z), (z, x, y), (x, z, y), (y, z, x), (z, y, x)]
-    later = [(x, y, z), (y, x, z), (z, x, y), (x, y, z), (y, x, z), (z, y, x)]
-    return [(*(turns if u < 6 else later)[u % 6], *far) for u in range(n_units)]
+    axes = [*near, *reversed(far)]
+    return [(*[axes[k] for k in turn], *axes[4:]) for turn in TURNS]
 
 
 def my_bit(bit):
@@ -310,8 +308,8 @@
 
 
 class Scatter:
-    def __init__(self, order, src, bufs, sends, recvs, unit):
-        self.order, self.held = order, [src, *bufs]
+    def __init__(self, order, held, sends, recvs, unit):
+        self.order, self.held = order, held
         self.sends, self.recvs, self.unit = sends, recvs, unit
 
     def pick(self, step, value):
@@ -379,12 +377,8 @@
     vx[0, 16 : 16 + heads // 2, 0 : r.table.shape[1]] = r.table[...]
     c_vec = link.copy(1, vx.at[0], vx.at[1])
     c_vec.start()
-    c_cot = link.copy(2, r.cot, r.cotb.at[1])
-    c_cot.start()
     c_wq = link.copy(3, r.wqkv, r.wqb.at[1])
     c_wq.start()
-    c_wp = link.copy(4, r.wp, r.wpb.at[pl.ds(half, half), :])
-    c_wp.start()
     late = [load(6, r.wqkv, r.wqb.at[0]), load(7, r.wp, r.wpb.at[pl.ds(0, half), :])]
     for one in late:
         one.start()
@@ -397,6 +391,14 @@
 
     token_rows, pixel_rows = spread(rows, tokens, windows)
     pixel_rows = ones(pixel_rows)
+    kept = r.keep[...].astype(F32).reshape(1, 2 * tokens)
+    kept = (kept[:, :tokens], kept[:, tokens:])
+    for side in range(2):
+        wide = jnp.broadcast_to(kept[side], (8, tokens)).astype(BF16)
+        r.kept_rows[side] = dot_nt(wide, ones(token_rows))
+    r.square[...] = jnp.zeros_like(r.square)
+    r.square[0:area, 0:area] = r.rel_index[...].astype(F32)
+    r.index[...] = r.square[...].T.astype(jnp.int32)
     for k in range(4):
         loads[k].wait()
         r.xb[k] = dot(
@@ -430,31 +432,28 @@
                 r.mnb[i, at, cols] = value.astype(BF16)
 
     steps(rows, 64, norm0)
+    store(r.mnb.at[0], r.mn_own)
+
+    entries = r.tableb.shape[1]
+    for side in range(2):
+        at = pl.ds(pl.multiple_of(who[side] * (heads // 2), heads // 2), heads // 2)
+        r.tableb[at, :] = vx[side, 16 : 16 + heads // 2, 0:entries]
+    turns = area // PAIRS
+    share = turns // 2 + 1
+    bias_spread(t * (turns - share), share, heads, r.tableb[...], r.index, r.biasb)
+    size = (turns - share) * PAIRS * heads
+    at = pl.ds(pl.multiple_of(t * share * PAIRS * heads, PAIRS * heads), size)
+    c_bias = link.copy(8, r.biasb.at[at, :], r.biasb.at[at, :])
+    c_bias.start()
+    r.biasb[pl.ds(area * heads, (PAD - area) * heads), :] = jnp.full(
+        ((PAD - area) * heads, 128), -1e30, F32
+    )
+    c_cot = link.copy(2, r.cot, r.cotb.at[1])
+    c_cot.start()
+    c_wp = link.copy(4, r.wp, r.wpb.at[pl.ds(half, half), :])
+    c_wp.start()
     c_mn = link.copy(6, r.mnb.at[1], r.mn_sib)
     c_mn.start()
-    store(r.mnb.at[0], r.mn_own)
-
-    entries = r.tableb.shape[1]
-    for side in range(2):
-        r.tableb[side * (heads // 2) : (side + 1) * (heads // 2), :] = vx[
-            side, 16 : 16 + heads // 2, 0:entries
-        ]
-    bias_spread(area, heads, r.tableb[...], r.index, r.biasb)
-    store(r.biasb, r.bias)
-
-    loads[4].wait()
-    c_cot.wait()
-    total = jnp.zeros((1, half), F32)
-    for side in range(2):
-        at = pl.ds(pl.multiple_of(who[side] * tokens, tokens), tokens)
-        pick = ones(jnp.logical_and(token_rows, r.keep[who[side]] > 0))
-        mine = dot(pick, r.cotb[0, at, :])
-        total += jnp.sum(mine, 0, keepdims=True)
-        here = pl.ds(side * rows, rows)
-        r.gfb[here, own_cols] = mine.astype(BF16)
-        r.gfb[here, oth_cols] = dot(pick, r.cotb[1, at, :]).astype(BF16)
-    r.gb2[...] = total
-    store(r.gfb, r.gf)
 
     loads[5].wait()
 
@@ -494,7 +493,10 @@
             r.qkvb[s, :, cols] = value.astype(BF16)
     store(r.qkvb, r.qkv)
 
-    @pl.loop(0, model // 128)
+    c_bias.wait()
+    store(r.biasb, r.bias)
+
+    @pl.loop(0, model // 128, unroll=2)
     def _(g):
         attention_forward(dim, heads, g, r)
 
@@ -519,8 +521,24 @@
         r.secb[at, :] = ((x - mean) * scale * nat[3:4, :] + nat[4:5, :]).astype(BF16)
 
     steps(rows, 112, norm2)
+    c_sec = link.copy(9, r.secb, r.second_sib)
+    c_sec.start()
     store(r.secb, r.second)
-    for one in (c_mn, c_first, c_att):
+
+    loads[4].wait()
+    c_cot.wait()
+    total = jnp.zeros((1, half), F32)
+    for side in range(2):
+        at = pl.ds(pl.multiple_of(who[side] * tokens, tokens), tokens)
+        pick = ones(jnp.logical_and(token_rows, jnp.where(who[side] == 0, kept[0], kept[1]) > 0))
+        mine = dot(pick, r.cotb[0, at, :])
+        total += jnp.sum(mine, 0, keepdims=True)
+        here = pl.ds(side * rows, rows)
+        r.gfb[here, own_cols] = mine.astype(BF16)
+        r.gfb[here, oth_cols] = dot(pick, r.cotb[1, at, :]).astype(BF16)
+    r.gb2[...] = total
+    store(r.gfb, r.gf)
+    for one in (c_mn, c_first, c_att, c_sec):
         one.wait()
     for one in stores:
         one.wait()
@@ -536,7 +554,7 @@
     big = dict(
         x=shape((4, rows, half), BF16), gf=shape((2 * rows, model), BF16),
         stream0=shape((rows, model)), stream1=shape((rows, model)),
-        second=shape((rows, model), BF16), qkv=shape((3, rows, model), BF16),
+        second=shape((rows, model), BF16), second_sib=shape((rows, model), BF16), qkv=shape((3, rows, model), BF16),
         bias=shape((PAD * heads, 128)), first_own=shape((rows, model), BF16),
         first_sib=shape((rows, model), BF16), mn_own=shape((rows, model), BF16),
         mn_sib=shape((rows, model), BF16), att_own=shape((rows, half), BF16),
@@ -546,6 +564,7 @@
     outs = dict(
         big, gb2=shape((1, half)), nat=shape((8, model)), mgo=shape((2, 1, model)),
         lse=shape((model // 128, windows * 128 // dim, 128)),
+        kept_rows=shape((2, 8, rows)), index=shape((128, 128), jnp.int32),
     )
     scratch = dict(
         wmb=vm((2, model, model), BF16), wqb=vm((2, 3, model, half), BF16),
@@ -556,7 +575,8 @@
         qkvb=vm((3, rows, model), BF16), biasb=vm((PAD * heads, 128), F32),
         attb=vm((rows, model), BF16), secb=vm((rows, model), BF16),
         vx=vm((2, 32, half), F32), mso=vm((2, 1, model), F32), tableb=vm((heads, slots), F32),
-        lsem=dma((8,)), ssem=dma((16,)), xsend=dma((8,)), xrecv=dma((8,)),
+        square=vm((128, 128), F32),
+        lsem=dma((8,)), ssem=dma((16,)), xsend=dma((10,)), xrecv=dma((10,)),
     )
 
     def body(r):
@@ -567,41 +587,40 @@
 
 CHUNK = 512
 PLAN = {
-    2: ((0, 0), (1, 0)),
-    3: ((2, 0),),
-    7: ((3, 0),),
-    9: ((4, 0),),
-    11: ((1, 1),),
-    12: ((5, 0),),
-    13: ((0, 1),),
-    15: ((3, 1),),
+    3: ((0, 0), (1, 0)),
+    8: ((2, 0),),
+    11: ((3, 0),),
+    12: ((4, 0),),
+    15: ((5, 0),),
     17: ((6, 0),),
-    19: ((4, 1),),
-    20: ((7, 0), (1, 2)),
+    18: ((3, 1), (7, 0)),
+    20: ((1, 1),),
     21: ((2, 1),),
-    25: ((5, 1), (4, 2)),
-    27: ((3, 2),),
-    29: ((7, 1), (8, 0)),
-    30: ((6, 1), (5, 2)),
-    31: ((0, 2),),
-    32: ((2, 2),),
-    33: ((1, 3),),
-    34: ((4, 3), (3, 3)),
-    35: ((7, 2), (9, 0)),
-    36: ((10, 0),),
-    37: ((8, 1),),
+    22: ((8, 0),),
+    23: ((5, 1),),
+    26: ((7, 1),),
+    27: ((4, 1),),
+    28: ((0, 1),),
+    31: ((6, 1), (1, 2), (3, 2), (0, 2)),
+    33: ((9, 0),),
+    35: ((10, 0), (8, 1), (11, 0), (2, 2), (5, 2), (7, 2), (4, 2)),
+    36: ((6, 2), (14, 0)),
+    37: ((1, 3), (12, 0), (3, 3)),
+    38: ((15, 0),),
+    39: ((0, 3),),
     40: (
-        (11, 0), (6, 2), (-1, 0), (13, 0), (5, 3), (-1, 1),
-        (12, 0), (0, 3), (-1, 2), (9, 1), (2, 3), (-1, 3),
-        (8, 2), (10, 1), (-1, 4), (7, 3), (6, 3), (11, 1),
-        (13, 1), (9, 2), (8, 3), (11, 2), (10, 2), (12, 1),
-        (13, 2), (9, 3), (11, 3), (10, 3), (12, 2), (13, 3),
-        (12, 3),
+        (13, 0), (2, 3), (-1, 0), (9, 1), (5, 3), (-1, 1),
+        (8, 2), (10, 1), (-1, 2), (7, 3), (14, 1), (-1, 3),
+        (4, 3), (11, 1), (-1, 4), (15, 1), (6, 3), (12, 1),
+        (9, 2), (11, 2), (13, 1), (8, 3), (10, 2), (14, 2),
+        (15, 2), (12, 2), (9, 3), (11, 3), (13, 2), (10, 3),
+        (14, 3), (15, 3), (12, 3), (13, 3),
     ),
 }
 
 
 def back_body(bits, orders, dim, heads, area, r):
+    n_units = len(orders)
     t = lax.axis_index("tp")
     who = (t, 1 - t)
     sec, gf, facc, gacc, st, ex = r.sec, r.gfb, r.facc, r.gacc, r.st, r.ex
@@ -622,18 +641,34 @@
     def load(k, src, dst):
         return pltpu.make_async_copy(src, dst, r.lsem.at[k])
 
+    whole_units = 2 * chunks + 4
+
+    def place_of(u):
+        if u < whole_units:
+            return u, pl.ds(0, CHUNK)
+        u -= whole_units
+        return whole_units + u // 2, pl.ds(u % 2 * (CHUNK // 2), CHUNK // 2)
+
     def unit(u):
-        bufs = [buf.at[u] for buf in r.bufs]
-        return Scatter(orders[u], r.src.at[u % 8], bufs, r.rsend, r.rrecv, u)
-
-    def put(u, value):
-        if u >= 8:
-            unit(u - 8).copy(0).wait_send()
-        r.src[u % 8] = value.astype(BF16).reshape(*([2] * bits), part, CHUNK)
-        unit(u).copy(0).start()
+        block, cols = place_of(u)
+        lead = tuple([slice(None)] * bits)
+        held = [r.src.at[(block % 8, *lead, slice(None), cols)]]
+        for k, buf in enumerate(r.bufs):
+            held.append(buf.at[(block, *lead[k + 1 :], slice(None), cols)])
+        return Scatter(orders[u], held, r.rsend, r.rrecv, u)
+
+    def put(block, value):
+        if block >= 8:
+            unit(block - 8).copy(0).wait_send()
+        r.src[block % 8] = value.astype(BF16).reshape(*([2] * bits), part, CHUNK)
+        for u in range(n_units):
+            if place_of(u)[0] == block:
+                unit(u).copy(0).start()
 
     def held(u):
-        return st.at[u // 2 * part : (u // 2 + 1) * part, (left, right)[u % 2]]
+        block, cols = place_of(u)
+        at = pl.ds(block % 2 * CHUNK + cols.start, cols.size)
+        return st.at[block // 2 * part : (block // 2 + 1) * part, at]
 
     def result(u):
         if u < 2 * chunks:
@@ -643,7 +678,7 @@
             return r.o_proj
         if u < 4:
             return r.o_qkv.at[u - 1]
-        return r.o_merge.at[:, (left, right)[u - 4]]
+        return r.o_merge.at[:, pl.ds((u - 4) * (CHUNK // 2), CHUNK // 2)]
 
     last_step = bits - 1
     copies = [
@@ -680,13 +715,7 @@
     def write(u):
         return pltpu.make_async_copy(held(u), result(u), r.osem.at[u])
 
-    enter(bits)
-    c_sec = link.copy(0, r.second, sec.at[theirs])
-    c_sec.start()
-    loads = [
-        load(0, r.second, sec.at[mine]), load(1, r.gf, gf), load(3, r.stream1, st),
-        load(4, r.qkv, qkvb),
-    ]
+    loads = [load(0, r.second, sec.at[mine]), load(2, r.second_sib, sec.at[theirs])]
     for one in loads:
         one.start()
 
@@ -700,12 +729,18 @@
 
     for one in weights(0):
         one.start()
-    for one in loads[0:2]:
+    late = [load(1, r.gf, gf), load(3, r.stream1, st), load(4, r.qkv, qkvb)]
+    for one in late:
+        one.start()
+    enter(bits)
+    for one in (*loads, late[0]):
         one.wait()
-    c_sec.wait()
 
     blocks = CHUNK // 128
     hid, dact, act, gh = r.sums, r.biasb, r.act, r.gh
+
+    def save(c):
+        return load(13, act, r.acts.at[c])
 
     @pl.loop(0, chunks)
     def _(c):
@@ -725,6 +760,10 @@
         value = dot_nt(gf[...], w2b[slot])
         for b in range(blocks):
             dact[b * 2 * rows : (b + 1) * 2 * rows, :] = value[:, b * 128 : (b + 1) * 128]
+        @pl.when(c > 0)
+        def _():
+            save(c - 1).wait()
+
         for b in range(blocks):
             lanes = pl.ds(b * 128, 128)
 
@@ -737,6 +776,7 @@
                 gh[at, lanes] = (dact[here, :] * (cdf + x * pdf)).astype(BF16)
 
             steps(2 * rows, 128, gelu)
+        save(c).start()
         r.gb1[:, of] = jnp.sum(gh[...].astype(F32), 0, keepdims=True)
         for k, value in enumerate((dot_tn(sec[...], gh[...]), dot_tn(gf[...], act[...]))):
             r.src[2 * c + k] = value.astype(BF16).reshape(*([2] * bits), part, CHUNK)
@@ -754,12 +794,10 @@
 
         @pl.when(c == 0)
         def _():
-            facc[...] = dot(act[...], w2b[slot])
             gacc[...] = dot_nt(gh[...], w1b[slot])
 
         @pl.when(c > 0)
         def _():
-            facc[...] += dot(act[...], w2b[slot])
             gacc[...] += dot_nt(gh[...], w1b[slot])
 
         for j in range(chunks):
@@ -769,6 +807,7 @@
                 pump(chunks + j)
 
     load(5, r.bias, r.biasb).start()
+    save(chunks - 1).wait()
     load(6, r.att_own, act.at[mine]).start()
     load(7, r.att_sib, act.at[theirs]).start()
     for k, src in enumerate((r.wp_own, r.wp_oth)):
@@ -777,21 +816,6 @@
     c_g2 = link.copy(1, ex.at[0], ex.at[1])
     c_g2.start()
     load(3, r.stream1, st).wait()
-    fsend, fland = gh, cotb.at[pl.ds(3, 2)]
-    fsend[mine, :] = facc[theirs, oth_cols].astype(BF16)
-    fsend[theirs, :] = (facc[mine, oth_cols] + st[:, oth_cols]).astype(BF16)
-    c_feed = [
-        link.copy(k, fsend.at[(mine, theirs)[k - 7]], fland.at[k - 7]) for k in (7, 8)
-    ]
-    for one in c_feed:
-        one.start()
-
-    def fold(at):
-        own = facc[at, own_cols] + st[at, own_cols]
-        oth = facc[pl.ds(pl.multiple_of(rows + at.start, 16), at.size), own_cols]
-        facc[at, left] = own
-        facc[at, right] = oth
-
     pump(8)
     v2 = r.v2
     v2[...] = jnp.zeros_like(v2)
@@ -814,7 +838,6 @@
     load(10, r.first_own, gf.at[mine]).start()
     load(11, r.first_sib, gf.at[theirs]).start()
     pump(9)
-    steps(rows, 112, fold)
     pump(10)
     for k, src in enumerate((r.wp_own, r.wp_oth)):
         load(8 + k, src, w2b.at[k]).wait()
@@ -836,9 +859,18 @@
     load(4, r.qkv, qkvb).wait()
     load(5, r.bias, r.biasb).wait()
 
-    @pl.loop(0, model // 128)
+    dland = cotb.at[pl.ds(0, 3)]
+    c_qkv = link.copy(4, qkvb.at[:, :, right], dland)
+    groups = model // 128
+
+    @pl.loop(0, groups)
     def _(g):
-        attention_back(dim, heads, g, r)
+        attention_back(dim, heads, lax.rem(g + groups // 2, groups), r)
+
+        @pl.when(g == groups // 2 - 1)
+        def _():
+            c_qkv.start()
+
 
         for k in range(8):
 
@@ -846,14 +878,45 @@
             def _():
                 pump(13 + k)
 
-    dland = cotb.at[pl.ds(0, 3)]
-    c_qkv = link.copy(4, qkvb.at[:, :, right], dland)
-    c_qkv.start()
-
     def slice_of(k):
         return (r.wqkv_own, r.wqkv_oth)[k // 3].at[k % 3]
 
     load(16, slice_of(0), w1b.at[0]).start()
+
+    load(10, r.first_own, gf.at[mine]).wait()
+    load(11, r.first_sib, gf.at[theirs]).wait()
+    c_qkv.wait()
+    for s in range(3):
+        put(u_qkv + s, dot_tn(gf[mine, :], qkvb[s, :, left]) + dot_tn(gf[theirs, :], dland[s]))
+        pump(28 + s)
+    load(10, r.mn_own, gf.at[mine]).start()
+    load(11, r.mn_sib, gf.at[theirs]).start()
+
+    kept = (act, gh)
+
+    def feed_loads(c):
+        slot = c % 2
+        rows_of = pl.ds(c * CHUNK, CHUNK)
+        return (
+            load(18 + slot, r.acts.at[c], kept[slot]),
+            load(20 + slot, r.fc2.at[rows_of, :], w2b.at[slot]),
+        )
+
+    def feed(c):
+        for one in feed_loads(c):
+            one.wait()
+        value = dot(kept[c % 2][...], w2b[c % 2])
+        if c == 0:
+            facc[...] = value
+        else:
+            facc[...] += value
+        if c + 2 < chunks:
+            for one in feed_loads(c + 2):
+                one.start()
+
+    for c in range(2):
+        for one in feed_loads(c):
+            one.start()
 
     for k in range(6):
         load(16 + k % 2, slice_of(k), w1b.at[k % 2]).wait()
@@ -879,18 +942,11 @@
     steps(rows, 112, norm1)
     c_s0 = link.copy(5, sec.at[mine], ex.at[1])
     c_s0.start()
-
-    load(10, r.first_own, gf.at[mine]).wait()
-    load(11, r.first_sib, gf.at[theirs]).wait()
-    for k in range(2):
-        load(8 + k, r.wm_own.at[(left, right)[k], :], w2b.at[k]).start()
-    c_qkv.wait()
+    again = gacc.at[theirs]
+    load(22, r.stream1, again).start()
     pump(27)
-    for s in range(3):
-        put(u_qkv + s, dot_tn(gf[mine, :], qkvb[s, :, left]) + dot_tn(gf[theirs, :], dland[s]))
-        pump(28 + s)
-    load(10, r.mn_own, gf.at[mine]).start()
-    load(11, r.mn_sib, gf.at[theirs]).start()
+    feed(0)
+    feed(1)
 
     c_s0.wait()
     load(10, r.mn_own, gf.at[mine]).wait()
@@ -900,24 +956,42 @@
         put(u_merge + k, dot_tn(sec[mine, :], gf[mine, cols]) + dot_tn(ex[1], gf[theirs, cols]))
         pump(31 + k)
 
+    for c in range(2, chunks):
+        feed(c)
+    for k in range(2):
+        load(8 + k, r.wm_own.at[(left, right)[k], :], w2b.at[k]).start()
+    load(22, r.stream1, again).wait()
+    fsend, fland = gh, cotb.at[pl.ds(3, 2)]
+    fsend[mine, :] = facc[theirs, oth_cols].astype(BF16)
+    fsend[theirs, :] = (facc[mine, oth_cols] + again[:, oth_cols]).astype(BF16)
+    c_feed = [
+        link.copy(k, fsend.at[(mine, theirs)[k - 7]], fland.at[k - 7]) for k in (7, 8)
+    ]
     for one in c_feed:
-        one.wait()
-    token_rows = gather_rows(rows, tokens, windows)[0]
-    outs = []
-    for side in range(2):
-        value = facc[mine, (left, right)[side]] + fland[side].astype(F32)
-        pick = ones(jnp.logical_and(token_rows, r.keep[who[side]] > 0))
-        fsend[side * rows : side * rows + tokens, :] = dot(pick, (value + r.b2[...]).astype(BF16)).astype(BF16)
-        at = pl.ds(pl.multiple_of(who[side] * tokens, tokens), tokens)
-        outs.append(load(14 + side, fsend.at[pl.ds(side * rows, tokens), :], r.out.at[at, :]))
-        outs[-1].start()
-    load(1, r.x, cotb.at[pl.ds(0, 4)]).start()
+        one.start()
     pump(33)
 
     r.rel[...] = jnp.zeros_like(r.rel)
     for k in range(2):
         rel_sum(k * 12, (area // PAIRS if k else 12), heads, r.index, r.sums, r.rel)
         pump(34 + k)
+        if k == 1:
+            continue
+        for one in c_feed:
+            one.wait()
+        token_rows = gather_rows(rows, tokens, windows)[0]
+        outs = []
+        for side in range(2):
+            value = facc[(mine, theirs)[side], own_cols] + fland[side].astype(F32)
+            if side == 0:
+                value += again[:, own_cols]
+            pick = ones(jnp.logical_and(token_rows, r.keep[who[side], 0:1, :] > 0))
+            value = dot(pick, (value + r.b2[...]).astype(BF16)).astype(BF16)
+            fsend[side * rows : side * rows + tokens, :] = value
+            at = pl.ds(pl.multiple_of(who[side] * tokens, tokens), tokens)
+            outs.append(load(14 + side, fsend.at[pl.ds(side * rows, tokens), :], r.out.at[at, :]))
+            outs[-1].start()
+        load(1, r.x, cotb.at[pl.ds(0, 4)]).start()
 
     for k in range(4):
         load(8 + k % 2, (r.wm_own, r.wm_oth)[k // 2].at[(left, right)[k % 2], :],
@@ -996,24 +1070,12 @@
             outs[-1].start()
     pump(39)
     pump(40)
-    v = vs.at[bits]
-    for i in range(2):
-        for j in range(2):
-            (r.o_mg, r.o_ms)[i][:, j * half : (j + 1) * half] = v[2 * i + j : 2 * i + j + 1, :]
-    for k, ref in enumerate((r.o_n1g, r.o_n1s)):
-        ref[...] = v[4 + k : 5 + k, :]
-    r.o_qb[...] = v[6:8, :]
-    for k, ref in enumerate((r.o_n2g, r.o_n2s, r.o_pb, r.o_b2)):
-        ref[...] = v[8 + k : 9 + k, :]
-    for j in range(hidden // half):
-        r.o_b1[:, j * half : (j + 1) * half] = v[12 + j : 13 + j, :]
-    r.o_rel[...] = v[16 : 16 + heads_here, 0 : r.o_rel.shape[1]]
-
+    r.o_vec[...] = vs[bits]
     outs[-1].wait()
-    for u in range(first_unit + 6):
+    for u in range(n_units):
         write(u).wait()
         for step in range(bits):
-            if step > 0 or u >= first_unit + 6 - 8:
+            if step > 0 or u >= first_unit - 2:
                 unit(u).copy(step).wait_send()
 
 
@@ -1025,21 +1087,18 @@
     half = model // 2
     side = int(area**0.5)
     slots = -(-entries // 128) * 128
-    n_units = 2 * (hidden // CHUNK) + 6
+    n_blocks = 2 * (hidden // CHUNK) + 6
+    n_units = n_blocks + 2
     part = model // count
-    orders = orders_of(count, n_units)
+    orders = orders_of(count)
     big = dict(
         out=shape((2 * tokens, half), BF16),
         pixels_grad=shape((side, 2, side, 2, windows, half)),
         o_fc1=shape((part, hidden)), o_fc2=shape((part, hidden)), o_qkv=shape((3, part, half)),
         o_proj=shape((part, half)), o_merge=shape((part, model)),
+        acts=shape((hidden // CHUNK, 2 * rows, CHUNK), BF16),
     )
-    outs = dict(
-        big, o_mg=shape((1, model)), o_ms=shape((1, model)),
-        o_n1g=shape((1, half)), o_n1s=shape((1, half)), o_qb=shape((2, half)),
-        o_n2g=shape((1, half)), o_n2s=shape((1, half)), o_pb=shape((1, half)),
-        o_b1=shape((1, hidden)), o_b2=shape((1, half)), o_rel=shape((heads // 2, entries)),
-    )
+    outs = dict(big, o_vec=shape((32, half)))
     vm, dma = pltpu.VMEM, pltpu.SemaphoreType.DMA
     scratch = dict(
         sec=vm((2 * rows, model), BF16), gfb=vm((2 * rows, model), BF16),
@@ -1051,11 +1110,11 @@
         act=vm((2 * rows, CHUNK), BF16), gh=vm((2 * rows, CHUNK), BF16),
         pix=vm((side, side, windows, half), F32),
         src=vm((8, *([2] * bits), part, CHUNK), BF16),
-        bufs=[vm((n_units, *([2] * k), part, CHUNK), BF16) for k in reversed(range(bits))],
+        bufs=[vm((n_blocks, *([2] * k), part, CHUNK), BF16) for k in reversed(range(bits))],
         v0=vm((4, model), F32), v1=vm((2, model), F32), v2=vm((3, model), F32),
         vq=vm((2, model), F32), rel=vm((heads, slots), F32), gb1=vm((1, hidden), F32),
         vs=vm((bits + 1, 32, half), F32), vx=vm((2, 32, half), F32), vbuf=vm((bits, 32, half), F32),
-        lsem=dma((18,)), wsem=dma((2, 2)), xsend=dma((9,)), xrecv=dma((9,)), osem=dma((n_units,)),
+        lsem=dma((23,)), wsem=dma((2, 2)), xsend=dma((9,)), xrecv=dma((9,)), osem=dma((n_units,)),
         rsend=dma((n_units, bits)), rrecv=dma((n_units, bits)),
         vsend=dma((bits,)), vrecv=dma((bits,)),
     )
@@ -1066,33 +1125,51 @@
     return kernel_call(body, small, large, outs, scratch, big, collective=1)
 
 
-def hand_on(arrays):
-    names = list(arrays)
-
+def hand_on(large, vec, hidden, heads, entries):
+    names, n = list(large), len(large)
+    half = vec.shape[1]
+    model = 2 * half
     free = pl.BlockSpec(memory_space=pl.ANY)
-    n = len(names)
+    small = dict(
+        mg=(0, model), ms=(2, model), n1g=(4, half), n1s=(5, half), n2g=(8, half),
+        n2s=(9, half), pb=(10, half), b2=(11, half), b1=(12, hidden),
+    )
+    tiny_shapes = [shape((1, width)) for _, width in small.values()]
+    tiny_shapes += [shape((2, half)), shape((heads // 2, entries))]
+    m = len(tiny_shapes)
 
     def run(*refs):
-        given, taken, held, sem = refs[:n], refs[n : 2 * n], refs[2 * n : 3 * n], refs[3 * n]
-        ins = [pltpu.make_async_copy(given[k], held[k], sem.at[0, k]) for k in range(n)]
-        outs = [pltpu.make_async_copy(held[k], taken[k], sem.at[1, k]) for k in range(n)]
+        given, taken = refs[: n + 1], refs[n + 1 : 2 * n + 1 + m]
+        held, v, sem = refs[2 * n + 1 + m : -2], refs[-2], refs[-1]
+        ins = [pltpu.make_async_copy(given[n], v, sem.at[0, n])]
+        ins += [pltpu.make_async_copy(given[k], held[k], sem.at[0, k]) for k in range(n)]
+        outs = [pltpu.make_async_copy(held[k], taken[k], sem.at[1, k]) for k in range(n + m)]
         for one in ins:
             one.start()
-        for one, other in zip(ins, outs):
+        ins[0].wait()
+        for ref, (row, width) in zip(held[n:], small.values()):
+            for j in range(width // half):
+                ref[:, j * half : (j + 1) * half] = v[row + j : row + j + 1, :]
+        held[-2][...] = v[6:8, :]
+        held[-1][...] = v[16 : 16 + heads // 2, 0:entries]
+        for one in outs[n:]:
+            one.start()
+        for one, other in zip(ins[1:], outs):
             one.wait()
             other.start()
         for one in outs:
             one.wait()
 
+    shapes = [*[shape(a.shape, a.dtype) for a in large.values()], *tiny_shapes]
     results = pl.pallas_call(
         run,
-        out_shape=tuple(shape(a.shape, a.dtype) for a in arrays.values()),
-        in_specs=[free] * n,
-        out_specs=(free,) * n,
-        scratch_shapes=[pltpu.VMEM(a.shape, a.dtype) for a in arrays.values()]
-        + [pltpu.SemaphoreType.DMA((2, n))],
-    )(*arrays.values())
-    return SimpleNamespace(**dict(zip(names, results)))
+        out_shape=tuple(shapes),
+        in_specs=[free] * (n + 1),
+        out_specs=(free,) * (n + m),
+        scratch_shapes=[pltpu.VMEM(a.shape, a.dtype) for a in shapes]
+        + [pltpu.VMEM(vec.shape, F32), pltpu.SemaphoreType.DMA((2, n + m))],
+    )(*large.values(), vec)
+    return SimpleNamespace(**dict(zip([*names, *small, "qb", "rel"], results)))
 
 
 def solution(mesh):
@@ -1116,18 +1193,13 @@
         def row(v):
             return v.reshape(1, -1)
 
-        index = jnp.pad(rel_index.T, ((0, 0), (0, 128 - area)))
-        kept = keep.reshape(2, 1, wins * area)
-        kept_rows = jnp.pad(
-            keep.reshape(2 * wins, area), ((0, 0), (0, PAD - area))
-        ).reshape(2, 1, rows)
         wqkv = qkv_weight.transpose(1, 0, 2)
         a = front(
             dim, heads, area, wins,
             dict(
                 mg=row(merge_gain), ms=row(merge_shift), n1g=row(norm1_gain),
                 n1s=row(norm1_shift), pb=row(proj_bias), n2g=row(norm2_gain),
-                n2s=row(norm2_shift), qb=qkv_bias, table=rel_table.T, index=index, keep=kept,
+                n2s=row(norm2_shift), qb=qkv_bias, table=rel_table.T, rel_index=rel_index, keep=keep,
             ),
             dict(
                 pixels=pixels.transpose(1, 2, 0, 3).reshape(side, 2, side, 2, wins, channels),
@@ -1137,11 +1209,11 @@
         b = back(
             count, dim, heads, area, wins, rel_table.shape[0],
             dict(
-                keep=kept_rows, b1=row(fc1_bias), b2=row(fc2_bias), nat=a.nat, mgo=a.mgo,
-                lse=a.lse, index=index, gb2=a.gb2,
+                keep=a.kept_rows, b1=row(fc1_bias), b2=row(fc2_bias), nat=a.nat, mgo=a.mgo,
+                lse=a.lse, index=a.index, gb2=a.gb2,
             ),
             dict(
-                second=a.second, gf=a.gf, stream1=a.stream1, stream0=a.stream0,
+                second=a.second, second_sib=a.second_sib, gf=a.gf, stream1=a.stream1, stream0=a.stream0,
                 fc1=fc1_weight, fc2=fc2_weight, wp_own=proj_weight, wp_oth=a.wp_oth,
                 wqkv_own=wqkv, wqkv_oth=a.wqkv_oth, wm_own=merge_weight, wm_oth=a.wm_oth,
                 att_own=a.att_own, att_sib=a.att_sib, qkv=a.qkv, bias=a.bias,
@@ -1149,17 +1221,20 @@
                 x=a.x,
             ),
         )
-        f = hand_on(vars(b))
+        large = vars(b)
+        vec = large.pop("o_vec")
+        large.pop("acts")
+        f = hand_on(large, vec, hidden, heads, rel_table.shape[0])
 
         def flat(v):
             return v.reshape(-1)
 
         pixels_grad = f.pixels_grad.reshape(height, height, wins, channels)
         return (
-            f.out, pixels_grad.transpose(2, 0, 1, 3), flat(f.o_mg), flat(f.o_ms), f.o_merge.T,
-            flat(f.o_n1g), flat(f.o_n1s), f.o_qkv.transpose(1, 0, 2), f.o_qb, f.o_rel.T,
-            f.o_proj.T, flat(f.o_pb), flat(f.o_n2g), flat(f.o_n2s), f.o_fc1, flat(f.o_b1),
-            f.o_fc2.T, flat(f.o_b2),
+            f.out, pixels_grad.transpose(2, 0, 1, 3), flat(f.mg), flat(f.ms), f.o_merge.T,
+            flat(f.n1g), flat(f.n1s), f.o_qkv.transpose(1, 0, 2), f.qb, f.rel.T,
+            f.o_proj.T, flat(f.pb), flat(f.n2g), flat(f.n2s), f.o_fc1, flat(f.b1),
+            f.o_fc2.T, flat(f.b2),
         )
 
     in_specs = (

time: 187 us -> 176 us (0.941)
  Pallas kernels: 181 us -> 175 us
  local copies, waits for them, and re-layouts: 4.34 us -> 0 us
    pallas_call x2, Pallas kernels: 176 us -> 170 us  [kernel_call(): pl.pallas_call(run, out_shape=tuple(outs.values()), in_specs=[vmem] * len...]
    reshape x3 -> x0, local copies, waits for them, and re-layouts: 2.79 us -> none  [the longest x1 1.36 us: shards(): kept = keep.reshape(2, 1, wins * area)]
where the time goes in v5:
time: 176 us
  Pallas kernels  175 us (99%)
    pallas_call x2, Pallas kernels, kernel_call(): pl.pallas_call(run, out_shape=tuple(outs.values()), in_specs=[vmem] * len...  170 us
    pallas_call x1, Pallas kernels, hand_on(): pl.pallas_call(run, out_shape=tuple(shapes), in_specs=[free] * (n + 1), o...  5.08 us

profile of v5, /device:TPU:0, one launch (start us, length us, event | category | flops | bytes accessed | tf_op | source)
XLA Modules:
  0.0 175.8 jit_solution(5371091407230843515)
XLA Ops:
  0.7 27.1 %shard_map.331 = (bf16[4,448,512]{2,1,0:T(8,128)(2,1)}, bf16[896,1024]{1,0:T(8,128)(2,1)}, f32[448,1024]{1,0:T(8,128)}, f32[448,1024]{1,0:T(8,128)}, bf16[448,10...) custom-call(f32[1,1024]{1,0:T(1,128)} %bitcast.36, ...), custom_call_target="tpu_custom_call" | custom-call | tf_op jit(solution)/shard_map/pallas_call | solution.py:30
  27.8 142.8 %shard_map.332 = (bf16[800,512]{1,0:T(8,128)(2,1)}, f32[10,2,10,2,4,512]{5,4,3,2,1,0:T(4,128)}, f32[64,2048]{1,0:T(8,128)}, f32[64,2048]{1,0:T(8,128)}, f32[3,64...) custom-call(f32[2,8,448]{2,1,0:T(8,128)} %get-tuple-element.67.refs_, ...), custom_call_target="tpu_custom_call" | custom-call | tf_op jit(solution)/shard_map/pallas_call | solution.py:30
  170.5 5.1 %shard_map.333 = (bf16[800,512]{1,0:T(8,128)(2,1)}, f32[10,2,10,2,4,512]{5,4,3,2,1,0:T(4,128)}, f32[64,2048]{1,0:T(8,128)}, f32[64,2048]{1,0:T(8,128)}, f32[3,64...) custom-call(bf16[800,512]{1,0:T(8,128)(2,1)} %get-tuple-element.90.r, ...), custom_call_target="tpu_custom_call" | custom-call | tf_op jit(solution)/shard_map/pallas_call | solution.py:1164

commit v6 on v5

--- a/solution.py
+++ b/solution.py
@@ -281,7 +281,7 @@
     return near, far
 
 
-TURNS = (((0,1,2,3),(1,0,2,3),(2,0,1,3),(0,2,1,3),(1,2,0,3),(2,1,0,3),(0,1,2,3),(1,0,2,3),(2,0,1,3),(0,1,2,3),(1,0,2,3),(2,1,0,3),(0,1,2,3),(0,1,2,3),(1,0,2,3),(1,0,2,3)))
+TURNS = (((0,1,2,3),(1,0,2,3),(2,0,1,3),(0,1,2,3),(1,0,2,3),(2,1,0,3),(0,1,2,3),(1,0,2,3),(2,0,1,3),(0,1,2,3),(1,0,2,3),(2,1,0,3),(2,0,1,3),(0,1,2,3),(2,1,0,3),(1,0,2,3)))
 
 
 def orders_of(count):
@@ -593,28 +593,26 @@
     12: ((4, 0),),
     15: ((5, 0),),
     17: ((6, 0),),
-    18: ((3, 1), (7, 0)),
+    18: ((7, 0),),
     20: ((1, 1),),
-    21: ((2, 1),),
-    22: ((8, 0),),
-    23: ((5, 1),),
-    26: ((7, 1),),
-    27: ((4, 1),),
-    28: ((0, 1),),
-    31: ((6, 1), (1, 2), (3, 2), (0, 2)),
-    33: ((9, 0),),
-    35: ((10, 0), (8, 1), (11, 0), (2, 2), (5, 2), (7, 2), (4, 2)),
-    36: ((6, 2), (14, 0)),
-    37: ((1, 3), (12, 0), (3, 3)),
-    38: ((15, 0),),
-    39: ((0, 3),),
+    23: ((3, 1), (1, 2)),
+    27: ((4, 1), (0, 2)),
+    29: ((8, 0), (0, 1)),
+    30: ((2, 1),),
+    31: ((5, 1), (7, 1)),
+    32: ((6, 1),),
+    34: ((11, 0), (3, 2)),
+    35: ((9, 0), (1, 3), (4, 2), (10, 0), (0, 3), (2, 2), (8, 1)),
+    36: ((12, 0),),
+    37: ((15, 0), (13, 0), (7, 2)),
+    39: ((5, 2),),
     40: (
-        (13, 0), (2, 3), (-1, 0), (9, 1), (5, 3), (-1, 1),
-        (8, 2), (10, 1), (-1, 2), (7, 3), (14, 1), (-1, 3),
-        (4, 3), (11, 1), (-1, 4), (15, 1), (6, 3), (12, 1),
-        (9, 2), (11, 2), (13, 1), (8, 3), (10, 2), (14, 2),
-        (15, 2), (12, 2), (9, 3), (11, 3), (13, 2), (10, 3),
-        (14, 3), (15, 3), (12, 3), (13, 3),
+        (11, 1), (14, 0), (-1, 0), (10, 1), (6, 2), (-1, 1),
+        (9, 1), (12, 1), (-1, 2), (3, 3), (8, 2), (-1, 3),
+        (15, 1), (4, 3), (-1, 4), (13, 1), (11, 2), (2, 3),
+        (14, 1), (7, 3), (12, 2), (14, 2), (5, 3), (10, 2),
+        (6, 3), (9, 2), (8, 3), (15, 2), (13, 2), (11, 3),
+        (12, 3), (14, 3), (10, 3), (9, 3), (15, 3), (13, 3),
     ),
 }
 

time: 176 us -> 174 us (0.989)
  Pallas kernels: 175 us -> 173 us
where the time goes in v6:
time: 174 us
  Pallas kernels  173 us (99%)
    pallas_call x2, Pallas kernels, kernel_call(): pl.pallas_call(run, out_shape=tuple(outs.values()), in_specs=[vmem] * len...  168 us
    pallas_call x1, Pallas kernels, hand_on(): pl.pallas_call(run, out_shape=tuple(shapes), in_specs=[free] * (n + 1), o...  5.08 us

profile of v6, /device:TPU:0, one launch (start us, length us, event | category | flops | bytes accessed | tf_op | source)
XLA Modules:
  0.0 174.1 jit_solution(15913428492103890244)
XLA Ops:
  0.7 27.1 %shard_map.331 = (bf16[4,448,512]{2,1,0:T(8,128)(2,1)}, bf16[896,1024]{1,0:T(8,128)(2,1)}, f32[448,1024]{1,0:T(8,128)}, f32[448,1024]{1,0:T(8,128)}, bf16[448,10...) custom-call(f32[1,1024]{1,0:T(1,128)} %bitcast.36, ...), custom_call_target="tpu_custom_call" | custom-call | tf_op jit(solution)/shard_map/pallas_call | solution.py:30
  27.8 141.0 %shard_map.332 = (bf16[800,512]{1,0:T(8,128)(2,1)}, f32[10,2,10,2,4,512]{5,4,3,2,1,0:T(4,128)}, f32[64,2048]{1,0:T(8,128)}, f32[64,2048]{1,0:T(8,128)}, f32[3,64...) custom-call(f32[2,8,448]{2,1,0:T(8,128)} %get-tuple-element.67.refs_, ...), custom_call_target="tpu_custom_call" | custom-call | tf_op jit(solution)/shard_map/pallas_call | solution.py:30
  168.8 5.1 %shard_map.333 = (bf16[800,512]{1,0:T(8,128)(2,1)}, f32[10,2,10,2,4,512]{5,4,3,2,1,0:T(4,128)}, f32[64,2048]{1,0:T(8,128)}, f32[64,2048]{1,0:T(8,128)}, f32[3,64...) custom-call(bf16[800,512]{1,0:T(8,128)(2,1)} %get-tuple-element.90.r, ...), custom_call_target="tpu_custom_call" | custom-call | tf_op jit(solution)/shard_map/pallas_call | solution.py:1162
